TPU v7x, 32 devices: a whole 2x2x4 slice. The times are simulated.
32 devices in a mesh: dp: 8 (over z, x), mp: 4 (over y, core).
Axes of the slice: x: 2, y: 2, z: 4, core: 2. Of those that a mesh axis runs over, the one named last changes fastest.
Arguments:
- block_in: bfloat16 [2, 1024, 16, 768], P(None, ('dp', 'mp')), may hold values from -6 to 6
- seq_lengths: int32 [2, 1024], P(None, ('dp', 'mp')), may hold values from 1 to 16, as said below
- image_embed: bfloat16 [2, 1024, 768], P(None, ('dp', 'mp')), may hold values from -6 to 6
- w_qkv: float32 [768, 3, 768], P('dp', None, 'mp'), may hold values from -0.21875 to 0.21875
- w_out: float32 [768, 768], P('dp', 'mp'), may hold values from -0.4375 to 0.4375
- w_up: float32 [768, 3072], P('dp', 'mp'), may hold values from -0.21875 to 0.21875
- w_down: float32 [768, 3072], P('dp', 'mp'), may hold values from -0.109375 to 0.109375
- norm_params: float32 [768, 4], replicated, as said below
- norm_second: float32 [768, 4], P('dp'), may hold values from 16384 to 65536
- qkv_left: float32 [8, 4, 96, 96], P('dp', 'mp'), as said below
- qkv_right: float32 [8, 4, 576, 576], P('dp', 'mp'), as said below
- qkv_left_root: float32 [8, 4, 96, 96], P('dp', 'mp'), as said below
- qkv_right_root: float32 [8, 4, 576, 576], P('dp', 'mp'), as said below
- out_left: float32 [8, 4, 96, 96], P('dp', 'mp'), as said below
- out_right: float32 [8, 4, 192, 192], P('dp', 'mp'), as said below
- out_left_root: float32 [8, 4, 96, 96], P('dp', 'mp'), as said below
- out_right_root: float32 [8, 4, 192, 192], P('dp', 'mp'), as said below
- up_left: float32 [8, 4, 96, 96], P('dp', 'mp'), as said below
- up_right: float32 [8, 4, 768, 768], P('dp', 'mp'), as said below
- up_left_root: float32 [8, 4, 96, 96], P('dp', 'mp'), as said below
- up_right_root: float32 [8, 4, 768, 768], P('dp', 'mp'), as said below
- down_left: float32 [8, 4, 96, 96], P('dp', 'mp'), as said below
- down_right: float32 [8, 4, 768, 768], P('dp', 'mp'), as said below
- down_left_root: float32 [8, 4, 96, 96], P('dp', 'mp'), as said below
- down_right_root: float32 [8, 4, 768, 768], P('dp', 'mp'), as said below
Outputs:
- block_out: bfloat16 [2, 1024, 16, 768], P(None, ('dp', 'mp'))
- input_grad: float32 [2, 1024, 16, 768], P(None, ('dp', 'mp'))
- text_loss: float32 [2, 1024], P(None, ('dp', 'mp'))
- qkv_grad: float32 [768, 3, 768], P('dp', None, 'mp')
- qkv_left_new: float32 [8, 4, 96, 96], P('dp', 'mp')
- qkv_right_new: float32 [8, 4, 576, 576], P('dp', 'mp')
- qkv_new: float32 [768, 3, 768], P('dp', None, 'mp')
- out_grad: float32 [768, 768], P('dp', 'mp')
- out_left_new: float32 [8, 4, 96, 96], P('dp', 'mp')
- out_right_new: float32 [8, 4, 192, 192], P('dp', 'mp')
- out_new: float32 [768, 768], P('dp', 'mp')
- up_grad: float32 [768, 3072], P('dp', 'mp')
- up_left_new: float32 [8, 4, 96, 96], P('dp', 'mp')
- up_right_new: float32 [8, 4, 768, 768], P('dp', 'mp')
- up_new: float32 [768, 3072], P('dp', 'mp')
- down_grad: float32 [768, 3072], P('dp', 'mp')
- down_left_new: float32 [8, 4, 96, 96], P('dp', 'mp')
- down_right_new: float32 [8, 4, 768, 768], P('dp', 'mp')
- down_new: float32 [768, 3072], P('dp', 'mp')
- norm_grad: float32 [768, 4], P('dp')
- norm_second_new: float32 [768, 4], P('dp')
- norm_new: float32 [768, 4], P('dp')
Inputs may be any that keep to these rules, and one draw needn't show every extreme that they name: seq_lengths[m, 1023] = 16 in every micro-batch. `qkv_left`: symmetric positive definite blocks. `qkv_right`: symmetric positive definite blocks. `qkv_left_root`: symmetric positive definite blocks. `qkv_right_root`: symmetric positive definite blocks. `out_left`: symmetric positive definite blocks. `out_right`: symmetric positive definite blocks. `out_left_root`: symmetric positive definite blocks. `out_right_root`: symmetric positive definite blocks. `up_left`: symmetric positive definite blocks. `up_right`: symmetric positive definite blocks. `up_left_root`: symmetric positive definite blocks. `up_right_root`: symmetric positive definite blocks. `down_left`: symmetric positive definite blocks. `down_right`: symmetric positive definite blocks. `down_left_root`: symmetric positive definite blocks. `down_right_root`: symmetric positive definite blocks. `norm_params`: gains (columns 0 and 2) are positive.
All inputs are finite; a program needn't handle non-finite values.
Results may differ from a plain program's by a relative error of at most 0.022.
Values may be sent and summed in bfloat16 or wider, within the bound.
No kernel may reach another device: no remote copies, remote signals or barrier semaphores. Data moves between devices by JAX's collectives and lax.ppermute only.
A program may use at most 256 MiB of HBM per device.

v0:
```python
import math

import jax
import jax.numpy as jnp
from jax import lax
from jax.sharding import PartitionSpec as P

HD = 64


FULL_PRECISION = lax.Precision.HIGHEST
EPSILON = 1e-06
SOFTMAX_TEMP = 2.0
LOSS_SCALE = 32.0
STAT_DECAY = 0.5
SHAMPOO_RATE = 0.3
NORM_RATE = 0.5


def product(left_side, right_side, left_dim, right_dim):
    return lax.dot_general(
        left_side,
        right_side,
        (((left_dim,), (right_dim,)), ((), ())),
        preferred_element_type=jnp.float32,
    )


def layer_norm(values, norm_gain, norm_shift):
    center = values - jnp.mean(values, axis=-1, keepdims=True)
    spread = jnp.mean(center * center, axis=-1, keepdims=True)
    return center * lax.rsqrt(spread + EPSILON) * norm_gain + norm_shift


def text_norm(pooled):
    return pooled * lax.rsqrt(jnp.mean(pooled * pooled, axis=-1, keepdims=True) + EPSILON)


def exact_gelu(values):
    return jax.nn.gelu(values, approximate=False)


def pool_rows(outputs, live_mask):
    return jnp.sum(outputs * live_mask[:, :, None], axis=1) / jnp.sum(live_mask, axis=1)[:, None]


def spread_back(grad_pooled, live_mask):
    return (
        grad_pooled[:, None, :] * live_mask[:, :, None] / jnp.sum(live_mask, axis=1)[:, None, None]
    )


def shampoo(gradient, left_stat, right_stat, left_root, right_root, master):
    left_new = STAT_DECAY * left_stat + (1.0 - STAT_DECAY) * jnp.dot(
        gradient, gradient.T, precision=FULL_PRECISION
    )
    right_new = STAT_DECAY * right_stat + (1.0 - STAT_DECAY) * jnp.dot(
        gradient.T, gradient, precision=FULL_PRECISION
    )
    update = jnp.dot(
        jnp.dot(left_root, gradient, precision=FULL_PRECISION), right_root, precision=FULL_PRECISION
    )
    return (left_new[None, None], right_new[None, None], master - SHAMPOO_RATE * update)


def per_device(
    block_in,
    seq_lengths,
    image_embed,
    w_qkv,
    w_out,
    w_up,
    w_down,
    norm_params,
    norm_second,
    qkv_left,
    qkv_right,
    qkv_left_root,
    qkv_right_root,
    out_left,
    out_right,
    out_left_root,
    out_right_root,
    up_left,
    up_right,
    up_left_root,
    up_right_root,
    down_left,
    down_right,
    down_left_root,
    down_right_root,
):
    micro_count, seq_count, seq_len, width_model = block_in.shape
    mp_count = lax.axis_size("mp")
    dp_index = lax.axis_index("dp")
    mp_index = lax.axis_index("mp")
    row_block = w_qkv.shape[0]
    head_width = w_out.shape[1]
    ff_width = w_up.shape[1]
    head_count = head_width // HD
    full_qkv, full_out, full_up, full_down = (
        lax.all_gather(w_qkv.astype(jnp.bfloat16), "dp", axis=0, tiled=True),
        lax.all_gather(w_out.astype(jnp.bfloat16), "dp", axis=0, tiled=True),
        lax.all_gather(w_up.astype(jnp.bfloat16), "dp", axis=0, tiled=True),
        lax.all_gather(w_down.astype(jnp.bfloat16), "dp", axis=0, tiled=True),
    )
    full_qkv = full_qkv.reshape(width_model, 3 * head_width)
    image_pool = lax.all_gather(image_embed, ("dp", "mp"), axis=1, tiled=True)
    pool_count = image_pool.shape[1]
    group_seqs = mp_count * seq_count
    row_count = group_seqs * seq_len
    own_rows = seq_count * seq_len
    score_scale = HD ** (-0.5)
    scale_text = SOFTMAX_TEMP / math.sqrt(width_model)
    positions = jnp.arange(seq_len)
    grad_qkv = jnp.zeros((width_model, 3 * head_width), jnp.float32)
    grad_out = jnp.zeros((width_model, head_width), jnp.float32)
    grad_up = jnp.zeros((width_model, ff_width), jnp.float32)
    grad_down = jnp.zeros((width_model, ff_width), jnp.float32)
    grad_norm = jnp.zeros((width_model, 4), jnp.float32)
    block_list = []
    input_list = []
    loss_list = []
    for micro_step in range(micro_count):
        gathered, gathered_lengths = (
            lax.all_gather(block_in[micro_step], "mp", axis=0, tiled=True),
            lax.all_gather(seq_lengths[micro_step].astype(jnp.bfloat16), "mp", axis=0, tiled=True),
        )
        lengths_all = gathered_lengths.astype(jnp.int32)
        key_live = positions[None, :] < lengths_all[:, None]
        inputs = gathered.astype(jnp.float32).reshape(row_count, width_model)
        normed = layer_norm(inputs, norm_params[:, 0], norm_params[:, 1]).astype(jnp.bfloat16)
        projected = product(normed, full_qkv, 1, 0).astype(jnp.bfloat16)
        projected = projected.reshape(group_seqs, seq_len, 3, head_count, HD)
        queries = projected[:, :, 0]
        key_vecs = projected[:, :, 1]
        value_vecs = projected[:, :, 2]
        scores = (
            jnp.einsum("sqhe,skhe->shqk", queries, key_vecs, preferred_element_type=jnp.float32)
            * score_scale
        )
        scores = jnp.where(key_live[:, None, None, :], scores, -1e30)
        totals = jax.scipy.special.logsumexp(scores, axis=-1, keepdims=True)
        attn_probs = jnp.exp(scores - totals).astype(jnp.bfloat16)
        head_rows = jnp.einsum(
            "shqk,skhe->sqhe", attn_probs, value_vecs, preferred_element_type=jnp.float32
        )
        head_rows = head_rows.astype(jnp.bfloat16).reshape(row_count, head_width)
        attention_part = product(head_rows, full_out, 1, 1).astype(jnp.bfloat16)
        attended = lax.psum(attention_part, "mp").astype(jnp.float32)
        middle = inputs + attended
        normed_two = layer_norm(middle, norm_params[:, 2], norm_params[:, 3]).astype(jnp.bfloat16)
        up_rows = product(normed_two, full_up, 1, 0)
        hidden = exact_gelu(up_rows).astype(jnp.bfloat16)
        mlp_result = lax.psum_scatter(
            product(hidden, full_down, 1, 1).astype(jnp.bfloat16),
            "mp",
            scatter_dimension=0,
            tiled=True,
        ).astype(jnp.float32)
        own_middle = lax.dynamic_slice_in_dim(middle, mp_index * own_rows, own_rows, 0)
        outputs = (own_middle + mlp_result).reshape(seq_count, seq_len, width_model)
        block_list.append(outputs.astype(jnp.bfloat16))
        own_live = (positions[None, :] < seq_lengths[micro_step][:, None]).astype(jnp.float32)
        pooled = pool_rows(outputs, own_live)
        image_vectors = image_pool[micro_step]
        text_vector, text_back = jax.vjp(text_norm, pooled)
        pair_logits = product(text_vector.astype(jnp.bfloat16), image_vectors, 1, 1) * scale_text
        log_totals = jax.scipy.special.logsumexp(pair_logits, axis=-1, keepdims=True)
        targets = (dp_index * mp_count + mp_index) * seq_count + jnp.arange(seq_count)
        onehot = (jnp.arange(pool_count)[None, :] == targets[:, None]).astype(jnp.float32)
        loss_list.append(log_totals[:, 0] - jnp.sum(pair_logits * onehot, axis=1))
        grad_logits = (LOSS_SCALE * (jnp.exp(pair_logits - log_totals) - onehot)).astype(
            jnp.bfloat16
        )
        grad_text = product(grad_logits, image_vectors, 1, 0) * scale_text
        grad_own = spread_back(text_back(grad_text)[0], own_live).reshape(own_rows, width_model)
        grad_rows = lax.all_gather(grad_own.astype(jnp.bfloat16), "mp", axis=0, tiled=True).astype(
            grad_own.dtype
        )
        grad_low = grad_rows.astype(jnp.bfloat16)
        grad_down = grad_down + product(grad_low, hidden, 0, 0)
        unused_hidden, gelu_back = jax.vjp(exact_gelu, up_rows)
        grad_up_rows = gelu_back(product(grad_low, full_down, 1, 0))[0].astype(jnp.bfloat16)
        grad_up = grad_up + product(normed_two, grad_up_rows, 0, 0)
        grad_normed_two = lax.psum(
            product(grad_up_rows, full_up, 1, 1).astype(jnp.bfloat16), "mp"
        ).astype(jnp.float32)
        unused_two, norm_two_back = jax.vjp(
            layer_norm, middle, norm_params[:, 2], norm_params[:, 3]
        )
        grad_middle, grad_gain_two, grad_shift_two = norm_two_back(grad_normed_two)
        grad_middle = grad_middle + grad_rows
        grad_mid_low = grad_middle.astype(jnp.bfloat16)
        grad_out = grad_out + product(grad_mid_low, head_rows, 0, 0)
        grad_heads = product(grad_mid_low, full_out, 1, 0).astype(jnp.bfloat16)
        grad_heads = grad_heads.reshape(group_seqs, seq_len, head_count, HD)
        scores_again = (
            jnp.einsum("sqhe,skhe->shqk", queries, key_vecs, preferred_element_type=jnp.float32)
            * score_scale
        )
        scores_again = jnp.where(key_live[:, None, None, :], scores_again, -1e30)
        soft_probs = jnp.exp(scores_again - totals)
        grad_probs = jnp.einsum(
            "sqhe,skhe->shqk", grad_heads, value_vecs, preferred_element_type=jnp.float32
        )
        grad_values = jnp.einsum(
            "shqk,sqhe->skhe",
            soft_probs.astype(jnp.bfloat16),
            grad_heads,
            preferred_element_type=jnp.float32,
        ).astype(jnp.bfloat16)
        grad_scores = (
            soft_probs * (grad_probs - jnp.sum(grad_probs * soft_probs, axis=-1, keepdims=True))
        ).astype(jnp.bfloat16)
        grad_queries = (
            jnp.einsum("shqk,skhe->sqhe", grad_scores, key_vecs, preferred_element_type=jnp.float32)
            * score_scale
        ).astype(jnp.bfloat16)
        grad_keys = (
            jnp.einsum("shqk,sqhe->skhe", grad_scores, queries, preferred_element_type=jnp.float32)
            * score_scale
        ).astype(jnp.bfloat16)
        grad_proj = jnp.stack([grad_queries, grad_keys, grad_values], axis=2).reshape(
            row_count, 3 * head_width
        )
        grad_qkv = grad_qkv + product(normed, grad_proj, 0, 0)
        grad_normed = lax.psum(
            product(grad_proj, full_qkv, 1, 1).astype(jnp.bfloat16), "mp"
        ).astype(jnp.float32)
        unused_one, norm_back = jax.vjp(layer_norm, inputs, norm_params[:, 0], norm_params[:, 1])
        grad_inputs, grad_gain, grad_shift = norm_back(grad_normed)
        grad_inputs = grad_inputs + grad_middle
        own_grad = lax.dynamic_slice_in_dim(grad_inputs, mp_index * own_rows, own_rows, 0)
        input_list.append(own_grad.reshape(seq_count, seq_len, width_model))
        grad_norm = grad_norm + jnp.stack(
            [grad_gain, grad_shift, grad_gain_two, grad_shift_two], axis=1
        )
    summed_qkv, summed_out, summed_up, summed_down, summed_norm = (
        lax.psum_scatter(grad_qkv, "dp", scatter_dimension=0, tiled=True),
        lax.psum_scatter(grad_out, "dp", scatter_dimension=0, tiled=True),
        lax.psum_scatter(grad_up, "dp", scatter_dimension=0, tiled=True),
        lax.psum_scatter(grad_down, "dp", scatter_dimension=0, tiled=True),
        lax.psum_scatter(grad_norm, "dp", scatter_dimension=0, tiled=True),
    )
    qkv_left_new, qkv_right_new, qkv_moved = shampoo(
        summed_qkv,
        qkv_left[0, 0],
        qkv_right[0, 0],
        qkv_left_root[0, 0],
        qkv_right_root[0, 0],
        w_qkv.reshape(row_block, 3 * head_width),
    )
    out_left_new, out_right_new, out_new = shampoo(
        summed_out,
        out_left[0, 0],
        out_right[0, 0],
        out_left_root[0, 0],
        out_right_root[0, 0],
        w_out,
    )
    up_left_new, up_right_new, up_new = shampoo(
        summed_up, up_left[0, 0], up_right[0, 0], up_left_root[0, 0], up_right_root[0, 0], w_up
    )
    down_left_new, down_right_new, down_new = shampoo(
        summed_down,
        down_left[0, 0],
        down_right[0, 0],
        down_left_root[0, 0],
        down_right_root[0, 0],
        w_down,
    )
    norm_second_new = STAT_DECAY * norm_second + (1.0 - STAT_DECAY) * summed_norm * summed_norm
    own_params = lax.dynamic_slice_in_dim(norm_params, dp_index * row_block, row_block, 0)
    norm_new = own_params - NORM_RATE * summed_norm / (jnp.sqrt(norm_second_new) + 1e-08)
    return (
        jnp.stack(block_list, axis=0),
        jnp.stack(input_list, axis=0),
        jnp.stack(loss_list, axis=0),
        summed_qkv.reshape(row_block, 3, head_width),
        qkv_left_new,
        qkv_right_new,
        qkv_moved.reshape(row_block, 3, head_width),
        summed_out,
        out_left_new,
        out_right_new,
        out_new,
        summed_up,
        up_left_new,
        up_right_new,
        up_new,
        summed_down,
        down_left_new,
        down_right_new,
        down_new,
        summed_norm,
        norm_second_new,
        norm_new,
    )


def solution(mesh):
    in_specs = (
        P(None, ("dp", "mp"), None, None),
        P(None, ("dp", "mp")),
        P(None, ("dp", "mp"), None),
        P("dp", None, "mp"),
        P("dp", "mp"),
        P("dp", "mp"),
        P("dp", "mp"),
        P(),
        P("dp", None),
        P("dp", "mp", None, None),
        P("dp", "mp", None, None),
        P("dp", "mp", None, None),
        P("dp", "mp", None, None),
        P("dp", "mp", None, None),
        P("dp", "mp", None, None),
        P("dp", "mp", None, None),
        P("dp", "mp", None, None),
        P("dp", "mp", None, None),
        P("dp", "mp", None, None),
        P("dp", "mp", None, None),
        P("dp", "mp", None, None),
        P("dp", "mp", None, None),
        P("dp", "mp", None, None),
        P("dp", "mp", None, None),
        P("dp", "mp", None, None),
    )
    out_specs = (
        P(None, ("dp", "mp"), None, None),
        P(None, ("dp", "mp"), None, None),
        P(None, ("dp", "mp")),
        P("dp", None, "mp"),
        P("dp", "mp", None, None),
        P("dp", "mp", None, None),
        P("dp", None, "mp"),
        P("dp", "mp"),
        P("dp", "mp", None, None),
        P("dp", "mp", None, None),
        P("dp", "mp"),
        P("dp", "mp"),
        P("dp", "mp", None, None),
        P("dp", "mp", None, None),
        P("dp", "mp"),
        P("dp", "mp"),
        P("dp", "mp", None, None),
        P("dp", "mp", None, None),
        P("dp", "mp"),
        P("dp", None),
        P("dp", None),
        P("dp", None),
    )
    return jax.shard_map(
        per_device, mesh=mesh, in_specs=in_specs, out_specs=out_specs, check_vma=False
    )
```

profile of v0, /device:TPU:0, one launch (start us, length us, event | category | flops | bytes accessed | tf_op | source)
XLA Modules:
  0.0 1152.0 jit_solution(1195805430639177504)
XLA Ops:
  11.9 40.5 %all_gather.34 = bf16[768,3,192]{2,1,0:T(4,128)(2,1)} all-gather(bf16[96,3,192]{2,1,0:T(4,128)(2,1)S(1)} %copy.127), channel_id=1, replica_groups=mesh['dp'=8,'mp'=4] {'dp'}, dimensions={0}, use_global_device_ids=true | all-gather | bytes 995328 | tf_op jit(solution)/shard_map/all_gather | solution.py:102
  64.5 31.2 %all_gather.36 = bf16[768,192]{1,0:T(8,128)(2,1)S(1)} all-gather(bf16[96,192]{1,0:T(8,128)(2,1)S(1)} %convert_element_type.282), channel_id=1, replica_groups=mesh['dp'=8,'mp'=4] {'dp'}, dimensions={0}, use_global_device_ids=true | all-gather | bytes 331776 | tf_op jit(solution)/shard_map/all_gather | solution.py:103
  120.4 12.2 %reshape.649 = bf16[128,16,3,3,64]{4,3,2,1,0:T(4,128)(2,1)} reshape(bf16[2048,576]{1,0:T(8,128)(2,1)} %copy.137) | data formatting | bytes 4718592 | tf_op jit(solution)/shard_map/reshape | solution.py:134
  160.0 12.2 %reshape.646 = bf16[128,16,3,3,64]{4,3,2,1,0:T(4,128)(2,1)} reshape(bf16[2048,576]{1,0:T(8,128)(2,1)} %copy.129) | data formatting | bytes 4718592 | tf_op jit(solution)/shard_map/reshape | solution.py:134
  199.5 116.6 %all-reduce.14.cloned.1.call-done = (bf16[2048,768]{1,0:T(8,128)(2,1)}, bf16[2048,768]{1,0:T(8,128)(2,1)}) async-done(((bf16[2048,768]{1,0:T(8,128)(2,1)}, bf16[2048,768]{1,0:T(8,128)(2,1)}), (bf16[2048,768]{1,0:T(8,128)(2,1)}, bf16[2048,768]{1,0:T(8,128)(2,1)})) %all-reduce.14.cloned.1.call-update) | async-done | bytes 6291472 | tf_op jit(solution)/shard_map/psum | solution.py:150
  336.8 18.7 %multiply_convert_fusion = (bf16[2048,768]{1,0:T(8,128)(2,1)}, f32[2048,768]{1,0:T(8,128)}, f32[2048,768]{1,0:T(8,128)}) fusion(bf16[2048,768]{1,0:T(8,128)(2,1)} %get-tuple-element.172, bf16[768,768]{1,0:T(8,128)(2,1)} %all-gather.10.cloned.1.call-done), kind=kOutput, calls=%fused_computation.64 | convolution fusion | flops 2518155264 | bytes 20054016 | tf_op jit(solution)/shard_map/dot_general | solution.py:21
  363.3 18.5 %multiply_convert_fusion.1 = (bf16[2048,768]{1,0:T(8,128)(2,1)S(1)}, f32[2048,768]{1,0:T(8,128)}, f32[2048,768]{1,0:T(8,128)}) fusion(bf16[2048,768]{1,0:T(8,128)(2,1)} %get-tuple-element.171, bf16[768,768]{1,0:T(8,128)(2,1)S(1)} %copy-done.122), kind=kOutput, calls=%fused_computation.79 | convolution fusion | flops 2518155264 | bytes 20054016 | tf_op jit(solution)/shard_map/dot_general | solution.py:21
  388.9 11.5 reduce-scatter.12.cloned.1.call-done
  403.6 37.6 %reduce-scatter.10.cloned.1.call-done = bf16[512,768]{1,0:T(8,128)(2,1)} async-done(((bf16[2048,768]{1,0:T(8,128)(2,1)}), bf16[512,768]{1,0:T(8,128)(2,1)}) %reduce-scatter.10.cloned.1.call-update) | async-done | bytes 786448 | tf_op jit(solution)/shard_map/reduce_scatter | solution.py:155
  444.4 9.9 all-gather.14.cloned.1.call-done
  465.7 23.5 %all-gather.18.cloned.1.call-done = bf16[2048,768]{1,0:T(8,128)(2,1)} async-done(((bf16[512,768]{1,0:T(8,128)(2,1)}), bf16[2048,768]{1,0:T(8,128)(2,1)}) %all-gather.18.cloned.1.call-update) | async-done | bytes 3145744 | tf_op jit(solution)/shard_map/all_gather | solution.py:178
  489.3 10.1 add_convert_fusion
  505.1 14.8 %all-gather.16.cloned.1.call-done = bf16[2048,768]{1,0:T(8,128)(2,1)} async-done(((bf16[512,768]{1,0:T(8,128)(2,1)}), bf16[2048,768]{1,0:T(8,128)(2,1)}) %all-gather.16.cloned.1.call-update) | async-done | bytes 3145744 | tf_op jit(solution)/shard_map/all_gather | solution.py:178
  520.0 10.1 add_convert_fusion.1
  536.0 119.7 %all-reduce.12.cloned.1.call-done = (bf16[2048,768]{1,0:T(8,128)(2,1)}, bf16[2048,768]{1,0:T(8,128)(2,1)}) async-done(((bf16[2048,768]{1,0:T(8,128)(2,1)}, bf16[2048,768]{1,0:T(8,128)(2,1)}), (bf16[2048,768]{1,0:T(8,128)(2,1)}, bf16[2048,768]{1,0:T(8,128)(2,1)})) %all-reduce.12.cloned.1.call-update) | async-done | bytes 6291472 | tf_op jit(solution)/shard_map/psum | solution.py:186
  662.3 9.5 fusion.14
  672.0 8.7 fusion.16
  735.8 11.6 %reshape.656 = bf16[2048,576]{1,0:T(8,128)(2,1)} reshape(bf16[128,16,3,3,64]{4,3,2,1,0:T(4,128)(2,1)} %copy.152) | data formatting | bytes 4718592 | tf_op jit(solution)/shard_map/reshape | solution.py:224
  761.5 11.6 %reshape.653 = bf16[2048,576]{1,0:T(8,128)(2,1)} reshape(bf16[128,16,3,3,64]{4,3,2,1,0:T(4,128)(2,1)} %copy.147) | data formatting | bytes 4718592 | tf_op jit(solution)/shard_map/reshape | solution.py:224
  826.4 72.8 %all-reduce.10.cloned.1.call-done = (bf16[2048,768]{1,0:T(8,128)(2,1)}, bf16[2048,768]{1,0:T(8,128)(2,1)}) async-done(((bf16[2048,768]{1,0:T(8,128)(2,1)}, bf16[2048,768]{1,0:T(8,128)(2,1)}), (bf16[2048,768]{1,0:T(8,128)(2,1)}, bf16[2048,768]{1,0:T(8,128)(2,1)})) %all-reduce.10.cloned.1.call-update) | async-done | bytes 6291472 | tf_op jit(solution)/shard_map/psum | solution.py:228
  899.2 8.6 fusion.15
  934.3 64.6 %reduce-scatter.20.cloned.1.call-done = f32[96,768]{1,0:T(8,128)} async-done(((f32[768,768]{1,0:T(8,128)}), f32[96,768]{1,0:T(8,128)}) %reduce-scatter.20.cloned.1.call-update) | async-done | bytes 294928 | tf_op jit(solution)/shard_map/reduce_scatter | solution.py:243
  1024.5 38.4 %reduce-scatter.22.cloned.1.call-done = f32[96,4]{1,0:T(8,128)} async-done(((f32[768,4]{1,0:T(8,128)}), f32[96,4]{1,0:T(8,128)}) %reduce-scatter.22.cloned.1.call-update) | async-done | bytes 1552
  1065.1 67.6 %reduce-scatter.14.cloned.1.call-done = f32[96,576]{1,0:T(8,128)} async-done(((f32[768,576]{1,0:T(8,128)}), f32[96,576]{1,0:T(8,128)}) %reduce-scatter.14.cloned.1.call-update) | async-done | bytes 221200 | tf_op jit(solution)/shard_map/reduce_scatter | solution.py:240
  (485 shorter events, 353.4 us)
Async XLA Ops:
  8.0 999.0 %copy-start = (f32[1,1,768,768]{3,2,1,0:T(8,128)S(1)}, f32[1,1,768,768]{3,2,1,0:T(8,128)}, u32[]{:S(2)}) copy-start(f32[1,1,768,768]{3,2,1,0:T(8,128)} %param.45) | copy-start | bytes 7077892
  8.1 87.9 %all-gather.20.cloned.1.call-start = ((), (), s32[]{:S(2)}) async-start(), calls=%async_computation.18 | async-start | bytes 3932160 | tf_op jit(solution)/shard_map/all_gather | solution.py:126
  10.9 89.5 %all-gather.22.cloned.1.call-start = ((), (), s32[]{:S(2)}) async-start(), calls=%async_computation.19 | async-start | bytes 3932160 | tf_op jit(solution)/shard_map/all_gather | solution.py:126
  11.7 304.4 %all-reduce.14.cloned.1.call-start = ((), (), s32[]{:S(2)}) async-start(), calls=%async_computation.23 | async-start | bytes 12582912 | tf_op jit(solution)/shard_map/psum | solution.py:150
  64.5 266.8 %copy-start.86 = (f32[768]{0:T(1024)}, f32[768]{0:T(1024)S(1)}, u32[]{:S(2)}) copy-start(f32[768]{0:T(1024)S(1)} %get-tuple-element.126) | copy-start | bytes 9220
  197.0 139.8 %all-gather.10.cloned.1.call-start = ((), (), s32[]{:S(2)}) async-start(), calls=%async_computation.7 | async-start | bytes 1327104 | tf_op jit(solution)/shard_map/all_gather | solution.py:104
  198.7 156.9 %all-gather.12.cloned.1.call-start = ((), (), s32[]{:S(2)}) async-start(), calls=%async_computation.8 | async-start | bytes 1327104 | tf_op jit(solution)/shard_map/all_gather | solution.py:105
  199.4 201.0 %reduce-scatter.12.cloned.1.call-start = ((), (), s32[]{:S(2)}) async-start(), calls=%async_computation.10 | async-start | bytes 3932160 | tf_op jit(solution)/shard_map/reduce_scatter | solution.py:155
  362.1 79.1 %reduce-scatter.10.cloned.1.call-start = ((), (), s32[]{:S(2)}) async-start(), calls=%async_computation.9 | async-start | bytes 3932160 | tf_op jit(solution)/shard_map/reduce_scatter | solution.py:155
  387.5 66.8 %all-gather.14.cloned.1.call-start = ((), (), s32[]{:S(2)}) async-start(), calls=%async_computation.11 | async-start | bytes 3244032 | tf_op jit(solution)/shard_map/all_gather | solution.py:108
  388.1 101.2 %all-gather.18.cloned.1.call-start = ((), (), s32[]{:S(2)}) async-start(), calls=%async_computation.13 | async-start | bytes 3932160 | tf_op jit(solution)/shard_map/all_gather | solution.py:178
  461.8 58.2 %all-gather.16.cloned.1.call-start = ((), (), s32[]{:S(2)}) async-start(), calls=%async_computation.12 | async-start | bytes 3932160 | tf_op jit(solution)/shard_map/all_gather | solution.py:178
  465.3 190.5 %all-reduce.12.cloned.1.call-start = ((), (), s32[]{:S(2)}) async-start(), calls=%async_computation.22 | async-start | bytes 12582912 | tf_op jit(solution)/shard_map/psum | solution.py:186
  535.8 120.0 %copy-start.79 = (f32[2048]{0:T(1024)S(1)}, f32[2048]{0:T(1024)}, u32[]{:S(2)}) copy-start(f32[2048]{0:T(1024)} %copy-done.78) | copy-start | bytes 24580
  535.8 120.0 %copy-start.87 = (f32[768]{0:T(1024)S(1)}, f32[768]{0:T(1024)}, u32[]{:S(2)}) copy-start(f32[768]{0:T(1024)} %copy-done.86) | copy-start | bytes 9220
  535.8 125.7 %copy-start.95 = (f32[2048]{0:T(1024)S(1)}, f32[2048]{0:T(1024)}, u32[]{:S(2)}) copy-start(f32[2048]{0:T(1024)} %copy-done.94) | copy-start | bytes 24580
  535.8 363.4 %all-reduce.10.cloned.1.call-start = ((), (), s32[]{:S(2)}) async-start(), calls=%async_computation.21 | async-start | bytes 12582912 | tf_op jit(solution)/shard_map/psum | solution.py:228
  779.1 137.6 %reduce-scatter.16.cloned.1.call-start = ((), (), s32[]{:S(2)}) async-start(), calls=%async_computation.15 | async-start | bytes 884736 | tf_op jit(solution)/shard_map/reduce_scatter | solution.py:241
  789.8 136.5 %reduce-scatter.18.cloned.1.call-start = ((), (), s32[]{:S(2)}) async-start(), calls=%async_computation.16 | async-start | bytes 2654208 | tf_op jit(solution)/shard_map/reduce_scatter | solution.py:242
  800.1 198.8 %reduce-scatter.20.cloned.1.call-start = ((), (), s32[]{:S(2)}) async-start(), calls=%async_computation.17 | async-start | bytes 2654208 | tf_op jit(solution)/shard_map/reduce_scatter | solution.py:243
  810.3 252.6 %reduce-scatter.22.cloned.1.call-start = ((), (), s32[]{:S(2)}) async-start(), calls=%async_computation.20 | async-start | bytes 442368
  908.9 223.7 %reduce-scatter.14.cloned.1.call-start = ((), (), s32[]{:S(2)}) async-start(), calls=%async_computation.14 | async-start | bytes 2211840 | tf_op jit(solution)/shard_map/reduce_scatter | solution.py:240
  1022.6 113.4 %copy-start.71 = (f32[96,576]{1,0:T(8,128)S(1)}, f32[96,576]{1,0:T(8,128)}, u32[]{:S(2)}) copy-start(f32[96,576]{1,0:T(8,128)} %copy.155) | copy-start | bytes 663556
  1024.5 115.1 %copy-start.102 = (f32[1,1,96,96]{3,2,1,0:T(8,128)S(1)}, f32[1,1,96,96]{3,2,1,0:T(8,128)}, u32[]{:S(2)}) copy-start(f32[1,1,96,96]{3,2,1,0:T(8,128)} %param.34) | copy-start | bytes 110596
  (123 other events, 1672.1 us)
Sparse Core Ops, SparseCore 0:
  11.0 31.2 all-gather.19
  44.4 28.6 all-gather.21
  197.2 118.9 all-reduce.13
  362.2 38.1 reduce-scatter.11
  402.9 38.2 reduce-scatter.9
  461.9 27.3 all-gather.17
  491.4 28.5 all-gather.15
  535.9 119.7 all-reduce.11
  779.2 120.0 all-reduce.9
Sparse Core Ops, SparseCore 1:
  200.3 40.5 all-gather.9
  243.5 40.0 all-gather.11
  390.9 63.4 all-gather.13
  789.9 63.0 reduce-scatter.15
  858.0 68.2 reduce-scatter.17
  930.8 68.0 reduce-scatter.19
  1002.3 60.5 reduce-scatter.21
  1066.6 66.0 reduce-scatter.13
where the time goes:
time: 1160 us; the launch traced here: 1150 us
  waiting for transfers between devices  582 us (50%)
  matrix products  224 us (19%)
  local copies, waits for them, and re-layouts  143 us (12%)
  other arithmetic  105 us (9%)
  blocking collectives  77.9 us (7%)
  between operations  18.1 us (2%)
    dot_general x28, matrix products, product(): lax.dot_general(left_side, right_side, (((left_dim,), (right_dim,)), ((),...  157 us
    psum x1, waiting for transfers between devices, per_device(): lax.psum(product(grad_up_rows, full_up, 1, 1).astype(jnp.bfloat16), 'mp')  120 us
    psum x1, waiting for transfers between devices, per_device(): attended = lax.psum(attention_part, 'mp').astype(jnp.float32)  117 us
    psum x1, waiting for transfers between devices, per_device(): lax.psum(product(grad_proj, full_qkv, 1, 1).astype(jnp.bfloat16), 'mp')  72.8 us
    reduce_scatter x1, waiting for transfers between devices, per_device(): lax.psum_scatter(grad_qkv, 'dp', scatter_dimension=0, tiled=True)  67.6 us
    reduce_scatter x1, waiting for transfers between devices, per_device(): lax.psum_scatter(grad_down, 'dp', scatter_dimension=0, tiled=True)  64.6 us
    reduce_scatter x2, waiting for transfers between devices, per_device(): lax.psum_scatter(product(hidden, full_down, 1, 1).astype(jnp.bfloat16), '...  49.1 us
    all_gather x1, blocking collectives, per_device(): lax.all_gather(w_qkv.astype(jnp.bfloat16), 'dp', axis=0, tiled=True)  40.5 us
  transfers between devices with their start and end apart: 17, of which 12 were waited for; matrix products, arithmetic and copies ran while one was open for 17% of the time, Pallas kernels for 0%

commit v1 on v0

v1 whole, which is shorter than its diff:
```python
import functools
import math

import jax
import jax.numpy as jnp
import numpy as np
from jax import lax
from jax.experimental import pallas as pl
from jax.experimental.pallas import tpu as pltpu
from jax.sharding import PartitionSpec as P

AXES = ("dp", "mp")
HD = 64
LANES = 128
EPSILON = 1e-06
SOFTMAX_TEMP = 2.0
LOSS_SCALE = 32.0
STAT_DECAY = 0.5
SHAMPOO_RATE = 0.3
NORM_RATE = 0.5
TILE = 256
VMEM_BYTES = 56 * 1024 * 1024
F32 = jnp.float32
BF16 = jnp.bfloat16


def exchange_steps(count):
    steps = []
    bit = count // 2
    while bit >= 8:
        steps.append([i ^ bit for i in range(count)])
        bit //= 2
    steps.append([i ^ (4 if i % 2 == 0 else 2) for i in range(count)])
    steps.append([i ^ (2 if i % 2 == 0 else 4) for i in range(count)])
    steps.append([i ^ 1 for i in range(count)])
    return steps


def source_table(count):
    table = np.arange(count)[:, None]
    for step in exchange_steps(count):
        table = np.concatenate([table, table[np.array(step)]], axis=1)
    return table


def swap(values, step):
    return lax.ppermute(values, AXES, list(enumerate(step)))


def gather_blocks(block, count):
    steps = exchange_steps(count)
    held = block[None]
    for step in steps[:-1]:
        held = jnp.concatenate([held, swap(held, step)], axis=0)
    return held, swap(held, steps[-1])


def sum_blocks(keep, send, count):
    steps = exchange_steps(count)
    received = swap(send, steps[-1])
    for step in steps[-2::-1]:
        half = keep.shape[0] // 2
        going = (keep[half:].astype(F32) + received[half:].astype(F32)).astype(BF16)
        keep = (keep[:half].astype(F32) + received[:half].astype(F32)).astype(BF16)
        received = swap(going, step)
    return keep[0].astype(F32) + received[0].astype(F32)


def dot(left, right, left_dim, right_dim):
    return lax.dot_general(
        left, right, (((left_dim,), (right_dim,)), ((), ())), preferred_element_type=F32
    )


def load_weights(order, own, other, weights, sems):
    half, rows, _ = own.shape
    groups = weights.shape[0]

    def start(q, base, ref):
        index = order[base + q]
        group = index % groups
        place = pl.multiple_of((index // groups) * rows, 16)
        pltpu.make_async_copy(
            ref.at[q], weights.at[group, pl.ds(place, rows), :], sems.at[group]
        ).start()

    def body(q, carry):
        start(q, 0, own)
        start(q, half, other)
        return carry

    lax.fori_loop(0, half, body, 0)


def wait_weights(weights, sems, group):
    pltpu.make_async_copy(weights.at[group], weights.at[group], sems.at[group]).wait()


def normalize(values):
    center = values - jnp.mean(values, axis=-1, keepdims=True)
    spread = jnp.mean(center * center, axis=-1, keepdims=True)
    scale = lax.rsqrt(spread + EPSILON)
    return center * scale, scale


def low_lanes(dtype=BF16):
    lane = lax.broadcasted_iota(jnp.int32, (1, LANES), 1)
    return jnp.where(lane < HD, 1.0, 0.0).astype(dtype)


def masked_scores(queries, keys, allowed):
    return jnp.where(allowed, dot(queries, keys, 1, 1) * (HD**-0.5), -1e30)


def allowed_pairs(key_live, seq_len):
    rows = lax.broadcasted_iota(jnp.int32, (LANES, LANES), 0) // seq_len
    cols = lax.broadcasted_iota(jnp.int32, (LANES, LANES), 1) // seq_len
    return jnp.logical_and(rows == cols, key_live > 0.0)


def attention_forward(
    order, x_ref, live_ref, norm_ref, own_ref, other_ref,
    h1_ref, proj_ref, heads_ref, lse_ref, mid_ref, h2_ref,
    weights, sems, *, seq_len,
):
    groups = weights.shape[0]
    first = pl.program_id(0) == 0

    @pl.when(first)
    def _():
        load_weights(order, own_ref, other_ref, weights, sems)

    x = x_ref[...].astype(F32)
    rows = x.shape[0]
    n1, _ = normalize(x)
    h1 = (n1 * norm_ref[0:1, :] + norm_ref[1:2, :]).astype(BF16)
    h1_ref[...] = h1
    low = low_lanes()
    high = 1 - low
    is_low = lax.broadcasted_iota(jnp.int32, (1, LANES), 1) < HD
    lane = lax.broadcasted_iota(jnp.int32, (1, LANES), 1)
    allowed = [allowed_pairs(live_ref[t], seq_len) for t in range(rows // LANES)]
    total = x
    lse_tiles = [jnp.zeros((LANES, LANES), F32) for _ in allowed]
    for group in range(groups):

        @pl.when(first)
        def _():
            wait_weights(weights, sems, group)

        proj = dot(h1, weights[group, :, : 5 * LANES], 1, 0).astype(BF16)
        proj_ref[:, group * 5 * LANES : (group + 1) * 5 * LANES] = proj
        parts = []
        for t, pairs in enumerate(allowed):
            b = [
                proj[t * LANES : (t + 1) * LANES, i * LANES : (i + 1) * LANES]
                for i in range(5)
            ]
            outs = []
            for h, (q, k, v) in enumerate(
                ((b[0] * low, b[1], b[2]), (b[0] * high, b[1], b[2]), (b[3] * low, b[4], b[3]))
            ):
                scores = masked_scores(q, k, pairs)
                top = jnp.max(scores, axis=1, keepdims=True)
                powers = jnp.exp(scores - top)
                total_power = jnp.sum(powers, axis=1, keepdims=True)
                lse_tiles[t] = jnp.where(
                    lane == group * 3 + h, top + jnp.log(total_power), lse_tiles[t]
                )
                probs = (powers * (1.0 / total_power)).astype(BF16)
                outs.append(dot(probs, v, 1, 0))
            parts.append(
                jnp.concatenate(
                    [jnp.where(is_low, 0.0, outs[2]), jnp.where(is_low, outs[0], outs[1])],
                    axis=1,
                ).astype(BF16)
            )
        heads = jnp.concatenate(parts, axis=0)
        heads_ref[:, group * 2 * LANES : (group + 1) * 2 * LANES] = heads
        total = total + dot(heads, weights[group, :, 4 * LANES :], 1, 1)
    for t, tile in enumerate(lse_tiles):
        lse_ref[t * LANES : (t + 1) * LANES, :] = tile
    mid_ref[...] = total
    n2, _ = normalize(total)
    h2_ref[...] = (n2 * norm_ref[2:3, :] + norm_ref[3:4, :]).astype(BF16)


def up_forward(
    order, h2_ref, live_ref, own_ref, other_ref,
    hid_ref, slope_ref, pooled_ref,
    weights, sems, *, seq_len,
):
    groups, _, width = weights.shape
    first = pl.program_id(0) == 0

    @pl.when(first)
    def _():
        load_weights(order, own_ref, other_ref, weights, sems)

    h2 = h2_ref[...]
    rows = h2.shape[0]
    live = live_ref[:, 0:1]
    seqs = rows // seq_len
    member = (
        lax.broadcasted_iota(jnp.int32, (seqs, rows), 1) // seq_len
        == lax.broadcasted_iota(jnp.int32, (seqs, rows), 0)
    )
    pool = jnp.where(member, 1.0, 0.0).astype(BF16)
    for group in range(groups):

        @pl.when(first)
        def _():
            wait_weights(weights, sems, group)

        cols = slice(group * width, (group + 1) * width)
        up = dot(h2, weights[group], 1, 0)
        gate = 0.5 + 0.5 * lax.erf(up * (0.5**0.5))
        hid = (up * gate).astype(BF16)
        hid_ref[:, cols] = hid
        bell = jnp.exp(up * up * -0.5) * (1.0 / math.sqrt(2.0 * math.pi))
        slope_ref[:, cols] = ((gate + up * bell) * live).astype(BF16)
        pooled_ref[:, cols] = dot(pool, hid * live.astype(BF16), 1, 0).astype(BF16)


def down_forward(
    order, hid_ref, mid_ref, live_ref, own_ref, other_ref,
    out_ref, pooled_ref, weights, sems, *, seq_len,
):
    groups, _, width = weights.shape
    first = pl.program_id(0) == 0

    @pl.when(first)
    def _():
        load_weights(order, own_ref, other_ref, weights, sems)

    total = mid_ref[...]
    for group in range(groups):

        @pl.when(first)
        def _():
            wait_weights(weights, sems, group)

        total = total + dot(
            hid_ref[:, group * width : (group + 1) * width], weights[group], 1, 1
        )
    out_ref[...] = total.astype(BF16)
    live = live_ref[:, 0:1]
    rows, features = total.shape
    seqs = rows // seq_len
    sums = jnp.sum((total * live).reshape(seqs, seq_len, features), axis=1)
    counts = jnp.sum(jnp.broadcast_to(live, (rows, LANES)).reshape(seqs, seq_len, LANES), axis=1)
    pooled_ref[...] = sums / counts[:, 0:1]


def contrast(pooled_ref, count_ref, own_ref, other_ref, loss_ref, grad_ref, low_ref, *, micros):
    pooled = pooled_ref[...]
    seqs, width = pooled.shape
    each = seqs // micros
    scale_text = SOFTMAX_TEMP / math.sqrt(width)
    r = lax.rsqrt(jnp.mean(pooled * pooled, axis=-1, keepdims=True) + EPSILON)
    text = (pooled * r).astype(BF16)
    row_micro = lax.broadcasted_iota(jnp.int32, (seqs, 1), 0) // each
    step = min(own_ref.shape[0], 1024)
    pieces = [
        ref[i : i + step, :]
        for ref in (own_ref, other_ref)
        for i in range(0, ref.shape[0], step)
    ]
    col = lax.broadcasted_iota(jnp.int32, (1, step), 1)
    same = (col // each) % micros == row_micro
    logits = [jnp.where(same, dot(text, piece, 1, 1) * scale_text, -1e30) for piece in pieces]
    top = functools.reduce(
        jnp.maximum, [jnp.max(part, axis=1, keepdims=True) for part in logits]
    )
    powers = [jnp.exp(part - top) for part in logits]
    total = functools.reduce(jnp.add, [jnp.sum(part, axis=1, keepdims=True) for part in powers])
    log_total = top + jnp.log(total)
    positive = lax.broadcasted_iota(jnp.int32, (seqs, 1), 0) == col
    loss = log_total - jnp.sum(jnp.where(positive, logits[0], 0.0), axis=1, keepdims=True)
    loss_ref[...] = jnp.broadcast_to(loss, loss_ref.shape)
    inverse = LOSS_SCALE / total
    grad_text = jnp.zeros((seqs, width), F32)
    for i, (part, piece) in enumerate(zip(powers, pieces)):
        grad_part = part * inverse
        if i == 0:
            grad_part = grad_part - jnp.where(positive, LOSS_SCALE, 0.0)
        grad_text = grad_text + dot(grad_part.astype(BF16), piece, 1, 0)
    grad_text = grad_text * scale_text
    along = jnp.mean(grad_text * pooled, axis=-1, keepdims=True)
    grad = (r * grad_text - (r * r * r) * pooled * along) / count_ref[:, 0:1]
    grad_ref[...] = grad
    low_ref[...] = grad.astype(BF16)


def weight_gradient(
    inverse, left_ref, right_ref, keep_ref, send_ref, turned, slots, sems, *extra, shared_cols
):
    group = pl.program_id(0)
    groups = pl.num_programs(0)
    half, rows, _ = keep_ref.shape
    depth = slots.shape[1]

    @pl.when(group == 0)
    def _():
        turned[...] = left_ref[...].T

    slot = group % 2

    def drain(which):
        pltpu.make_async_copy(slots.at[which], slots.at[which], sems.at[which]).wait()

    @pl.when(group >= 2)
    def _():
        drain(slot)

    slots[slot] = dot(turned[...], right_ref[...], 1, 0).astype(BF16)

    def body(p, carry):
        position = inverse[p * groups + group]
        source = slots.at[slot, pl.ds(pl.multiple_of(p * rows, 16), rows), :]

        @pl.when(position < half)
        def _():
            pltpu.make_async_copy(source, keep_ref.at[position], sems.at[slot]).start()

        @pl.when(position >= half)
        def _():
            pltpu.make_async_copy(source, send_ref.at[position - half], sems.at[slot]).start()

        return carry

    lax.fori_loop(0, depth // rows, body, 0)

    @pl.when(group == groups - 1)
    def _():
        drain(slot)

        @pl.when(groups >= 2)
        def _():
            drain(1 - slot)


def attention_gradient(
    inverse, h1_ref, proj_ref, mid_ref, heads_ref, keep_ref, send_ref,
    turned, turned_mid, slots, sems,
):
    group = pl.program_id(0)
    groups = pl.num_programs(0)
    half, rows, _ = keep_ref.shape
    depth = slots.shape[1]

    @pl.when(group == 0)
    def _():
        turned[...] = h1_ref[...].T
        turned_mid[...] = mid_ref[...].T

    slot = group % 2

    def drain(which):
        pltpu.make_async_copy(slots.at[which], slots.at[which], sems.at[which]).wait()

    @pl.when(group >= 2)
    def _():
        drain(slot)

    slots[slot, :, : 4 * LANES] = dot(turned[...], proj_ref[:, : 4 * LANES], 1, 0).astype(BF16)
    tail = dot(turned_mid[...], heads_ref[...], 1, 0)
    keys = dot(turned[...], proj_ref[:, 4 * LANES :], 1, 0)
    slots[slot, :, 4 * LANES : 5 * LANES] = (keys + tail[:, :LANES]).astype(BF16)
    slots[slot, :, 5 * LANES :] = tail[:, LANES:].astype(BF16)

    def body(p, carry):
        position = inverse[p * groups + group]
        source = slots.at[slot, pl.ds(pl.multiple_of(p * rows, 16), rows), :]

        @pl.when(position < half)
        def _():
            pltpu.make_async_copy(source, keep_ref.at[position], sems.at[slot]).start()

        @pl.when(position >= half)
        def _():
            pltpu.make_async_copy(source, send_ref.at[position - half], sems.at[slot]).start()

        return carry

    lax.fori_loop(0, depth // rows, body, 0)

    @pl.when(group == groups - 1)
    def _():
        drain(slot)

        @pl.when(groups >= 2)
        def _():
            drain(1 - slot)


def norm_back(grad, gain, values):
    n, scale = normalize(values)
    scaled = grad * gain
    moved = scale * (
        scaled
        - jnp.mean(scaled, axis=-1, keepdims=True)
        - n * jnp.mean(scaled * n, axis=-1, keepdims=True)
    )
    gain_grad = jnp.sum(grad * n, axis=0, keepdims=True)
    shift_grad = jnp.sum(grad, axis=0, keepdims=True)
    return moved, gain_grad, shift_grad


def mlp_backward(
    order, grad_ref, low_ref, slope_ref, live_ref, mid_ref, norm_ref,
    up_own, up_other, down_own, down_other,
    dup_ref, dmid_ref, dmid_low_ref, sums_ref,
    up_w, down_w, up_sems, down_sems, *, seq_len,
):
    groups, _, width = up_w.shape
    first = pl.program_id(0) == 0

    @pl.when(first)
    def _():
        load_weights(order, down_own, down_other, down_w, down_sems)
        load_weights(order, up_own, up_other, up_w, up_sems)
        sums_ref[...] = jnp.zeros_like(sums_ref)

    grad = grad_ref[...]
    low = low_ref[...]
    mid = mid_ref[...]
    rows, features = mid.shape
    seqs = rows // seq_len

    def spread(values):
        return jnp.broadcast_to(
            values[:, None, :], (seqs, seq_len, values.shape[1])
        ).reshape(rows, values.shape[1])

    total = jnp.zeros((rows, features), F32)
    for group in range(groups):

        @pl.when(first)
        def _():
            wait_weights(down_w, down_sems, group)
            wait_weights(up_w, up_sems, group)

        cols = slice(group * width, (group + 1) * width)
        by_seq = dot(low, down_w[group], 1, 0)
        dup = (slope_ref[:, cols].astype(F32) * spread(by_seq)).astype(BF16)
        dup_ref[:, cols] = dup
        total = total + dot(dup, up_w[group], 1, 1)
    moved, gain_grad, shift_grad = norm_back(total, norm_ref[2:3, :], mid)
    dmid = spread(grad) * live_ref[:, 0:1] + moved
    dmid_ref[...] = dmid
    dmid_low_ref[...] = dmid.astype(BF16)
    sums_ref[0:1, :] += gain_grad
    sums_ref[1:2, :] += shift_grad


def attention_backward(
    order, x_ref, live_ref, norm_ref, proj_ref, lse_ref, dmid_ref, dmid_low_ref,
    own_ref, other_ref,
    dproj_ref, dx_ref, sums_ref,
    weights, sems, *, seq_len,
):
    groups = weights.shape[0]
    first = pl.program_id(0) == 0

    @pl.when(first)
    def _():
        load_weights(order, own_ref, other_ref, weights, sems)
        sums_ref[...] = jnp.zeros_like(sums_ref)

    x = x_ref[...].astype(F32)
    rows = x.shape[0]
    dmid_low = dmid_low_ref[...]
    low = low_lanes()
    high = 1 - low
    is_low = lax.broadcasted_iota(jnp.int32, (1, LANES), 1) < HD
    allowed = [allowed_pairs(live_ref[t], seq_len) for t in range(rows // LANES)]
    score_scale = HD**-0.5
    total = jnp.zeros(x.shape, F32)
    for group in range(groups):

        @pl.when(first)
        def _():
            wait_weights(weights, sems, group)

        dheads = dot(dmid_low, weights[group, :, 4 * LANES :], 1, 0).astype(BF16)
        parts = []
        for t, pairs in enumerate(allowed):
            span = slice(t * LANES, (t + 1) * LANES)
            base = group * 5 * LANES
            b = [proj_ref[span, base + i * LANES : base + (i + 1) * LANES] for i in range(5)]
            d0 = dheads[span, :LANES]
            d1 = dheads[span, LANES:]
            grads = []
            for h, (q_sel, q, k, d_sel, v) in enumerate(
                (
                    (low, b[0], b[1], d1 * low, b[2]),
                    (high, b[0], b[1], d1 * high, b[2]),
                    (low, b[3], b[4], d0 * high, b[3]),
                )
            ):
                scores = masked_scores(q * q_sel, k, pairs)
                column = group * 3 + h
                probs = jnp.exp(scores - lse_ref[span, column : column + 1])
                dprobs = dot(d_sel, v, 1, 1)
                inner = jnp.sum(probs * dprobs, axis=1, keepdims=True)
                dscores = (probs * (dprobs - inner) * score_scale).astype(BF16)
                d_full = d0 if h == 2 else d1
                grads.append(
                    (
                        dot(dscores, k, 1, 0),
                        dot(dscores, q, 0, 0),
                        dot(probs.astype(BF16), d_full, 0, 0),
                    )
                )
            blocks = (
                jnp.where(is_low, grads[0][0], grads[1][0]),
                jnp.where(is_low, grads[0][1], grads[1][1]),
                jnp.where(is_low, grads[0][2], grads[1][2]),
                jnp.where(is_low, grads[2][0], grads[2][2]),
                jnp.where(is_low, grads[2][1], 0.0),
            )
            parts.append(jnp.concatenate(blocks, axis=1).astype(BF16))
        dproj = jnp.concatenate(parts, axis=0)
        dproj_ref[:, group * 5 * LANES : (group + 1) * 5 * LANES] = dproj
        total = total + dot(dproj, weights[group, :, : 5 * LANES], 1, 1)
    moved, gain_grad, shift_grad = norm_back(total, norm_ref[0:1, :], x)
    dx_ref[...] = dmid_ref[...] + moved
    sums_ref[0:1, :] += gain_grad
    sums_ref[1:2, :] += shift_grad


def shampoo_kernel(
    grad_ref, left_ref, right_ref, left_root_ref, right_root_ref, master_ref,
    left_new_ref, right_new_ref, new_ref,
):
    grad = grad_ref[...]
    low = grad.astype(BF16)
    keep = 1.0 - STAT_DECAY
    left_new_ref[...] = STAT_DECAY * left_ref[...] + keep * dot(low, low, 1, 1)
    right_new_ref[...] = STAT_DECAY * right_ref[...] + keep * dot(low, low, 0, 0)
    half = dot(left_root_ref[...].astype(BF16), low, 1, 0).astype(BF16)
    update = dot(half, right_root_ref[...].astype(BF16), 1, 0)
    new_ref[...] = master_ref[...] - SHAMPOO_RATE * update


ANY = pl.BlockSpec(memory_space=pl.ANY)
SMEM = pl.BlockSpec(memory_space=pltpu.SMEM)
WHOLE = pl.BlockSpec(memory_space=pltpu.VMEM)


def rows_of(width, height=TILE):
    return pl.BlockSpec((height, width), lambda i: (i, 0))


def fixed(shape):
    return pl.BlockSpec(shape, lambda i: (0,) * len(shape))


def params():
    return pltpu.CompilerParams(vmem_limit_bytes=VMEM_BYTES)


def cost(flops, bytes_accessed):
    return pl.CostEstimate(flops=int(flops), bytes_accessed=int(bytes_accessed), transcendentals=0)


def shape_of(*dims, dtype=BF16):
    return jax.ShapeDtypeStruct(dims, dtype)


def shampoo(gradient, left_stat, right_stat, left_root, right_root, master):
    rows, cols = gradient.shape
    left_new, right_new, new = pl.pallas_call(
        shampoo_kernel,
        out_shape=(
            shape_of(rows, rows, dtype=F32),
            shape_of(cols, cols, dtype=F32),
            shape_of(rows, cols, dtype=F32),
        ),
        in_specs=[WHOLE] * 6,
        out_specs=(WHOLE,) * 3,
        compiler_params=params(),
        cost_estimate=cost(4 * rows * cols * cols, 12 * cols * cols),
        name="shampoo",
    )(gradient, left_stat[0, 0], right_stat[0, 0], left_root[0, 0], right_root[0, 0], master)
    return left_new[None, None], right_new[None, None], new


def pack_attention(qkv, out):
    q, k, v = (qkv[:, i] for i in range(3))
    a, b = 2 * HD, 3 * HD
    return jnp.concatenate(
        [q[:, :a], k[:, :a], v[:, :a], q[:, a:b], v[:, a:b], k[:, a:b], out[:, a:b], out[:, :a]],
        axis=1,
    )


def unpack_attention(packed):
    c = [packed[:, i * HD : (i + 1) * HD] for i in range(12)]
    qkv = jnp.concatenate([c[0], c[1], c[6], c[2], c[3], c[8], c[4], c[5], c[7]], axis=1)
    return qkv, jnp.concatenate([c[10], c[11], c[9]], axis=1)


def per_device(
    block_in, seq_lengths, image_embed, w_qkv, w_out, w_up, w_down, norm_params, norm_second,
    qkv_left, qkv_right, qkv_left_root, qkv_right_root,
    out_left, out_right, out_left_root, out_right_root,
    up_left, up_right, up_left_root, up_right_root,
    down_left, down_right, down_left_root, down_right_root,
):
    micros, seqs, seq_len, width = block_in.shape
    dp_count, groups = lax.axis_size("dp"), lax.axis_size("mp")
    count = dp_count * groups
    dp_index = lax.axis_index("dp")
    me = dp_index * groups + lax.axis_index("mp")
    owned = w_up.shape[0]
    ff = w_up.shape[1]
    all_seqs = micros * seqs
    rows = all_seqs * seq_len
    tiles = rows // TILE
    seq_tile = TILE // seq_len
    direct = owned % 16 == 0

    table = source_table(count)
    order = jnp.asarray(table, jnp.int32)[me]
    inverse = jnp.asarray(np.argsort(table, axis=1), jnp.int32)[me]

    def gathered(block):
        own, other = gather_blocks(block, count)
        if direct:
            return own, other
        whole = jnp.concatenate([own, other], axis=0)[inverse]
        whole = whole.reshape(dp_count, groups, owned, block.shape[1])
        whole = whole.transpose(1, 0, 2, 3).reshape(groups, width, block.shape[1])
        return whole[: groups // 2], whole[groups // 2 :]

    kernel_order = order if direct else jnp.arange(groups, dtype=jnp.int32)
    kernel_inverse = inverse if direct else jnp.arange(groups, dtype=jnp.int32)
    block_rows = owned if direct else width
    block_half = (count if direct else groups) // 2

    def summed(keep, send):
        if not direct:
            whole = jnp.concatenate([keep, send], axis=0)
            whole = whole.reshape(groups, dp_count, owned, whole.shape[2])
            whole = whole.transpose(1, 0, 2, 3).reshape(count, owned, whole.shape[3])[order]
            keep, send = whole[: count // 2], whole[count // 2 :]
        return sum_blocks(keep, send, count)

    attention_w = gathered(pack_attention(w_qkv.astype(BF16), w_out.astype(BF16)))
    up_w = gathered(w_up.astype(BF16))
    down_w = gathered(w_down.astype(BF16))
    images = gather_blocks(image_embed.reshape(all_seqs, width), count)
    images = [part.reshape(-1, width) for part in images]

    x = block_in.reshape(rows, width)
    norms = norm_params.T
    lengths = seq_lengths.reshape(all_seqs)
    live = (jnp.arange(seq_len)[None, :] < lengths[:, None]).astype(F32).reshape(rows)
    live_cols = jnp.broadcast_to(live[:, None], (rows, LANES))
    live_keys = live.reshape(rows // LANES, 1, LANES)
    counts = jnp.broadcast_to(lengths.astype(F32)[:, None], (all_seqs, LANES))

    live_spec = rows_of(LANES)
    keys_spec = pl.BlockSpec((TILE // LANES, 1, LANES), lambda i: (i, 0, 0))
    norm_spec = fixed((4, width))

    def weight_scratch(cols):
        return [pltpu.VMEM((groups, width, cols), BF16), pltpu.SemaphoreType.DMA((groups,))]

    packed = 6 * LANES
    h1, proj, heads, lse, mid, h2 = pl.pallas_call(
        functools.partial(attention_forward, seq_len=seq_len),
        grid=(tiles,),
        in_specs=[SMEM, rows_of(width), keys_spec, norm_spec, ANY, ANY],
        out_specs=(
            rows_of(width), rows_of(groups * 5 * LANES), rows_of(groups * 2 * LANES),
            rows_of(LANES), rows_of(width), rows_of(width),
        ),
        out_shape=(
            shape_of(rows, width), shape_of(rows, groups * 5 * LANES),
            shape_of(rows, groups * 2 * LANES), shape_of(rows, LANES, dtype=F32),
            shape_of(rows, width, dtype=F32), shape_of(rows, width),
        ),
        scratch_shapes=weight_scratch(packed),
        compiler_params=params(),
        cost_estimate=cost(2 * rows * width * groups * 900, 12e6),
        name="attention_forward",
    )(kernel_order, x, live_keys, norms, *attention_w)

    hid, slope, pooled_hid = pl.pallas_call(
        functools.partial(up_forward, seq_len=seq_len),
        grid=(tiles,),
        in_specs=[SMEM, rows_of(width), live_spec, ANY, ANY],
        out_specs=(rows_of(groups * ff), rows_of(groups * ff), rows_of(groups * ff, seq_tile)),
        out_shape=(
            shape_of(rows, groups * ff), shape_of(rows, groups * ff), shape_of(all_seqs, groups * ff),
        ),
        scratch_shapes=weight_scratch(ff),
        compiler_params=params(),
        cost_estimate=cost(2 * rows * width * groups * ff, 20e6),
        name="up_forward",
    )(kernel_order, h2, live_cols, *up_w)

    block_out, pooled = pl.pallas_call(
        functools.partial(down_forward, seq_len=seq_len),
        grid=(tiles,),
        in_specs=[SMEM, rows_of(groups * ff), rows_of(width), live_spec, ANY, ANY],
        out_specs=(rows_of(width), rows_of(width, seq_tile)),
        out_shape=(shape_of(rows, width), shape_of(all_seqs, width, dtype=F32)),
        scratch_shapes=weight_scratch(ff),
        compiler_params=params(),
        cost_estimate=cost(2 * rows * width * groups * ff, 20e6),
        name="down_forward",
    )(kernel_order, hid, mid, live_cols, *down_w)

    loss, grad_seq, grad_low = pl.pallas_call(
        functools.partial(contrast, micros=micros),
        in_specs=[WHOLE] * 4,
        out_specs=(WHOLE,) * 3,
        out_shape=(
            shape_of(all_seqs, LANES, dtype=F32), shape_of(all_seqs, width, dtype=F32),
            shape_of(all_seqs, width),
        ),
        compiler_params=params(),
        cost_estimate=cost(4 * all_seqs * width * images[0].shape[0] * 2, 4e6),
        name="contrast",
    )(pooled, counts, *images)

    gradient_out = (shape_of(block_half, block_rows, packed),) * 2

    def gradient(left, right):
        depth = left.shape[0]
        return pl.pallas_call(
            functools.partial(weight_gradient, shared_cols=0),
            grid=(groups,),
            in_specs=[SMEM, fixed((depth, width)), pl.BlockSpec((depth, ff), lambda i: (0, i))],
            out_specs=(ANY, ANY),
            out_shape=gradient_out,
            scratch_shapes=[
                pltpu.VMEM((width, depth), BF16),
                pltpu.VMEM((2, width, ff), BF16),
                pltpu.SemaphoreType.DMA((2,)),
            ],
            compiler_params=params(),
            cost_estimate=cost(2 * depth * width * groups * ff, 12e6),
            name="weight_gradient",
        )(kernel_inverse, left, right)

    down_parts = gradient(grad_low, pooled_hid)
    grad_down = summed(*down_parts)

    dup, dmid, dmid_low, sums_two = pl.pallas_call(
        functools.partial(mlp_backward, seq_len=seq_len),
        grid=(tiles,),
        in_specs=[
            SMEM, rows_of(width, seq_tile), rows_of(width, seq_tile), rows_of(groups * ff),
            live_spec, rows_of(width), norm_spec, ANY, ANY, ANY, ANY,
        ],
        out_specs=(rows_of(groups * ff), rows_of(width), rows_of(width), fixed((8, width))),
        out_shape=(
            shape_of(rows, groups * ff), shape_of(rows, width, dtype=F32), shape_of(rows, width),
            shape_of(8, width, dtype=F32),
        ),
        scratch_shapes=[
            pltpu.VMEM((groups, width, ff), BF16), pltpu.VMEM((groups, width, ff), BF16),
            pltpu.SemaphoreType.DMA((groups,)), pltpu.SemaphoreType.DMA((groups,)),
        ],
        compiler_params=params(),
        cost_estimate=cost(2 * rows * width * groups * ff, 25e6),
        name="mlp_backward",
    )(kernel_order, grad_seq, grad_low, slope, live_cols, mid, norms, *up_w, *down_w)

    up_parts = gradient(h2, dup)
    grad_up = summed(*up_parts)

    dproj, input_grad, sums_one = pl.pallas_call(
        functools.partial(attention_backward, seq_len=seq_len),
        grid=(tiles,),
        in_specs=[
            SMEM, rows_of(width), keys_spec, norm_spec, rows_of(groups * 5 * LANES),
            rows_of(LANES), rows_of(width), rows_of(width), ANY, ANY,
        ],
        out_specs=(rows_of(groups * 5 * LANES), rows_of(width), fixed((8, width))),
        out_shape=(
            shape_of(rows, groups * 5 * LANES), shape_of(rows, width, dtype=F32),
            shape_of(8, width, dtype=F32),
        ),
        scratch_shapes=weight_scratch(packed),
        compiler_params=params(),
        cost_estimate=cost(2 * rows * width * groups * 1300, 20e6),
        name="attention_backward",
    )(kernel_order, x, live_keys, norms, proj, lse, dmid, dmid_low, *attention_w)

    attention_parts = pl.pallas_call(
        attention_gradient,
        grid=(groups,),
        in_specs=[
            SMEM, fixed((rows, width)), pl.BlockSpec((rows, 5 * LANES), lambda i: (0, i)),
            fixed((rows, width)), pl.BlockSpec((rows, 2 * LANES), lambda i: (0, i)),
        ],
        out_specs=(ANY, ANY),
        out_shape=gradient_out,
        scratch_shapes=[
            pltpu.VMEM((width, rows), BF16),
            pltpu.VMEM((width, rows), BF16),
            pltpu.VMEM((2, width, packed), BF16),
            pltpu.SemaphoreType.DMA((2,)),
        ],
        compiler_params=params(),
        cost_estimate=cost(2 * rows * width * groups * 900, 12e6),
        name="attention_gradient",
    )(kernel_inverse, h1, dproj, dmid_low, heads)
    grad_attention = summed(*attention_parts)

    norm_sum = jnp.concatenate([sums_one[:2], sums_two[:2]], axis=0)
    bit = 1
    while bit < count:
        norm_sum = norm_sum + swap(norm_sum, [i ^ bit for i in range(count)])
        bit *= 2
    grad_norm = lax.dynamic_slice_in_dim(norm_sum, dp_index * owned, owned, 1).T

    down_left_new, down_right_new, down_new = shampoo(
        grad_down, down_left, down_right, down_left_root, down_right_root, w_down
    )
    up_left_new, up_right_new, up_new = shampoo(
        grad_up, up_left, up_right, up_left_root, up_right_root, w_up
    )
    grad_qkv, grad_out = unpack_attention(grad_attention)
    qkv_left_new, qkv_right_new, qkv_new = shampoo(
        grad_qkv, qkv_left, qkv_right, qkv_left_root, qkv_right_root, w_qkv.reshape(owned, -1)
    )
    out_left_new, out_right_new, out_new = shampoo(
        grad_out, out_left, out_right, out_left_root, out_right_root, w_out
    )
    norm_second_new = STAT_DECAY * norm_second + (1.0 - STAT_DECAY) * grad_norm * grad_norm
    own_params = lax.dynamic_slice_in_dim(norm_params, dp_index * owned, owned, 0)
    norm_new = own_params - NORM_RATE * grad_norm / (jnp.sqrt(norm_second_new) + 1e-08)
    return (
        block_out.reshape(block_in.shape),
        input_grad.reshape(block_in.shape),
        loss[:, 0].reshape(micros, seqs),
        grad_qkv.reshape(w_qkv.shape), qkv_left_new, qkv_right_new, qkv_new.reshape(w_qkv.shape),
        grad_out, out_left_new, out_right_new, out_new,
        grad_up, up_left_new, up_right_new, up_new,
        grad_down, down_left_new, down_right_new, down_new,
        grad_norm, norm_second_new, norm_new,
    )


def solution(mesh):
    sequence = P(None, AXES)
    stat = P("dp", "mp", None, None)
    weight = P("dp", "mp")
    qkv = P("dp", None, "mp")
    norm = P("dp", None)
    in_specs = (sequence, sequence, sequence, qkv, weight, weight, weight, P(), norm) + (stat,) * 16
    out_specs = (
        (sequence, sequence, sequence)
        + (qkv, stat, stat, qkv)
        + (weight, stat, stat, weight) * 3
        + (norm, norm, norm)
    )
    return jax.shard_map(
        per_device, mesh=mesh, in_specs=in_specs, out_specs=out_specs, check_vma=False
    )
```

time: 1160 us -> 415 us (0.36)
  waiting for transfers between devices: 582 us -> 100 us
  matrix products: 224 us -> 0 us
  Pallas kernels: 0 us -> 190 us
  local copies, waits for them, and re-layouts: 143 us -> 32.4 us
  blocking collectives: 77.9 us -> 0 us
  other arithmetic: 105 us -> 27.7 us
  starting transfers between devices: 1.68 us -> 61.7 us
  between operations: 18.1 us -> 1.07 us
    psum x3 -> x0, waiting for transfers between devices: 309 us -> none  [the longest x1 120 us: per_device(): lax.psum(product(grad_up_rows, full_up, 1, 1).astype(jnp.bfloat16), 'mp')]
    dot_general x56 -> x0, matrix products: 224 us -> none  [the longest x28 157 us: product(): lax.dot_general(left_side, right_side, (((left_dim,), (right_dim,)), ((),...]
    pallas_call x0 -> x13, Pallas kernels: none -> 190 us  [the longest x1 47.9 us: per_device(): pl.pallas_call(functools.partial(attention_backward, seq_len=seq_len), gr...]
    reduce_scatter x6 -> x0, waiting for transfers between devices: 185 us -> none  [the longest x1 67.6 us: per_device(): lax.psum_scatter(grad_qkv, 'dp', scatter_dimension=0, tiled=True)]
    ppermute x0 -> x40, waiting for transfers between devices: none -> 100 us  [swap(): return lax.ppermute(values, AXES, list(enumerate(step)))]
    all_gather x2 -> x0, blocking collectives: 71.7 us -> none  [the longest x1 40.5 us: per_device(): lax.all_gather(w_qkv.astype(jnp.bfloat16), 'dp', axis=0, tiled=True)]
    reshape x9 -> x1, local copies, waits for them, and re-layouts: 66.4 us -> 1.81 us  [per_device(): w_qkv.reshape(owned, -1)]
    ppermute x0 -> x40, starting transfers between devices: none -> 61.7 us  [swap(): return lax.ppermute(values, AXES, list(enumerate(step)))]
  transfers between devices with their start and end apart: 17 -> 40, of which waited for: 12 -> 18; matrix products, arithmetic and copies ran while one was open for 17% -> 14% of each run, Pallas kernels for 0% -> 24%
where the time goes in v1:
time: 415 us; the launch traced here: 413 us
  Pallas kernels  190 us (46%)
  waiting for transfers between devices  100 us (24%)
  starting transfers between devices  61.7 us (15%)
  local copies, waits for them, and re-layouts  32.4 us (8%)
  other arithmetic  27.7 us (7%)
    ppermute x40, waiting for transfers between devices, swap(): return lax.ppermute(values, AXES, list(enumerate(step)))  100 us
    ppermute x40, starting transfers between devices, swap(): return lax.ppermute(values, AXES, list(enumerate(step)))  61.7 us
    pallas_call x1, Pallas kernels, per_device(): pl.pallas_call(functools.partial(attention_backward, seq_len=seq_len), gr...  47.9 us
    pallas_call x1, Pallas kernels, per_device(): pl.pallas_call(functools.partial(attention_forward, seq_len=seq_len), gri...  41.4 us
    pallas_call x1, Pallas kernels, per_device(): pl.pallas_call(functools.partial(mlp_backward, seq_len=seq_len), grid=(ti...  22.1 us
    pallas_call x1, Pallas kernels, per_device(): pl.pallas_call(functools.partial(up_forward, seq_len=seq_len), grid=(tile...  18.2 us
    unnamed x53, local copies, waits for them, and re-layouts  15.6 us
    pallas_call x4, Pallas kernels, shampoo(): pl.pallas_call(shampoo_kernel, out_shape=(shape_of(rows, rows, dtype=F32)...  15.1 us
  transfers between devices with their start and end apart: 40, of which 18 were waited for; matrix products, arithmetic and copies ran while one was open for 14% of the time, Pallas kernels for 24%

profile of v1, /device:TPU:0, one launch (start us, length us, event | category | flops | bytes accessed | tf_op | source)
XLA Modules:
  0.0 413.4 jit_solution(4710058280995728817)
XLA Ops:
  2.8 4.1 collective-permute-start
  6.9 7.0 %collective-permute-done = bf16[1,96,768]{2,1,0:T(8,128)(2,1)S(1)} collective-permute-done((bf16[1,96,768]{2,1,0:T(8,128)(2,1)S(1)}, bf16[1,96,768]{2,1,0:T(8,128)(2,1)S(1)}, u32[]{:S(2)}, u32[]{:S(2)}) %collective-permute-start) | collective-permute-done | bytes 147488 | tf_op jit(solution)/shard_map/ppermute | solution.py:47
  18.8 5.5 %collective-permute-done.5 = bf16[1,96,768]{2,1,0:T(8,128)(2,1)S(1)} collective-permute-done((bf16[1,96,768]{2,1,0:T(8,128)(2,1)S(1)}, bf16[1,96,768]{2,1,0:T(8,128)(2,1)S(1)}, u32[]{:S(2)}, u32[]{:S(2)}) %collective-permute-start.5) | collective-permute-done | bytes 147488 | tf_op jit(solution)/shard_map/ppermute | solution.py:47
  24.4 4.2 %collective-permute-start.6 = (bf16[2,96,768]{2,1,0:T(8,128)(2,1)S(1)}, bf16[2,96,768]{2,1,0:T(8,128)(2,1)S(1)}, u32[]{:S(2)}, u32[]{:S(2)}) collective-permute-start(bf16[2,96,768]{2,1,0:T(8,128)(2,1)S(1)} %pad_maximum_fusion.9), channel_id=1, source_target_pairs={{0,8},{1,9},{2,10},{3,11},{4,12},{5,13},{6,14},{7,15},{8,0},{9,1},... | collective-permute-start | bytes 884744 | tf_op jit(solution)/shard_map/ppermute | solution.py:47
  30.3 8.8 %collective-permute-done.10 = bf16[1,96,768]{2,1,0:T(8,128)(2,1)S(1)} collective-permute-done((bf16[1,96,768]{2,1,0:T(8,128)(2,1)S(1)}, bf16[1,96,768]{2,1,0:T(8,128)(2,1)S(1)}, u32[]{:S(2)}, u32[]{:S(2)}) %collective-permute-start.10) | collective-permute-done | bytes 147488 | tf_op jit(solution)/shard_map/ppermute | solution.py:47
  63.1 4.5 %collective-permute-done.12 = bf16[4,96,768]{2,1,0:T(8,128)(2,1)} collective-permute-done((bf16[4,96,768]{2,1,0:T(8,128)(2,1)}, bf16[4,96,768]{2,1,0:T(8,128)(2,1)}, u32[]{:S(2)}, u32[]{:S(2)}) %collective-permute-start.12) | collective-permute-done | bytes 589856 | tf_op jit(solution)/shard_map/ppermute | solution.py:47
  86.8 9.4 %collective-permute-done.13 = bf16[8,96,768]{2,1,0:T(8,128)(2,1)S(1)} collective-permute-done((bf16[8,96,768]{2,1,0:T(8,128)(2,1)S(1)}, bf16[8,96,768]{2,1,0:T(8,128)(2,1)S(1)}, u32[]{:S(2)}, u32[]{:S(2)}) %collective-permute-start.13) | collective-permute-done | bytes 1179680 | tf_op jit(solution)/shard_map/ppermute | solution.py:47
  106.5 6.8 %collective-permute-done.18 = bf16[8,64,768]{2,1,0:T(8,128)(2,1)S(1)} collective-permute-done((bf16[8,64,768]{2,1,0:T(8,128)(2,1)S(1)}, bf16[8,64,768]{2,1,0:T(8,128)(2,1)S(1)}, u32[]{:S(2)}, u32[]{:S(2)}) %collective-permute-start.18) | collective-permute-done | bytes 786464 | tf_op jit(solution)/shard_map/ppermute | solution.py:47
  116.8 41.4 %attention_forward.1 = (bf16[1024,768]{1,0:T(8,128)(2,1)}, bf16[1024,2560]{1,0:T(8,128)(2,1)}, bf16[1024,1024]{1,0:T(8,128)(2,1)}, f32[1024,128]{1,0:T(8,128)}, ...) custom-call(s32[32]{0:T(128)} %fusion.4.order, bf16[1024,768]{1,0:T(8,128)(2,1)} %bitcast.91, ...), custom_call_target="tpu_custom_call" | custom-call | flops 5662310400 | bytes 12000000 | tf_op jit(solution)/shard_map/attention_forward/pallas_call | solution.py:673
  159.2 18.2 %up_forward.1 = (bf16[1024,3072]{1,0:T(8,128)(2,1)}, bf16[1024,3072]{1,0:T(8,128)(2,1)}, bf16[64,3072]{1,0:T(8,128)(2,1)}) custom-call(s32[32]{0:T(128)} %fusion.4.order, bf16[1024,768]{1,0:T(8,128)(2,1)} %get-tuple-element.61.h2_ref.left_ref, f32[1024,128]{1,0:T(8,128)} %broadcast_in_dim.46.live_ref, ...), custom_call_target="tpu_custom_call" | custom-call | flops 4831838208 | bytes 20000000 | tf_op jit(solution)/shard_map/up_forward/pallas_call | solution.py:692
  177.4 13.9 %down_forward.1 = (bf16[1024,768]{1,0:T(8,128)(2,1)}, f32[64,768]{1,0:T(8,128)}) custom-call(s32[32]{0:T(128)} %fusion.4.order, bf16[1024,3072]{1,0:T(8,128)(2,1)} %get-tuple-element.62.hid_ref, f32[1024,768]{1,0:T(8,128)} %get-tuple-element.63.mid_ref, f32[1024,128]{1,0:T(8,128)} %broadcast_in_dim.46.live_ref, bf16[16,96,768]{2,1,0:T(8,128)(2,1)} %copy-done, ...), custom_call_target="tpu_custom_call" | custom-call | flops 4831838208 | bytes 20000000 | tf_op jit(solution)/shard_map/down_forward/pallas_call | solution.py:706
  192.0 5.0 %contrast.1 = (f32[64,128]{1,0:T(8,128)}, f32[64,768]{1,0:T(8,128)}, bf16[64,768]{1,0:T(8,128)(2,1)}) custom-call(f32[64,768]{1,0:T(8,128)} %get-tuple-element.67.pooled_ref, f32[64,128]{1,0:T(8,128)} %broadcast_in_dim.49.count_ref, bf16[1024,768]{1,0:T(8,128)(2,1)} %bitcast.11.own_ref, bf16[1024,768]{1,0:T(8,128)(2,1)} %bitcast.12.other_ref), custom_call_target="tpu_custom_call" | custom-call | flops 402653184 | bytes 4000000 | tf_op jit(solution)/shard_map/contrast/pallas_call | solution.py:718
  197.0 22.1 %mlp_backward.1 = (bf16[1024,3072]{1,0:T(8,128)(2,1)}, f32[1024,768]{1,0:T(8,128)}, bf16[1024,768]{1,0:T(8,128)(2,1)}, f32[8,768]{1,0:T(8,128)}) custom-call(s32[32]{0:T(128)} %fusion.4.order, f32[64,768]{1,0:T(8,128)} %get-tuple-element.68.grad_ref, bf16[64,768]{1,0:T(8,128)(2,1)} %get-tuple-element.69.low_ref.left_ref, ...), custom_call_target="tpu_custom_call" | custom-call | flops 4831838208 | bytes 25000000 | tf_op jit(solution)/shard_map/mlp_backward/pallas_call | solution.py:754
  219.1 47.9 %attention_backward.1 = (bf16[1024,2560]{1,0:T(8,128)(2,1)}, f32[1024,768]{1,0:T(8,128)}, f32[8,768]{1,0:T(8,128)}) custom-call(s32[32]{0:T(128)} %fusion.4.order, bf16[1024,768]{1,0:T(8,128)(2,1)} %bitcast.92, f32[8,1,128]{2,1,0:T(1,128)} %compare_convert_fusion.live_ref, f32[4,768]{1,0:T(4,128)} %bitcast.88, ...), custom_call_target="tpu_custom_call" | custom-call | flops 8178892800 | bytes 20000000 | tf_op jit(solution)/shard_map/attention_backward/pallas_call | solution.py:778
  267.0 12.0 %attention_gradient.1 = (bf16[16,96,768]{2,1,0:T(8,128)(2,1)}, bf16[16,96,768]{2,1,0:T(8,128)(2,1)}) custom-call(s32[32]{0:T(128)} %fusion.5.inverse, bf16[1024,768]{1,0:T(8,128)(2,1)} %get-tuple-element.75.h1_ref, bf16[1024,2560]{1,0:T(8,128)(2,1)} %get-tuple-element.76.proj_ref, bf16[1024,768]{1,0:T(8,128)(2,1)} %get-tuple-element.72.dmid_low_ref.mid_ref, ...), custom_call_target="tpu_custom_call" | custom-call | flops 5662310400 | bytes 12000000 | tf_op jit(solution)/shard_map/attention_gradient/pallas_call | solution.py:796
  279.9 9.8 %weight_gradient.2 = (bf16[16,96,768]{2,1,0:T(8,128)(2,1)}, bf16[16,96,768]{2,1,0:T(8,128)(2,1)}) custom-call(s32[32]{0:T(128)} %fusion.5.inverse, bf16[1024,768]{1,0:T(8,128)(2,1)} %get-tuple-element.61.h2_ref.left_ref, bf16[1024,3072]{1,0:T(8,128)(2,1)} %get-tuple-element.86.right_ref), custom_call_target="tpu_custom_call" | custom-call | flops 4831838208 | bytes 12000000 | tf_op jit(solution)/shard_map/weight_gradient/pallas_call | solution.py:735
  290.0 4.7 %weight_gradient.3 = (bf16[16,96,768]{2,1,0:T(8,128)(2,1)}, bf16[16,96,768]{2,1,0:T(8,128)(2,1)}) custom-call(s32[32]{0:T(128)} %fusion.5.inverse, bf16[64,768]{1,0:T(8,128)(2,1)} %get-tuple-element.69.low_ref.left_ref, bf16[64,3072]{1,0:T(8,128)(2,1)} %get-tuple-element.92.right_ref), custom_call_target="tpu_custom_call" | custom-call | flops 301989888 | bytes 12000000 | tf_op jit(solution)/shard_map/weight_gradient/pallas_call | solution.py:735
  296.7 5.1 %collective-permute-start.21 = (bf16[8,96,768]{2,1,0:T(8,128)(2,1)}, bf16[8,96,768]{2,1,0:T(8,128)(2,1)}, u32[]{:S(2)}, u32[]{:S(2)}) collective-permute-start(bf16[8,96,768]{2,1,0:T(8,128)(2,1)} %get-tuple-element.156), channel_id=1, source_target_pairs={{0,2},{1,5},{2,0},{3,7},{4,6},{5,1},{6,4},{7,3},{8,10},{9,13},{10,... | collective-permute-start | bytes 3538952 | tf_op jit(solution)/shard_map/ppermute | solution.py:47
  310.6 31.1 %collective-permute-done.36 = f32[4,768]{1,0:T(4,128)S(1)} collective-permute-done((f32[4,768]{1,0:T(4,128)S(1)}, f32[4,768]{1,0:T(4,128)S(1)}, u32[]{:S(2)}, u32[]{:S(2)}) %collective-permute-start.36) | collective-permute-done | bytes 12320 | tf_op jit(solution)/shard_map/ppermute | solution.py:47
  367.2 4.4 %collective-permute-done.27 = bf16[4,96,768]{2,1,0:T(8,128)(2,1)S(1)} collective-permute-done((bf16[4,96,768]{2,1,0:T(8,128)(2,1)S(1)}, bf16[4,96,768]{2,1,0:T(8,128)(2,1)S(1)}, u32[]{:S(2)}, u32[]{:S(2)}) %collective-permute-start.27) | collective-permute-done | bytes 589856 | tf_op jit(solution)/shard_map/ppermute | solution.py:47
  373.5 4.4 %collective-permute-done.32 = bf16[4,96,768]{2,1,0:T(8,128)(2,1)S(1)} collective-permute-done((bf16[4,96,768]{2,1,0:T(8,128)(2,1)S(1)}, bf16[4,96,768]{2,1,0:T(8,128)(2,1)S(1)}, u32[]{:S(2)}, u32[]{:S(2)}) %collective-permute-start.32) | collective-permute-done | bytes 589856 | tf_op jit(solution)/shard_map/ppermute | solution.py:47
  384.2 4.0 collective-permute-done.33
  403.3 4.7 %shampoo.6 = (f32[96,96]{1,0:T(8,128)}, f32[768,768]{1,0:T(8,128)}, f32[96,768]{1,0:T(8,128)}) custom-call(f32[96,768]{1,0:T(8,128)} %add_bitcast_fusion.1.grad_ref, f32[96,96]{1,0:T(8,128)} %bitcast.80, f32[768,768]{1,0:T(8,128)} %bitcast.67, f32[96,96]{1,0:T(8,128)} %bitcast.81, f32[768,768]{1,0:T(8,128)} %bitcast.68, f32[96,768]{1,0:T(8,128)} %master_ref.4), custom_call_target="tpu_custom_call" | custom-call | flops 226492416 | bytes 7077888 | tf_op jit(solution)/shard_map/shampoo/pallas_call | solution.py:574
  408.7 4.7 %shampoo.7 = (f32[96,96]{1,0:T(8,128)}, f32[768,768]{1,0:T(8,128)}, f32[96,768]{1,0:T(8,128)}) custom-call(f32[96,768]{1,0:T(8,128)} %add_bitcast_fusion.grad_ref, f32[96,96]{1,0:T(8,128)} %bitcast.82, f32[768,768]{1,0:T(8,128)} %bitcast.69, f32[96,96]{1,0:T(8,128)} %bitcast.83, f32[768,768]{1,0:T(8,128)} %bitcast.70, f32[96,768]{1,0:T(8,128)} %master_ref.5), custom_call_target="tpu_custom_call" | custom-call | flops 226492416 | bytes 7077888 | tf_op jit(solution)/shard_map/shampoo/pallas_call | solution.py:574
  (198 shorter events, 128.7 us)
Async XLA Ops:
  14.0 14.6 %collective-permute-start.1 = (bf16[2,96,768]{2,1,0:T(8,128)(2,1)S(1)}, bf16[2,96,768]{2,1,0:T(8,128)(2,1)S(1)}, u32[]{:S(2)}, u32[]{:S(2)}) collective-permute-start(bf16[2,96,768]{2,1,0:T(8,128)(2,1)S(1)} %pad_maximum_fusion.8), channel_id=1, source_target_pairs={{0,8},{1,9},{2,10},{3,11},{4,12},{5,13},{6,14},{7,15},{8,0},{9,1},... | collective-permute-start | bytes 884744 | tf_op jit(solution)/shard_map/ppermute | solution.py:47
  24.4 14.9 %collective-permute-start.6 = (bf16[2,96,768]{2,1,0:T(8,128)(2,1)S(1)}, bf16[2,96,768]{2,1,0:T(8,128)(2,1)S(1)}, u32[]{:S(2)}, u32[]{:S(2)}) collective-permute-start(bf16[2,96,768]{2,1,0:T(8,128)(2,1)S(1)} %pad_maximum_fusion.9), channel_id=1, source_target_pairs={{0,8},{1,9},{2,10},{3,11},{4,12},{5,13},{6,14},{7,15},{8,0},{9,1},... | collective-permute-start | bytes 884744 | tf_op jit(solution)/shard_map/ppermute | solution.py:47
  28.7 15.2 %collective-permute-start.2 = (bf16[4,96,768]{2,1,0:T(8,128)(2,1)S(1)}, bf16[4,96,768]{2,1,0:T(8,128)(2,1)S(1)}, u32[]{:S(2)}, u32[]{:S(2)}) collective-permute-start(bf16[4,96,768]{2,1,0:T(8,128)(2,1)S(1)} %pad_maximum_fusion.4), channel_id=1, source_target_pairs={{0,4},{1,3},{2,6},{3,1},{4,0},{5,7},{6,2},{7,5},{8,12},{9,11},{10,... | collective-permute-start | bytes 1769480 | tf_op jit(solution)/shard_map/ppermute | solution.py:47
  40.2 14.8 %collective-permute-start.7 = (bf16[4,96,768]{2,1,0:T(8,128)(2,1)}, bf16[4,96,768]{2,1,0:T(8,128)(2,1)}, u32[]{:S(2)}, u32[]{:S(2)}) collective-permute-start(bf16[4,96,768]{2,1,0:T(8,128)(2,1)} %pad_maximum_fusion.5), channel_id=1, source_target_pairs={{0,4},{1,3},{2,6},{3,1},{4,0},{5,7},{6,2},{7,5},{8,12},{9,11},{10,... | collective-permute-start | bytes 1769480 | tf_op jit(solution)/shard_map/ppermute | solution.py:47
  41.7 17.3 %collective-permute-start.15 = (bf16[1,64,768]{2,1,0:T(8,128)(2,1)}, bf16[1,64,768]{2,1,0:T(8,128)(2,1)}, u32[]{:S(2)}, u32[]{:S(2)}) collective-permute-start(bf16[1,64,768]{2,1,0:T(8,128)(2,1)} %bitcast.10), channel_id=1, source_target_pairs={{0,16},{1,17},{2,18},{3,19},{4,20},{5,21},{6,22},{7,23},{8,24},{9,... | collective-permute-start | bytes 294920 | tf_op jit(solution)/shard_map/ppermute | solution.py:47
  45.1 28.0 %collective-permute-start.3 = (bf16[8,96,768]{2,1,0:T(8,128)(2,1)}, bf16[8,96,768]{2,1,0:T(8,128)(2,1)}, u32[]{:S(2)}, u32[]{:S(2)}) collective-permute-start(bf16[8,96,768]{2,1,0:T(8,128)(2,1)} %pad_maximum_fusion), channel_id=1, source_target_pairs={{0,2},{1,5},{2,0},{3,7},{4,6},{5,1},{6,4},{7,3},{8,10},{9,13},{10,... | collective-permute-start | bytes 3538952 | tf_op jit(solution)/shard_map/ppermute | solution.py:47
  48.9 18.7 %collective-permute-start.12 = (bf16[4,96,768]{2,1,0:T(8,128)(2,1)}, bf16[4,96,768]{2,1,0:T(8,128)(2,1)}, u32[]{:S(2)}, u32[]{:S(2)}) collective-permute-start(bf16[4,96,768]{2,1,0:T(8,128)(2,1)} %pad_maximum_fusion.6), channel_id=1, source_target_pairs={{0,4},{1,3},{2,6},{3,1},{4,0},{5,7},{6,2},{7,5},{8,12},{9,11},{10,... | collective-permute-start | bytes 1769480 | tf_op jit(solution)/shard_map/ppermute | solution.py:47
  56.3 23.0 %collective-permute-start.8 = (bf16[8,96,768]{2,1,0:T(8,128)(2,1)S(1)}, bf16[8,96,768]{2,1,0:T(8,128)(2,1)S(1)}, u32[]{:S(2)}, u32[]{:S(2)}) collective-permute-start(bf16[8,96,768]{2,1,0:T(8,128)(2,1)S(1)} %pad_maximum_fusion.1), channel_id=1, source_target_pairs={{0,2},{1,5},{2,0},{3,7},{4,6},{5,1},{6,4},{7,3},{8,10},{9,13},{10,... | collective-permute-start | bytes 3538952 | tf_op jit(solution)/shard_map/ppermute | solution.py:47
  60.0 23.1 %collective-permute-start.16 = (bf16[2,64,768]{2,1,0:T(8,128)(2,1)S(1)}, bf16[2,64,768]{2,1,0:T(8,128)(2,1)S(1)}, u32[]{:S(2)}, u32[]{:S(2)}) collective-permute-start(bf16[2,64,768]{2,1,0:T(8,128)(2,1)S(1)} %pad_maximum_fusion.11), channel_id=1, source_target_pairs={{0,8},{1,9},{2,10},{3,11},{4,12},{5,13},{6,14},{7,15},{8,0},{9,1},... | collective-permute-start | bytes 589832 | tf_op jit(solution)/shard_map/ppermute | solution.py:47
  68.8 27.3 %collective-permute-start.13 = (bf16[8,96,768]{2,1,0:T(8,128)(2,1)S(1)}, bf16[8,96,768]{2,1,0:T(8,128)(2,1)S(1)}, u32[]{:S(2)}, u32[]{:S(2)}) collective-permute-start(bf16[8,96,768]{2,1,0:T(8,128)(2,1)S(1)} %pad_maximum_fusion.2), channel_id=1, source_target_pairs={{0,2},{1,5},{2,0},{3,7},{4,6},{5,1},{6,4},{7,3},{8,10},{9,13},{10,... | collective-permute-start | bytes 3538952 | tf_op jit(solution)/shard_map/ppermute | solution.py:47
  75.5 41.3 %collective-permute-start.4 = (bf16[16,96,768]{2,1,0:T(8,128)(2,1)}, bf16[16,96,768]{2,1,0:T(8,128)(2,1)}, u32[]{:S(2)}, u32[]{:S(2)}) collective-permute-start(bf16[16,96,768]{2,1,0:T(8,128)(2,1)} %constant_dynamic-update-slice_fusion.own_ref), channel_id=1, source_target_pairs={{0,1},{1,0},{2,3},{3,2},{4,5},{5,4},{6,7},{7,6},{8,9},{9,8},{10,11... | collective-permute-start | bytes 7077896 | tf_op jit(solution)/shard_map/ppermute | solution.py:47
  80.4 77.8 %collective-permute-start.9 = (bf16[16,96,768]{2,1,0:T(8,128)(2,1)}, bf16[16,96,768]{2,1,0:T(8,128)(2,1)}, u32[]{:S(2)}, u32[]{:S(2)}) collective-permute-start(bf16[16,96,768]{2,1,0:T(8,128)(2,1)} %constant_dynamic-update-slice_fusion.5.own_ref.up_own), channel_id=1, source_target_pairs={{0,1},{1,0},{2,3},{3,2},{4,5},{5,4},{6,7},{7,6},{8,9},{9,8},{10,11... | collective-permute-start | bytes 7077896 | tf_op jit(solution)/shard_map/ppermute | solution.py:47
  84.1 16.2 %collective-permute-start.17 = (bf16[4,64,768]{2,1,0:T(8,128)(2,1)S(1)}, bf16[4,64,768]{2,1,0:T(8,128)(2,1)S(1)}, u32[]{:S(2)}, u32[]{:S(2)}) collective-permute-start(bf16[4,64,768]{2,1,0:T(8,128)(2,1)S(1)} %pad_maximum_fusion.7), channel_id=1, source_target_pairs={{0,4},{1,3},{2,6},{3,1},{4,0},{5,7},{6,2},{7,5},{8,12},{9,11},{10,... | collective-permute-start | bytes 1179656 | tf_op jit(solution)/shard_map/ppermute | solution.py:47
  96.2 81.2 %collective-permute-start.14 = (bf16[16,96,768]{2,1,0:T(8,128)(2,1)S(1)}, bf16[16,96,768]{2,1,0:T(8,128)(2,1)}, u32[]{:S(2)}, u32[]{:S(2)}) collective-permute-start(bf16[16,96,768]{2,1,0:T(8,128)(2,1)S(1)} %constant_dynamic-update-slice_fusion.10.own_ref.down_own), channel_id=1, source_target_pairs={{0,1},{1,0},{2,3},{3,2},{4,5},{5,4},{6,7},{7,6},{8,9},{9,8},{10,11... | collective-permute-start | bytes 7077896 | tf_op jit(solution)/shard_map/ppermute | solution.py:47
  114.3 77.1 %collective-permute-start.19 = (bf16[16,64,768]{2,1,0:T(8,128)(2,1)}, bf16[16,64,768]{2,1,0:T(8,128)(2,1)}, u32[]{:S(2)}, u32[]{:S(2)}) collective-permute-start(bf16[16,64,768]{2,1,0:T(8,128)(2,1)} %constant_dynamic-update-slice_fusion.15), channel_id=1, source_target_pairs={{0,1},{1,0},{2,3},{3,2},{4,5},{5,4},{6,7},{7,6},{8,9},{9,8},{10,11... | collective-permute-start | bytes 4718600 | tf_op jit(solution)/shard_map/ppermute | solution.py:47
  279.1 15.9 %collective-permute-start.20 = (bf16[16,96,768]{2,1,0:T(8,128)(2,1)}, bf16[16,96,768]{2,1,0:T(8,128)(2,1)S(1)}, u32[]{:S(2)}, u32[]{:S(2)}) collective-permute-start(bf16[16,96,768]{2,1,0:T(8,128)(2,1)} %get-tuple-element.79), channel_id=1, source_target_pairs={{0,1},{1,0},{2,3},{3,2},{4,5},{5,4},{6,7},{7,6},{8,9},{9,8},{10,11... | collective-permute-start | bytes 7077896 | tf_op jit(solution)/shard_map/ppermute | solution.py:47
  296.7 57.1 %collective-permute-start.21 = (bf16[8,96,768]{2,1,0:T(8,128)(2,1)}, bf16[8,96,768]{2,1,0:T(8,128)(2,1)}, u32[]{:S(2)}, u32[]{:S(2)}) collective-permute-start(bf16[8,96,768]{2,1,0:T(8,128)(2,1)} %get-tuple-element.156), channel_id=1, source_target_pairs={{0,2},{1,5},{2,0},{3,7},{4,6},{5,1},{6,4},{7,3},{8,10},{9,13},{10,... | collective-permute-start | bytes 3538952 | tf_op jit(solution)/shard_map/ppermute | solution.py:47
  303.5 52.4 %collective-permute-start.26 = (bf16[8,96,768]{2,1,0:T(8,128)(2,1)}, bf16[8,96,768]{2,1,0:T(8,128)(2,1)}, u32[]{:S(2)}, u32[]{:S(2)}) collective-permute-start(bf16[8,96,768]{2,1,0:T(8,128)(2,1)} %get-tuple-element.154), channel_id=1, source_target_pairs={{0,2},{1,5},{2,0},{3,7},{4,6},{5,1},{6,4},{7,3},{8,10},{9,13},{10,... | collective-permute-start | bytes 3538952 | tf_op jit(solution)/shard_map/ppermute | solution.py:47
  305.2 53.8 %collective-permute-start.31 = (bf16[8,96,768]{2,1,0:T(8,128)(2,1)}, bf16[8,96,768]{2,1,0:T(8,128)(2,1)}, u32[]{:S(2)}, u32[]{:S(2)}) collective-permute-start(bf16[8,96,768]{2,1,0:T(8,128)(2,1)} %get-tuple-element.152), channel_id=1, source_target_pairs={{0,2},{1,5},{2,0},{3,7},{4,6},{5,1},{6,4},{7,3},{8,10},{9,13},{10,... | collective-permute-start | bytes 3538952 | tf_op jit(solution)/shard_map/ppermute | solution.py:47
  310.0 31.7 %collective-permute-start.36 = (f32[4,768]{1,0:T(4,128)S(1)}, f32[4,768]{1,0:T(4,128)S(1)}, u32[]{:S(2)}, u32[]{:S(2)}) collective-permute-start(f32[4,768]{1,0:T(4,128)S(1)} %fusion.6), channel_id=1, source_target_pairs={{0,2},{1,3},{2,0},{3,1},{4,6},{5,7},{6,4},{7,5},{8,10},{9,11},{10,... | collective-permute-start | bytes 36872 | tf_op jit(solution)/shard_map/ppermute | solution.py:47
  360.5 17.4 %collective-permute-start.32 = (bf16[4,96,768]{2,1,0:T(8,128)(2,1)S(1)}, bf16[4,96,768]{2,1,0:T(8,128)(2,1)S(1)}, u32[]{:S(2)}, u32[]{:S(2)}) collective-permute-start(bf16[4,96,768]{2,1,0:T(8,128)(2,1)S(1)} %get-tuple-element.158), channel_id=1, source_target_pairs={{0,4},{1,3},{2,6},{3,1},{4,0},{5,7},{6,2},{7,5},{8,12},{9,11},{10,... | collective-permute-start | bytes 1769480 | tf_op jit(solution)/shard_map/ppermute | solution.py:47
  365.4 14.4 %collective-permute-start.23 = (bf16[2,96,768]{2,1,0:T(8,128)(2,1)S(1)}, bf16[2,96,768]{2,1,0:T(8,128)(2,1)S(1)}, u32[]{:S(2)}, u32[]{:S(2)}) collective-permute-start(bf16[2,96,768]{2,1,0:T(8,128)(2,1)S(1)} %get-tuple-element.168), channel_id=1, source_target_pairs={{0,8},{1,9},{2,10},{3,11},{4,12},{5,13},{6,14},{7,15},{8,0},{9,1},... | collective-permute-start | bytes 884744 | tf_op jit(solution)/shard_map/ppermute | solution.py:47
  382.9 19.6 %collective-permute-start.29 = (bf16[1,96,768]{2,1,0:T(8,128)(2,1)S(1)}, bf16[1,96,768]{2,1,0:T(8,128)(2,1)S(1)}, u32[]{:S(2)}, u32[]{:S(2)}) collective-permute-start(bf16[1,96,768]{2,1,0:T(8,128)(2,1)S(1)} %add_convert_fusion.20), channel_id=1, source_target_pairs={{0,16},{1,17},{2,18},{3,19},{4,20},{5,21},{6,22},{7,23},{8,24},{9,... | collective-permute-start | bytes 442376 | tf_op jit(solution)/shard_map/ppermute | solution.py:47
  388.2 19.7 %collective-permute-start.34 = (bf16[1,96,768]{2,1,0:T(8,128)(2,1)S(1)}, bf16[1,96,768]{2,1,0:T(8,128)(2,1)S(1)}, u32[]{:S(2)}, u32[]{:S(2)}) collective-permute-start(bf16[1,96,768]{2,1,0:T(8,128)(2,1)S(1)} %add_convert_fusion.18), channel_id=1, source_target_pairs={{0,16},{1,17},{2,18},{3,19},{4,20},{5,21},{6,22},{7,23},{8,24},{9,... | collective-permute-start | bytes 442376 | tf_op jit(solution)/shard_map/ppermute | solution.py:47
  (34 other events, 358.7 us)

commit v2 on v1

v2 whole, which is shorter than its diff:
```python
import functools
import math

import jax
import jax.numpy as jnp
import numpy as np
from jax import lax
from jax.experimental import pallas as pl
from jax.experimental.pallas import tpu as pltpu
from jax.sharding import PartitionSpec as P

AXES = ("dp", "mp")
HD = 64
LANES = 128
EPSILON = 1e-06
SOFTMAX_TEMP = 2.0
LOSS_SCALE = 32.0
STAT_DECAY = 0.5
SHAMPOO_RATE = 0.3
NORM_RATE = 0.5
TILE = 256
VMEM_BYTES = 56 * 1024 * 1024
F32 = jnp.float32
BF16 = jnp.bfloat16


def far_digits(count):
    digits = []
    weight = 8
    while weight < count:
        size = min(4, count // weight)
        digits.append((weight, size))
        weight *= size
    return digits


def near_steps(count):
    return (
        [i ^ (4 if i % 2 == 0 else 2) for i in range(count)],
        [i ^ (2 if i % 2 == 0 else 4) for i in range(count)],
        [i ^ 1 for i in range(count)],
    )


def far_steps(count, weight, size):
    return [[i ^ (weight * m) for i in range(count)] for m in range(1, size)]


def source_table(count, near_first):
    first, second, third = near_steps(count)
    far = [far_steps(count, weight, size) for weight, size in far_digits(count)]
    rounds = [[first]] + far if near_first else far + [[first]]
    table = np.arange(count)[:, None]
    for steps in rounds + [[second], [third]]:
        table = np.concatenate([table] + [table[np.array(step)] for step in steps], axis=1)
    return table


def swap(values, step):
    return lax.ppermute(values, AXES, list(enumerate(step)))


class Gather:
    def __init__(self, block, count):
        self.count = count
        self.near = near_steps(count)
        self.held = block[None]
        self.received = []

    def keep(self, *earlier):
        if self.received:
            self.received = after(self.received, *earlier)
            self.held = jnp.concatenate([self.held] + self.received, axis=0)
            self.received = []

    def far(self, *earlier):
        (self.held,) = after([self.held], *earlier)
        for weight, size in far_digits(self.count):
            self.keep()
            steps = far_steps(self.count, weight, size)
            self.received = [swap(self.held, step) for step in steps]

    def first(self, *earlier):
        (self.held,) = after([self.held], *earlier)
        self.received = [swap(self.held, self.near[0])]

    def second(self, *earlier):
        (self.held,) = after([self.held], *earlier)
        self.across = swap(self.held, self.near[1])

    def third(self, *earlier):
        (self.held,) = after([self.held], *earlier)
        self.held_other = swap(self.held, self.near[2])

    def last(self, *earlier):
        (self.across,) = after([self.across], *earlier)
        self.across_other = swap(self.across, self.near[2])

    def quarters(self):
        return self.held, self.across, self.held_other, self.across_other


def join(*values):
    return lax.optimization_barrier(values)


def after(values, *earlier, keep=None):
    if not earlier:
        return list(values)
    return list(lax.optimization_barrier((*values, *earlier)))[: keep or len(values)]


def add_low(*terms):
    return sum(term.astype(F32) for term in terms).astype(BF16)


class Sum:
    def __init__(self, quarters, count):
        self.count = count
        self.near = near_steps(count)
        self.held, self.across, held_other, across_other = quarters
        self.from_across = swap(across_other, self.near[2])
        self.from_held = swap(held_other, self.near[2])

    def second(self, *earlier):
        (received,) = after([self.from_across], *earlier)
        self.going = add_low(self.across, received)
        self.received = swap(self.going, self.near[1])

    def first(self, *earlier):
        (received,) = after([self.received], *earlier)
        half = self.held.shape[0] // 2
        terms = self.held, self.from_held, received
        self.going = add_low(*(term[half:] for term in terms))
        self.keep = add_low(*(term[:half] for term in terms))
        self.received = swap(self.going, self.near[0])

    def far(self, *earlier):
        (received,) = after([self.received], *earlier)
        keep = [self.keep, received]
        for weight, size in far_digits(self.count)[::-1]:
            step_size = keep[0].shape[0] // size
            parts = [
                add_low(*(term[m * step_size : (m + 1) * step_size] for term in keep))
                for m in range(1, size)
            ]
            keep = [term[:step_size] if step_size > 1 else term for term in keep] + [
                swap(part, step)
                for part, step in zip(parts, far_steps(self.count, weight, size))
            ]
        self.going = parts[-1]
        self.keep = keep


def dot(left, right, left_dim, right_dim):
    return lax.dot_general(
        left, right, (((left_dim,), (right_dim,)), ((), ())), preferred_element_type=F32
    )


def load_weights(order, parts, weights, sems):
    size, rows, _ = parts[0].shape
    groups = weights.shape[0]

    def body(q, carry):
        for i, part in enumerate(parts):
            index = order[i * size + q]
            group = index % groups
            place = pl.multiple_of((index // groups) * rows, 16)
            pltpu.make_async_copy(
                part.at[q], weights.at[group, pl.ds(place, rows), :], sems.at[group]
            ).start()
        return carry

    lax.fori_loop(0, size, body, 0)


def store_blocks(inverse, source, group, groups, parts, sem):
    size, rows, _ = parts[0].shape

    def body(p, carry):
        position = inverse[p * groups + group]
        block = source.at[pl.ds(pl.multiple_of(p * rows, 16), rows), :]
        for i, part in enumerate(parts):

            @pl.when(jnp.logical_and(position >= i * size, position < (i + 1) * size))
            def _():
                pltpu.make_async_copy(block, part.at[position - i * size], sem).start()

        return carry

    lax.fori_loop(0, source.shape[0] // rows, body, 0)


def wait_weights(weights, sems, group):
    pltpu.make_async_copy(weights.at[group], weights.at[group], sems.at[group]).wait()


def normalize(values):
    center = values - jnp.mean(values, axis=-1, keepdims=True)
    spread = jnp.mean(center * center, axis=-1, keepdims=True)
    scale = lax.rsqrt(spread + EPSILON)
    return center * scale, scale


def low_lanes(dtype=BF16):
    lane = lax.broadcasted_iota(jnp.int32, (1, LANES), 1)
    return jnp.where(lane < HD, 1.0, 0.0).astype(dtype)


def pairs_of(blocks, low):
    first, second = blocks

    def join(left, right, high_half):
        if high_half:
            return jnp.where(low, turn(left), right)
        return jnp.where(low, left, turn(right))

    return (
        (first[0], first[1], first[2]),
        (second[0], second[1], second[2]),
        (
            join(first[3], second[3], False),
            join(first[4], second[4], False),
            join(first[3], second[3], True),
        ),
    )


def turn(values):
    return jnp.concatenate([values[:, HD:], values[:, :HD]], axis=1)


def both_heads(values, low_mask, high_mask):
    return jnp.concatenate([values * low_mask, values * high_mask], axis=0)


def diagonal(full, seq_len, own_cols):
    picked = full[:seq_len]
    for i, own in enumerate(own_cols):
        if i:
            picked = jnp.where(own, full[i * seq_len : (i + 1) * seq_len], picked)
    return picked


def undiagonal(compact, own_cols):
    return jnp.concatenate(
        [jnp.where(own, compact, jnp.zeros_like(compact)) for own in own_cols], axis=0
    )


def sequence_columns(seq_len):
    lane = lax.broadcasted_iota(jnp.int32, (seq_len, 2 * LANES), 1) % LANES
    return [lane // seq_len == i for i in range(LANES // seq_len)]


def stack_heads(values):
    return jnp.concatenate([values[:, :LANES], values[:, LANES:]], axis=0)


def first_norm(x_ref, norm_ref, h1_ref):
    n1, _ = normalize(x_ref[...].astype(F32))
    h1_ref[...] = (n1 * norm_ref[0:1, :] + norm_ref[1:2, :]).astype(BF16)


def attention_forward(
    order, x_ref, h1_ref, live_ref, norm_ref, w0, w1, w2, w3,
    proj_ref, heads_ref, lse_ref, mid_ref, h2_ref,
    weights, sems, *, seq_len,
):
    groups = weights.shape[0]
    first = pl.program_id(0) == 0

    @pl.when(first)
    def _():
        load_weights(order, (w0, w1, w2, w3), weights, sems)
        for group in range(weights.shape[0]):
            wait_weights(weights, sems, group)

    x = x_ref[...].astype(F32)
    rows = x.shape[0]
    h1 = h1_ref[...]
    low_mask = low_lanes()
    high_mask = 1 - low_mask
    low = lax.broadcasted_iota(jnp.int32, (1, LANES), 1) < HD
    own_cols = sequence_columns(seq_len)
    count = rows // LANES
    duos = groups // 2
    projected = [
        dot(h1, weights[group, :, : 5 * LANES], 1, 0).astype(BF16) for group in range(groups)
    ]
    chains = []
    for duo in range(duos):
        for t in range(count):
            span = slice(t * LANES, (t + 1) * LANES)
            blocks = [
                [proj[span, i * LANES : (i + 1) * LANES] for i in range(5)]
                for proj in projected[2 * duo : 2 * duo + 2]
            ]
            for i, (q, k, v) in enumerate(pairs_of(blocks, low)):
                for which, part in enumerate((q, k, v)):
                    at = ((duo * 3 + i) * 3 + which) * LANES
                    proj_ref[span, at : at + LANES] = part
                chains.append((t, duo * 3 + i, q, k, v))
    scores = [dot(k, both_heads(q, low_mask, high_mask), 1, 1) for t, i, q, k, v in chains]
    probs = []
    for (t, i, *_), full in zip(chains, scores):
        compact = diagonal(full, seq_len, own_cols) * (HD**-0.5)
        compact = jnp.where(live_ref[t] > 0.0, compact, -1e30)
        top = jnp.max(compact, axis=0, keepdims=True)
        powers = jnp.exp(compact - top)
        power = jnp.sum(powers, axis=0, keepdims=True)
        lse_ref[t, i : i + 1, :] = top + jnp.log(power)
        probs.append(undiagonal((powers * (1.0 / power)).astype(BF16), own_cols))
    outs = [
        dot(stack_heads(part), both_heads(v, low_mask, high_mask), 0, 0)
        for part, (t, i, q, k, v) in zip(probs, chains)
    ]
    total = x
    for duo in range(duos):
        heads = [[], []]
        for t in range(count):
            at = 3 * (duo * count + t)
            one, two, third = outs[at : at + 3]
            heads[0].append(
                jnp.concatenate([jnp.where(low, 0.0, turn(third)), one], axis=1).astype(BF16)
            )
            heads[1].append(
                jnp.concatenate([jnp.where(low, 0.0, third), two], axis=1).astype(BF16)
            )
        for side, group in enumerate((2 * duo, 2 * duo + 1)):
            joined = jnp.concatenate(heads[side], axis=0)
            heads_ref[:, group * 2 * LANES : (group + 1) * 2 * LANES] = joined
            total = total + dot(joined, weights[group, :, 4 * LANES :], 1, 1)
    mid_ref[...] = total
    n2, _ = normalize(total)
    h2_ref[...] = (n2 * norm_ref[2:3, :] + norm_ref[3:4, :]).astype(BF16)


def up_forward(
    order, h2_ref, live_ref, w0, w1, w2, w3,
    hid_ref, slope_ref, pooled_ref,
    weights, sems, *, seq_len,
):
    groups, _, width = weights.shape
    first = pl.program_id(0) == 0

    @pl.when(first)
    def _():
        load_weights(order, (w0, w1, w2, w3), weights, sems)
        for group in range(weights.shape[0]):
            wait_weights(weights, sems, group)

    h2 = h2_ref[...]
    rows = h2.shape[0]
    live = live_ref[:, 0:1]
    seqs = rows // seq_len
    member = (
        lax.broadcasted_iota(jnp.int32, (seqs, rows), 1) // seq_len
        == lax.broadcasted_iota(jnp.int32, (seqs, rows), 0)
    )
    pool = jnp.where(member, 1.0, 0.0).astype(BF16)
    for group in range(groups):


        cols = slice(group * width, (group + 1) * width)
        up = dot(h2, weights[group], 1, 0)
        gate = 0.5 + 0.5 * lax.erf(up * (0.5**0.5))
        hid = (up * gate).astype(BF16)
        hid_ref[:, cols] = hid
        bell = jnp.exp(up * up * -0.5) * (1.0 / math.sqrt(2.0 * math.pi))
        slope_ref[:, cols] = ((gate + up * bell) * live).astype(BF16)
        pooled_ref[:, cols] = dot(pool, hid * live.astype(BF16), 1, 0).astype(BF16)


def down_forward(
    order, hid_ref, mid_ref, live_ref, w0, w1, w2, w3,
    out_ref, pooled_ref, weights, sems, *, seq_len,
):
    groups, _, width = weights.shape
    first = pl.program_id(0) == 0

    @pl.when(first)
    def _():
        load_weights(order, (w0, w1, w2, w3), weights, sems)
        for group in range(weights.shape[0]):
            wait_weights(weights, sems, group)

    total = mid_ref[...]
    for group in range(groups):


        total = total + dot(
            hid_ref[:, group * width : (group + 1) * width], weights[group], 1, 1
        )
    out_ref[...] = total.astype(BF16)
    live = live_ref[:, 0:1]
    rows, features = total.shape
    seqs = rows // seq_len
    sums = jnp.sum((total * live).reshape(seqs, seq_len, features), axis=1)
    counts = jnp.sum(jnp.broadcast_to(live, (rows, LANES)).reshape(seqs, seq_len, LANES), axis=1)
    pooled_ref[...] = sums / counts[:, 0:1]


def contrast(pooled_ref, count_ref, m0, m1, m2, m3, loss_ref, grad_ref, low_ref, *, micros):
    pooled = pooled_ref[...]
    seqs, width = pooled.shape
    each = seqs // micros
    scale_text = SOFTMAX_TEMP / math.sqrt(width)
    r = lax.rsqrt(jnp.mean(pooled * pooled, axis=-1, keepdims=True) + EPSILON)
    text = (pooled * r).astype(BF16)
    row_micro = lax.broadcasted_iota(jnp.int32, (seqs, 1), 0) // each
    step = min(m0.shape[0], 1024)
    pieces = [
        ref[i : i + step, :]
        for ref in (m0, m1, m2, m3)
        for i in range(0, ref.shape[0], step)
    ]
    col = lax.broadcasted_iota(jnp.int32, (1, step), 1)
    same = (col // each) % micros == row_micro
    logits = [jnp.where(same, dot(text, piece, 1, 1) * scale_text, -1e30) for piece in pieces]
    top = functools.reduce(
        jnp.maximum, [jnp.max(part, axis=1, keepdims=True) for part in logits]
    )
    powers = [jnp.exp(part - top) for part in logits]
    total = functools.reduce(jnp.add, [jnp.sum(part, axis=1, keepdims=True) for part in powers])
    log_total = top + jnp.log(total)
    positive = lax.broadcasted_iota(jnp.int32, (seqs, 1), 0) == col
    loss = log_total - jnp.sum(jnp.where(positive, logits[0], 0.0), axis=1, keepdims=True)
    loss_ref[...] = jnp.broadcast_to(loss, loss_ref.shape)
    inverse = LOSS_SCALE / total
    grad_text = jnp.zeros((seqs, width), F32)
    for i, (part, piece) in enumerate(zip(powers, pieces)):
        grad_part = part * inverse
        if i == 0:
            grad_part = grad_part - jnp.where(positive, LOSS_SCALE, 0.0)
        grad_text = grad_text + dot(grad_part.astype(BF16), piece, 1, 0)
    grad_text = grad_text * scale_text
    along = jnp.mean(grad_text * pooled, axis=-1, keepdims=True)
    grad = (r * grad_text - (r * r * r) * pooled * along) / count_ref[:, 0:1]
    grad_ref[...] = grad
    low_ref[...] = grad.astype(BF16)


def drain(slots, sems, which):
    pltpu.make_async_copy(slots.at[which], slots.at[which], sems.at[which]).wait()


def finish_blocks(slots, sems, group, groups, slot):
    @pl.when(group == groups - 1)
    def _():
        drain(slots, sems, slot)

        @pl.when(groups >= 2)
        def _():
            drain(slots, sems, 1 - slot)


def weight_gradient(
    inverse, left_ref, right_ref, g0, g1, g2, g3, turned, slots, sems
):
    group = pl.program_id(0)
    groups = pl.num_programs(0)
    slot = group % 2

    @pl.when(group == 0)
    def _():
        turned[...] = left_ref[...].T

    @pl.when(group >= 2)
    def _():
        drain(slots, sems, slot)

    slots[slot] = dot(turned[...], right_ref[...], 1, 0).astype(BF16)
    store_blocks(inverse, slots.at[slot], group, groups, (g0, g1, g2, g3), sems.at[slot])
    finish_blocks(slots, sems, group, groups, slot)


def attention_gradient(
    inverse, h1_ref, proj_ref, mid_ref, heads_ref, g0, g1, g2, g3,
    turned, turned_mid, slots, sems,
):
    group = pl.program_id(0)
    groups = pl.num_programs(0)
    slot = group % 2

    @pl.when(group == 0)
    def _():
        turned[...] = h1_ref[...].T
        turned_mid[...] = mid_ref[...].T

    @pl.when(group >= 2)
    def _():
        drain(slots, sems, slot)

    slots[slot, :, : 4 * LANES] = dot(turned[...], proj_ref[:, : 4 * LANES], 1, 0).astype(BF16)
    tail = dot(turned_mid[...], heads_ref[...], 1, 0)
    keys = dot(turned[...], proj_ref[:, 4 * LANES :], 1, 0)
    slots[slot, :, 4 * LANES : 5 * LANES] = (keys + tail[:, :LANES]).astype(BF16)
    slots[slot, :, 5 * LANES :] = tail[:, LANES:].astype(BF16)
    store_blocks(inverse, slots.at[slot], group, groups, (g0, g1, g2, g3), sems.at[slot])
    finish_blocks(slots, sems, group, groups, slot)


def norm_back(grad, gain, values):
    n, scale = normalize(values)
    scaled = grad * gain
    moved = scale * (
        scaled
        - jnp.mean(scaled, axis=-1, keepdims=True)
        - n * jnp.mean(scaled * n, axis=-1, keepdims=True)
    )
    gain_grad = jnp.sum(grad * n, axis=0, keepdims=True)
    shift_grad = jnp.sum(grad, axis=0, keepdims=True)
    return moved, gain_grad, shift_grad


def down_backward(order, low_ref, w0, w1, w2, w3, by_seq_ref, weights, sems):
    groups, _, width = weights.shape
    load_weights(order, (w0, w1, w2, w3), weights, sems)
    for group in range(groups):
        wait_weights(weights, sems, group)
        by_seq_ref[:, group * width : (group + 1) * width] = dot(
            low_ref[...], weights[group], 1, 0
        )


def mlp_backward(
    order, grad_ref, by_seq_ref, slope_ref, live_ref, mid_ref, norm_ref,
    w0, w1, w2, w3,
    dup_ref, dmid_ref, dmid_low_ref, sums_ref,
    weights, sems, *, seq_len,
):
    groups, _, width = weights.shape

    @pl.when(pl.program_id(0) == 0)
    def _():
        load_weights(order, (w0, w1, w2, w3), weights, sems)
        sums_ref[...] = jnp.zeros_like(sums_ref)
        for group in range(groups):
            wait_weights(weights, sems, group)

    grad = grad_ref[...]
    mid = mid_ref[...]
    rows, features = mid.shape
    seqs = rows // seq_len

    def spread(values):
        return jnp.broadcast_to(
            values[:, None, :], (seqs, seq_len, values.shape[1])
        ).reshape(rows, values.shape[1])

    total = jnp.zeros((rows, features), F32)
    for group in range(groups):


        cols = slice(group * width, (group + 1) * width)
        dup = (slope_ref[:, cols].astype(F32) * spread(by_seq_ref[:, cols])).astype(BF16)
        dup_ref[:, cols] = dup
        total = total + dot(dup, weights[group], 1, 1)
    moved, gain_grad, shift_grad = norm_back(total, norm_ref[2:3, :], mid)
    dmid = spread(grad) * live_ref[:, 0:1] + moved
    dmid_ref[...] = dmid
    dmid_low_ref[...] = dmid.astype(BF16)
    sums_ref[0:1, :] += gain_grad
    sums_ref[1:2, :] += shift_grad


def attention_backward(
    order, x_ref, live_ref, norm_ref, proj_ref, lse_ref, dmid_ref, dmid_low_ref,
    w0, w1, w2, w3, *rest, seq_len,
):
    dproj_ref, dx_ref, sums_ref, weights, sems = rest[-5:]
    groups = weights.shape[0]
    first = pl.program_id(0) == 0

    @pl.when(first)
    def _():
        load_weights(order, (w0, w1, w2, w3), weights, sems)
        for group in range(weights.shape[0]):
            wait_weights(weights, sems, group)
        sums_ref[...] = jnp.zeros_like(sums_ref)

    x = x_ref[...].astype(F32)
    rows = x.shape[0]
    dmid_low = dmid_low_ref[...]
    low_mask = low_lanes()
    high_mask = 1 - low_mask
    low = lax.broadcasted_iota(jnp.int32, (1, LANES), 1) < HD
    own_cols = sequence_columns(seq_len)
    score_scale = HD**-0.5
    count = rows // LANES
    duos = groups // 2
    dheads = [
        dot(dmid_low, weights[group, :, 4 * LANES :], 1, 0).astype(BF16) for group in range(groups)
    ]
    chains = []
    for duo in range(duos):
        first_d, second_d = dheads[2 * duo : 2 * duo + 2]
        for t in range(count):
            span = slice(t * LANES, (t + 1) * LANES)
            for i, d in enumerate(
                (
                    first_d[span, LANES:],
                    second_d[span, LANES:],
                    jnp.where(low, turn(first_d[span, :LANES]), second_d[span, :LANES]),
                )
            ):
                at = (duo * 3 + i) * 3 * LANES
                q, k, v = (
                    proj_ref[span, at + j * LANES : at + (j + 1) * LANES] for j in range(3)
                )
                qq, kk, dd = (both_heads(part, low_mask, high_mask) for part in (q, k, d))
                chains.append((t, duo * 3 + i, k, v, qq, kk, dd))
    scores = [dot(k, qq, 1, 1) for t, i, k, v, qq, kk, dd in chains]
    powers = [dot(v, dd, 1, 1) for t, i, k, v, qq, kk, dd in chains]
    wide = []
    for (t, i, *_), full, power in zip(chains, scores, powers):
        live = live_ref[t] > 0.0
        compact = diagonal(full, seq_len, own_cols) * score_scale
        lse = lse_ref[t, i : i + 1, :]
        probs = jnp.where(live, jnp.exp(jnp.where(live, compact - lse, 0.0)), 0.0)
        dprobs = diagonal(power, seq_len, own_cols)
        inner = jnp.sum(probs * dprobs, axis=0, keepdims=True)
        dscores = probs * (dprobs - inner) * score_scale
        wide.append(
            (
                undiagonal(dscores.astype(BF16), own_cols),
                undiagonal(probs.astype(BF16), own_cols),
            )
        )
    outs = [
        (dot(stack_heads(ds), kk, 0, 0), dot(ds, qq, 1, 0), dot(p, dd, 1, 0))
        for (ds, p), (t, i, k, v, qq, kk, dd) in zip(wide, chains)
    ]
    total = jnp.zeros(x.shape, F32)
    for duo in range(duos):
        grads = [[], []]
        for t in range(count):
            at = 3 * (duo * count + t)
            one, two, third = outs[at : at + 3]
            grads[0].append(
                jnp.concatenate(
                    one
                    + (jnp.where(low, third[0], turn(third[2])), jnp.where(low, third[1], 0.0)),
                    axis=1,
                ).astype(BF16)
            )
            grads[1].append(
                jnp.concatenate(
                    two
                    + (jnp.where(low, turn(third[0]), third[2]), jnp.where(low, turn(third[1]), 0.0)),
                    axis=1,
                ).astype(BF16)
            )
        for side, group in enumerate((2 * duo, 2 * duo + 1)):
            dproj = jnp.concatenate(grads[side], axis=0)
            dproj_ref[:, group * 5 * LANES : (group + 1) * 5 * LANES] = dproj
            total = total + dot(dproj, weights[group, :, : 5 * LANES], 1, 1)
    moved, gain_grad, shift_grad = norm_back(total, norm_ref[0:1, :], x)
    dx_ref[...] = dmid_ref[...] + moved
    sums_ref[0:1, :] += gain_grad
    sums_ref[1:2, :] += shift_grad


def renew(grad, left, right, left_root, right_root):
    low = grad.astype(BF16)
    keep = 1.0 - STAT_DECAY
    half = dot(left_root.astype(BF16), low, 1, 0).astype(BF16)
    return (
        STAT_DECAY * left + keep * dot(low, low, 1, 1),
        STAT_DECAY * right + keep * dot(low, low, 0, 0),
        SHAMPOO_RATE * dot(half, right_root.astype(BF16), 1, 0),
    )


def shampoo_kernel(*refs):
    terms = refs[:-9]
    stats, master_ref = refs[-9:-5], refs[-5]
    grad_ref, left_new_ref, right_new_ref, new_ref = refs[-4:]
    grad = sum(term[0].astype(F32) for term in terms)
    grad_ref[...] = grad
    left_new_ref[...], right_new_ref[...], step = renew(grad, *(ref[...] for ref in stats))
    new_ref[...] = master_ref[...] - step


def attention_shampoo(*refs):
    terms = refs[:-18]
    qkv_ref, out_ref, *stats = refs[-18:-8]
    qkv_grad, qkv_left, qkv_right, qkv_new, out_grad, out_left, out_right, out_new = refs[-8:]
    packed = sum(term[0].astype(F32) for term in terms)
    qkv, out = unpack_attention(packed)
    out_grad[...] = out
    qkv_left[...], qkv_right[...], step = renew(qkv, *(ref[...] for ref in stats[:4]))
    width = qkv_ref.shape[2]
    for i in range(3):
        cols = slice(i * width, (i + 1) * width)
        qkv_grad[i] = qkv[:, cols]
        qkv_new[i] = qkv_ref[i] - step[:, cols]
    out_left[...], out_right[...], step = renew(out, *(ref[...] for ref in stats[4:]))
    out_new[...] = out_ref[...] - step


ANY = pl.BlockSpec(memory_space=pl.ANY)
SMEM = pl.BlockSpec(memory_space=pltpu.SMEM)
WHOLE = pl.BlockSpec(memory_space=pltpu.VMEM)


def rows_of(width, height=TILE, start=0):
    return pl.BlockSpec((height, width), lambda i: (i + start, 0))


def fixed(shape):
    return pl.BlockSpec(shape, lambda i: (0,) * len(shape))


def params():
    return pltpu.CompilerParams(vmem_limit_bytes=VMEM_BYTES)


def cost(flops, bytes_accessed):
    return pl.CostEstimate(flops=4 * int(flops), bytes_accessed=int(bytes_accessed), transcendentals=0)


def shape_of(*dims, dtype=BF16):
    return jax.ShapeDtypeStruct(dims, dtype)


def shampoo(terms, left_stat, right_stat, left_root, right_root, master):
    rows, cols = master.shape
    grad, left_new, right_new, new = pl.pallas_call(
        shampoo_kernel,
        grid=(1,),
        out_shape=(
            shape_of(rows, cols, dtype=F32),
            shape_of(rows, rows, dtype=F32),
            shape_of(cols, cols, dtype=F32),
            shape_of(rows, cols, dtype=F32),
        ),
        in_specs=[pl.BlockSpec((1, rows, cols), lambda i: (0, 0, 0))] * len(terms) + [WHOLE] * 5,
        out_specs=(WHOLE,) * 4,
        compiler_params=params(),
        cost_estimate=cost(4 * rows * cols * cols, 12 * cols * cols),
        name="shampoo",
    )(*terms, left_stat[0, 0], right_stat[0, 0], left_root[0, 0], right_root[0, 0], master)
    return grad, left_new[None, None], right_new[None, None], new


def pack_attention(qkv, out):
    q, k, v = (qkv[:, i] for i in range(3))
    a, b = 2 * HD, 3 * HD
    return jnp.concatenate(
        [q[:, :a], k[:, :a], v[:, :a], q[:, a:b], v[:, a:b], k[:, a:b], out[:, a:b], out[:, :a]],
        axis=1,
    )


def unpack_attention(packed):
    c = [packed[:, i * HD : (i + 1) * HD] for i in range(12)]
    qkv = jnp.concatenate([c[0], c[1], c[6], c[2], c[3], c[8], c[4], c[5], c[7]], axis=1)
    return qkv, jnp.concatenate([c[10], c[11], c[9]], axis=1)


def per_device(
    block_in, seq_lengths, image_embed, w_qkv, w_out, w_up, w_down, norm_params, norm_second,
    qkv_left, qkv_right, qkv_left_root, qkv_right_root,
    out_left, out_right, out_left_root, out_right_root,
    up_left, up_right, up_left_root, up_right_root,
    down_left, down_right, down_left_root, down_right_root,
):
    micros, seqs, seq_len, width = block_in.shape
    dp_count, groups = lax.axis_size("dp"), lax.axis_size("mp")
    count = dp_count * groups
    dp_index = lax.axis_index("dp")
    me = dp_index * groups + lax.axis_index("mp")
    owned = w_up.shape[0]
    ff = w_up.shape[1]
    all_seqs = micros * seqs
    rows = all_seqs * seq_len
    tiles = rows // TILE
    seq_tile = TILE // seq_len
    direct = owned % 16 == 0

    def places(near_first):
        table = source_table(count, near_first)
        return (
            jnp.asarray(table, jnp.int32)[me],
            jnp.asarray(np.argsort(table, axis=1), jnp.int32)[me],
        )

    order, inverse = places(False)
    near_order, near_inverse = places(True)

    def weights_of(gather, inverse):
        quarters = gather.quarters()
        if direct:
            return quarters
        whole = jnp.concatenate(quarters, axis=0)[inverse]
        whole = whole.reshape(dp_count, groups, owned, whole.shape[-1])
        whole = whole.transpose(1, 0, 2, 3).reshape(groups, width, whole.shape[-1])
        return tuple(jnp.split(whole, 4, axis=0))

    kernel_order = order if direct else jnp.arange(groups, dtype=jnp.int32)
    kernel_near_order = near_order if direct else kernel_order
    kernel_inverse = inverse if direct else jnp.arange(groups, dtype=jnp.int32)
    block_rows = owned if direct else width
    quarter = (count if direct else groups) // 4

    def sum_of(quarters):
        if not direct:
            whole = jnp.concatenate(quarters, axis=0)
            whole = whole.reshape(groups, dp_count, owned, whole.shape[2])
            whole = whole.transpose(1, 0, 2, 3).reshape(count, owned, whole.shape[3])[order]
            quarters = jnp.split(whole, 4, axis=0)
        return Sum(quarters, count)

    own_blocks = [w_up.astype(BF16), w_down.astype(BF16), image_embed.reshape(all_seqs, width)]
    gather_attention = Gather(pack_attention(w_qkv.astype(BF16), w_out.astype(BF16)), count)
    gather_up, gather_down, gather_images = (Gather(block, count) for block in own_blocks)
    gather_attention.far()
    from_near = swap(jnp.concatenate(own_blocks, axis=0), near_steps(count)[0])
    from_near = jnp.split(from_near, (owned, 2 * owned), axis=0)
    for gather, received in zip((gather_up, gather_down, gather_images), from_near):
        gather.received = [received[None]]
    gather_up.keep()
    gather_attention.keep(gather_up.held)
    gather_attention.first()
    gather_up.far(gather_attention.held)

    x = block_in.reshape(rows, width)
    norms = norm_params.T
    lengths = seq_lengths.reshape(all_seqs)
    live = (jnp.arange(seq_len)[None, :] < lengths[:, None]).astype(F32).reshape(rows)
    live_cols = jnp.broadcast_to(live[:, None], (rows, LANES))
    tile_seqs = LANES // seq_len
    live_keys = live.reshape(rows // LANES, tile_seqs, 1, seq_len)
    live_keys = jnp.broadcast_to(
        live_keys, (rows // LANES, tile_seqs, seq_len, seq_len)
    ).transpose(0, 3, 1, 2).reshape(rows // LANES, seq_len, LANES)
    live_keys = jnp.concatenate([live_keys, live_keys], axis=2)
    counts = jnp.broadcast_to(lengths.astype(F32)[:, None], (all_seqs, LANES))

    live_spec = rows_of(LANES)
    keys_spec = pl.BlockSpec((TILE // LANES, seq_len, 2 * LANES), lambda i: (i, 0, 0))
    lse_spec = pl.BlockSpec((TILE // LANES, 8, 2 * LANES), lambda i: (i, 0, 0))
    norm_spec = fixed((4, width))

    def weight_scratch(cols):
        return [pltpu.VMEM((groups, width, cols), BF16), pltpu.SemaphoreType.DMA((groups,))]

    packed = 6 * LANES
    (x_ready,) = after([x], gather_attention.held)
    h1 = pl.pallas_call(
        first_norm,
        grid=(tiles,),
        in_specs=[rows_of(width), norm_spec],
        out_specs=rows_of(width),
        out_shape=shape_of(rows, width),
        compiler_params=params(),
        cost_estimate=cost(1, 100e6),
        name="first_norm",
    )(x_ready, norms)

    gather_attention.keep(h1)
    gather_attention.held, *gather_up.received = join(
        gather_attention.held, *gather_up.received[:-1]
    ) + (gather_up.received[-1],)
    gather_attention.second()
    gather_attention.third()
    gather_attention.across, *gather_up.received = join(
        gather_attention.across, *gather_up.received
    )
    gather_attention.last()
    gather_up.keep()
    gather_up.second(gather_attention.across)
    gather_up.third()
    attention_w = weights_of(gather_attention, inverse)
    gather_down.keep()
    gather_down.far(gather_up.held)

    (h1_ready,) = after([h1], gather_up.held)
    proj, heads, lse, mid, h2 = pl.pallas_call(
        functools.partial(attention_forward, seq_len=seq_len),
        grid=(tiles,),
        in_specs=[SMEM, rows_of(width), rows_of(width), keys_spec, norm_spec, ANY, ANY, ANY, ANY],
        out_specs=(
            rows_of(3 * width), rows_of(groups * 2 * LANES), lse_spec, rows_of(width),
            rows_of(width),
        ),
        out_shape=(
            shape_of(rows, 3 * width), shape_of(rows, groups * 2 * LANES),
            shape_of(rows // LANES, 8, 2 * LANES, dtype=F32),
            shape_of(rows, width, dtype=F32), shape_of(rows, width),
        ),
        scratch_shapes=weight_scratch(packed),
        compiler_params=params(),
        cost_estimate=cost(2 * rows * width * groups * 900, 12e6),
        name="attention_forward",
    )(kernel_order, x, h1_ready, live_keys, norms, *attention_w)

    gather_down.keep(h2)
    gather_up.last(gather_down.held)
    gather_down.second()
    gather_down.third()
    gather_images.keep()
    gather_images.far(gather_down.held)
    up_w = weights_of(gather_up, near_inverse)
    (h2_ready,) = after([h2], gather_down.held)

    hid, slope, pooled_hid = pl.pallas_call(
        functools.partial(up_forward, seq_len=seq_len),
        grid=(tiles,),
        in_specs=[SMEM, rows_of(width), live_spec, ANY, ANY, ANY, ANY],
        out_specs=(rows_of(groups * ff), rows_of(groups * ff), rows_of(groups * ff, seq_tile)),
        out_shape=(
            shape_of(rows, groups * ff), shape_of(rows, groups * ff), shape_of(all_seqs, groups * ff),
        ),
        scratch_shapes=weight_scratch(ff),
        compiler_params=params(),
        cost_estimate=cost(2 * rows * width * groups * ff, 20e6),
        name="up_forward",
    )(kernel_near_order, h2_ready, live_cols, *up_w)

    gather_images.keep(hid)
    gather_down.last(hid, gather_images.held)
    gather_images.second(gather_down.across)
    gather_images.third()
    down_w = weights_of(gather_down, near_inverse)
    (hid_ready,) = after([hid], gather_images.held)

    block_out, pooled = pl.pallas_call(
        functools.partial(down_forward, seq_len=seq_len),
        grid=(tiles,),
        in_specs=[SMEM, rows_of(groups * ff), rows_of(width), live_spec, ANY, ANY, ANY, ANY],
        out_specs=(rows_of(width), rows_of(width, seq_tile)),
        out_shape=(shape_of(rows, width), shape_of(all_seqs, width, dtype=F32)),
        scratch_shapes=weight_scratch(ff),
        compiler_params=params(),
        cost_estimate=cost(2 * rows * width * groups * ff, 20e6),
        name="down_forward",
    )(kernel_near_order, hid_ready, mid, live_cols, *down_w)

    gather_images.last(pooled)
    images = gather_images.quarters()
    images = [part.reshape(-1, width) for part in images]
    loss, grad_seq, grad_low = pl.pallas_call(
        functools.partial(contrast, micros=micros),
        in_specs=[WHOLE] * 6,
        out_specs=(WHOLE,) * 3,
        out_shape=(
            shape_of(all_seqs, LANES, dtype=F32), shape_of(all_seqs, width, dtype=F32),
            shape_of(all_seqs, width),
        ),
        compiler_params=params(),
        cost_estimate=cost(4 * all_seqs * width * images[0].shape[0] * 4, 4e6),
        name="contrast",
    )(pooled, counts, *images)

    gradient_out = (shape_of(quarter, block_rows, packed),) * 4

    def gradient(kernel, lefts, rights, widths):
        depth = lefts[0].shape[0]
        specs = [
            (fixed((depth, width)), pl.BlockSpec((depth, cols), lambda i: (0, i)))
            for cols in widths
        ]
        return pl.pallas_call(
            kernel,
            grid=(groups,),
            in_specs=[SMEM] + [spec for pair in specs for spec in pair],
            out_specs=(ANY,) * 4,
            out_shape=gradient_out,
            scratch_shapes=[pltpu.VMEM((width, depth), BF16) for _ in lefts]
            + [pltpu.VMEM((2, width, packed), BF16), pltpu.SemaphoreType.DMA((2,))],
            compiler_params=params(),
            cost_estimate=cost(2 * depth * width * groups * 900, 10e6),
            name=kernel.__name__,
        )(kernel_inverse, *(part for pair in zip(lefts, rights) for part in pair))

    sum_down = sum_of(gradient(weight_gradient, (grad_low,), (pooled_hid,), (ff,)))

    by_seq = pl.pallas_call(
        down_backward,
        in_specs=[SMEM, WHOLE, ANY, ANY, ANY, ANY],
        out_specs=WHOLE,
        out_shape=shape_of(all_seqs, groups * ff, dtype=F32),
        scratch_shapes=weight_scratch(ff),
        compiler_params=params(),
        cost_estimate=cost(8 * all_seqs * width * groups * ff, 6e6),
        name="down_backward",
    )(kernel_near_order, grad_low, *down_w)

    sum_down.second(by_seq)
    (grad_ready,) = after([grad_seq], sum_down.going)
    dup, dmid, dmid_low, sums_two = pl.pallas_call(
        functools.partial(mlp_backward, seq_len=seq_len),
        grid=(tiles,),
        in_specs=[
            SMEM, rows_of(width, seq_tile), rows_of(groups * ff, seq_tile), rows_of(groups * ff),
            live_spec, rows_of(width), norm_spec, ANY, ANY, ANY, ANY,
        ],
        out_specs=(rows_of(groups * ff), rows_of(width), rows_of(width), fixed((8, width))),
        out_shape=(
            shape_of(rows, groups * ff), shape_of(rows, width, dtype=F32), shape_of(rows, width),
            shape_of(8, width, dtype=F32),
        ),
        scratch_shapes=weight_scratch(ff),
        compiler_params=params(),
        cost_estimate=cost(2 * rows * width * groups * ff, 25e6),
        name="mlp_backward",
    )(kernel_near_order, grad_ready, by_seq, slope, live_cols, mid, norms, *up_w)

    sum_down.first(dmid)
    (h2_ready,) = after([h2], sum_down.going)
    up_parts = gradient(weight_gradient, (h2_ready,), (dup,), (ff,))
    *up_parts, sum_down.received = join(*up_parts, sum_down.received)
    sum_up = sum_of(up_parts)
    sum_down.far()
    sum_up.second()

    def backward(start, ready, earlier=()):
        return pl.pallas_call(
            functools.partial(attention_backward, seq_len=seq_len),
            grid=(tiles,),
            in_specs=[
                SMEM, rows_of(width, start=start),
                pl.BlockSpec((TILE // LANES, seq_len, 2 * LANES), lambda i: (i + start, 0, 0)),
                norm_spec, rows_of(3 * width, start=start),
                pl.BlockSpec((TILE // LANES, 8, 2 * LANES), lambda i: (i + start, 0, 0)),
                rows_of(width, start=start), rows_of(width, start=start),
            ] + [ANY] * (4 + len(earlier)),
            out_specs=(
                rows_of(groups * 5 * LANES, start=start), rows_of(width, start=start),
                fixed((8, width)),
            ),
            out_shape=(
                shape_of(rows, groups * 5 * LANES), shape_of(rows, width, dtype=F32),
                shape_of(8, width, dtype=F32),
            ),
            scratch_shapes=weight_scratch(packed),
            input_output_aliases={12 + i: i for i in range(len(earlier))},
            compiler_params=params(),
            cost_estimate=cost(rows * width * groups * 1300, 20e6),
            name="attention_backward",
        )(
            kernel_order, ready, live_keys, norms, proj, lse, dmid, dmid_low, *attention_w, *earlier
        )

    (x_ready,) = after([x], sum_up.going, sum_down.going)
    dproj, input_grad, sums_one = backward(0, x_ready)
    sum_up.first(sums_one)
    norm_sum = jnp.concatenate([sums_one[:2], sums_two[:2]], axis=0)

    def exchanged(values, bit):
        return swap(values, [i ^ bit for i in range(count)])

    (h1_ready,) = after([h1], sum_up.going, *sum_down.keep)
    received = exchanged(norm_sum, 1)
    attention_parts = gradient(
        attention_gradient, (h1_ready, dmid_low), (dproj, heads), (5 * LANES, 2 * LANES)
    )
    *attention_parts, sum_up.received, received = join(
        *attention_parts, sum_up.received, received
    )
    norm_sum = norm_sum + received
    sum_attention = sum_of(attention_parts)
    sum_attention.second()
    sum_up.far()
    sum_down.keep = after(sum_down.keep, sum_attention.going)
    grad_down, down_left_new, down_right_new, down_new = shampoo(
        sum_down.keep, down_left, down_right, down_left_root, down_right_root, w_down
    )
    (norm_sum,) = after([norm_sum], sum_attention.going)
    bit = 8
    while bit < count:
        norm_sum = norm_sum + exchanged(norm_sum, bit)
        bit *= 2
    sum_attention.first(norm_sum, down_new)
    sum_up.keep = after(sum_up.keep, sum_attention.going)
    grad_up, up_left_new, up_right_new, up_new = shampoo(
        sum_up.keep, up_left, up_right, up_left_root, up_right_root, w_up
    )
    sum_attention.far(up_new)
    (norm_sum,) = after([norm_sum], sum_attention.going)
    for bit in (2, 4):
        norm_sum = norm_sum + exchanged(norm_sum, bit)
    *sum_attention.keep, norm_sum = join(*sum_attention.keep, norm_sum)
    grad_norm = lax.dynamic_slice_in_dim(norm_sum, dp_index * owned, owned, 1).T

    qkv_turned = w_qkv.transpose(1, 0, 2)
    (
        grad_qkv, qkv_left_new, qkv_right_new, qkv_new,
        grad_out, out_left_new, out_right_new, out_new,
    ) = pl.pallas_call(
        attention_shampoo,
        grid=(1,),
        in_specs=[pl.BlockSpec((1, owned, packed), lambda i: (0, 0, 0))] * len(sum_attention.keep)
        + [WHOLE] * 10,
        out_specs=(WHOLE,) * 8,
        out_shape=(
            shape_of(*qkv_turned.shape, dtype=F32), shape_of(owned, owned, dtype=F32),
            shape_of(*qkv_right.shape[2:], dtype=F32), shape_of(*qkv_turned.shape, dtype=F32),
            shape_of(*w_out.shape, dtype=F32), shape_of(owned, owned, dtype=F32),
            shape_of(*out_right.shape[2:], dtype=F32), shape_of(*w_out.shape, dtype=F32),
        ),
        compiler_params=params(),
        cost_estimate=cost(4 * owned * 576 * 576, 12 * 576 * 576),
        name="attention_shampoo",
    )(
        *sum_attention.keep, qkv_turned, w_out,
        *(
            stat[0, 0]
            for stat in (
                qkv_left, qkv_right, qkv_left_root, qkv_right_root,
                out_left, out_right, out_left_root, out_right_root,
            )
        ),
    )
    grad_qkv, qkv_new = grad_qkv.transpose(1, 0, 2), qkv_new.transpose(1, 0, 2)
    qkv_left_new, qkv_right_new, out_left_new, out_right_new = (
        stat[None, None] for stat in (qkv_left_new, qkv_right_new, out_left_new, out_right_new)
    )
    norm_second_new = STAT_DECAY * norm_second + (1.0 - STAT_DECAY) * grad_norm * grad_norm
    own_params = lax.dynamic_slice_in_dim(norm_params, dp_index * owned, owned, 0)
    norm_new = own_params - NORM_RATE * grad_norm / (jnp.sqrt(norm_second_new) + 1e-08)
    return (
        block_out.reshape(block_in.shape),
        input_grad.reshape(block_in.shape),
        loss[:, 0].reshape(micros, seqs),
        grad_qkv, qkv_left_new, qkv_right_new, qkv_new,
        grad_out, out_left_new, out_right_new, out_new,
        grad_up, up_left_new, up_right_new, up_new,
        grad_down, down_left_new, down_right_new, down_new,
        grad_norm, norm_second_new, norm_new,
    )


def solution(mesh):
    sequence = P(None, AXES)
    stat = P("dp", "mp", None, None)
    weight = P("dp", "mp")
    qkv = P("dp", None, "mp")
    norm = P("dp", None)
    in_specs = (sequence, sequence, sequence, qkv, weight, weight, weight, P(), norm) + (stat,) * 16
    out_specs = (
        (sequence, sequence, sequence)
        + (qkv, stat, stat, qkv)
        + (weight, stat, stat, weight) * 3
        + (norm, norm, norm)
    )
    return jax.shard_map(
        per_device, mesh=mesh, in_specs=in_specs, out_specs=out_specs, check_vma=False
    )
```

time: 415 us -> 279 us (0.67)
  Pallas kernels: 190 us -> 134 us
  waiting for transfers between devices: 100 us -> 61.6 us
  other arithmetic: 27.7 us -> 8.68 us
  local copies, waits for them, and re-layouts: 32.4 us -> 15.9 us
  starting transfers between devices: 61.7 us -> 55.4 us
    ppermute x40 -> x52, waiting for transfers between devices: 100 us -> 61.6 us  [swap(): return lax.ppermute(values, AXES, list(enumerate(step)))]
    pallas_call x1, Pallas kernels: 41.4 us -> 16.4 us  [per_device(): pl.pallas_call(functools.partial(attention_forward, seq_len=seq_len), gri...]
    pallas_call x8 -> x9, Pallas kernels: 89.5 us -> 71.6 us  [the longest x3 26.8 us: gradient(): pl.pallas_call(kernel, grid=(groups,), in_specs=[SMEM] + [spec for pair i...]
    unnamed x53 -> x93, local copies, waits for them, and re-layouts: 15.6 us -> 6.22 us
    pallas_call x1, Pallas kernels: 22.1 us -> 14 us  [per_device(): pl.pallas_call(functools.partial(mlp_backward, seq_len=seq_len), grid=(ti...]
    concatenate x13 -> x6, other arithmetic: 9.17 us -> 1.27 us  [the longest x1 0.96 us: per_device(): from_near = swap(jnp.concatenate(own_blocks, axis=0), near_steps(count)[0])]
    ppermute x40 -> x52, starting transfers between devices: 61.7 us -> 55.4 us  [swap(): return lax.ppermute(values, AXES, list(enumerate(step)))]
    convert_element_type x12 -> x11, other arithmetic: 10.2 us -> 5.82 us  [the longest x9 3.8 us: add_low(): return sum((term.astype(F32) for term in terms)).astype(BF16)]
  transfers between devices with their start and end apart: 40 -> 52, of which waited for: 18 -> 19; matrix products, arithmetic and copies ran while one was open for 14% -> 5% of each run, Pallas kernels for 24% -> 43%
where the time goes in v2:
time: 279 us; the launch traced here: 277 us
  Pallas kernels  134 us (48%)
  waiting for transfers between devices  61.6 us (22%)
  starting transfers between devices  55.4 us (20%)
  local copies, waits for them, and re-layouts  15.9 us (6%)
  other arithmetic  8.68 us (3%)
    ppermute x52, waiting for transfers between devices, swap(): return lax.ppermute(values, AXES, list(enumerate(step)))  61.6 us
    ppermute x52, starting transfers between devices, swap(): return lax.ppermute(values, AXES, list(enumerate(step)))  55.4 us
    pallas_call x3, Pallas kernels, gradient(): pl.pallas_call(kernel, grid=(groups,), in_specs=[SMEM] + [spec for pair i...  26.8 us
    pallas_call x1, Pallas kernels, backward(): pl.pallas_call(functools.partial(attention_backward, seq_len=seq_len), gr...  20.6 us
    pallas_call x1, Pallas kernels, per_device(): pl.pallas_call(functools.partial(attention_forward, seq_len=seq_len), gri...  16.4 us
    pallas_call x1, Pallas kernels, per_device(): pl.pallas_call(functools.partial(up_forward, seq_len=seq_len), grid=(tile...  15.9 us
    pallas_call x1, Pallas kernels, per_device(): pl.pallas_call(functools.partial(mlp_backward, seq_len=seq_len), grid=(ti...  14 us
    pallas_call x1, Pallas kernels, per_device(): pl.pallas_call(functools.partial(down_forward, seq_len=seq_len), grid=(ti...  11.3 us
  transfers between devices with their start and end apart: 52, of which 19 were waited for; matrix products, arithmetic and copies ran while one was open for 5% of the time, Pallas kernels for 43%

profile of v2, /device:TPU:0, one launch (start us, length us, event | category | flops | bytes accessed | tf_op | source)
XLA Modules:
  0.0 277.3 jit_solution(4371690105435278263)
XLA Ops:
  7.0 3.7 %collective-permute-start.2 = (bf16[1,96,768]{2,1,0:T(8,128)(2,1)S(1)}, bf16[1,96,768]{2,1,0:T(8,128)(2,1)S(1)}, u32[]{:S(2)}, u32[]{:S(2)}) collective-permute-start(bf16[1,96,768]{2,1,0:T(8,128)(2,1)S(1)} %bitcast.77), channel_id=1, source_target_pairs={{0,24},{1,25},{2,26},{3,27},{4,28},{5,29},{6,30},{7,31},{8,16},{9,... | collective-permute-start | bytes 442376 | tf_op jit(solution)/shard_map/ppermute | solution.py:60
  15.6 7.2 %collective-permute-done.1 = bf16[1,96,768]{2,1,0:T(8,128)(2,1)S(1)} collective-permute-done((bf16[1,96,768]{2,1,0:T(8,128)(2,1)S(1)}, bf16[1,96,768]{2,1,0:T(8,128)(2,1)S(1)}, u32[]{:S(2)}, u32[]{:S(2)}) %collective-permute-start.1) | collective-permute-done | bytes 147488 | tf_op jit(solution)/shard_map/ppermute | solution.py:60
  29.5 4.1 %first_norm.1.h1_ref = bf16[1024,768]{1,0:T(8,128)(2,1)} custom-call(bf16[1024,768]{1,0:T(8,128)(2,1)} %bitcast.72, f32[4,768]{1,0:T(4,128)} %bitcast.95), custom_call_target="tpu_custom_call" | custom-call | flops 4 | bytes 100000000 | tf_op jit(solution)/shard_map/first_norm/pallas_call | solution.py:853
  35.2 3.2 %collective-permute-done.6 = bf16[2,96,768]{2,1,0:T(8,128)(2,1)S(1)} collective-permute-done((bf16[2,96,768]{2,1,0:T(8,128)(2,1)S(1)}, bf16[2,96,768]{2,1,0:T(8,128)(2,1)S(1)}, u32[]{:S(2)}, u32[]{:S(2)}) %collective-permute-start.6) | collective-permute-done | bytes 294944 | tf_op jit(solution)/shard_map/ppermute | solution.py:60
  42.3 9.2 %collective-permute-done.8 = bf16[2,96,768]{2,1,0:T(8,128)(2,1)S(1)} collective-permute-done((bf16[2,96,768]{2,1,0:T(8,128)(2,1)S(1)}, bf16[2,96,768]{2,1,0:T(8,128)(2,1)S(1)}, u32[]{:S(2)}, u32[]{:S(2)}) %collective-permute-start.8) | collective-permute-done | bytes 294944 | tf_op jit(solution)/shard_map/ppermute | solution.py:60
  51.5 3.6 %collective-permute-done.7.w1 = bf16[8,96,768]{2,1,0:T(8,128)(2,1)} collective-permute-done((bf16[8,96,768]{2,1,0:T(8,128)(2,1)}, bf16[8,96,768]{2,1,0:T(8,128)(2,1)}, u32[]{:S(2)}, u32[]{:S(2)}) %collective-permute-start.7) | collective-permute-done | bytes 1179680 | tf_op jit(solution)/shard_map/ppermute | solution.py:60
  63.8 16.4 %attention_forward.1 = (bf16[1024,2304]{1,0:T(8,128)(2,1)}, bf16[1024,1024]{1,0:T(8,128)(2,1)}, f32[8,8,256]{2,1,0:T(8,128)}, f32[1024,768]{1,0:T(8,128)}, bf16[1024,768]{1,0:T(8,128)(2,1)}) custom-call(s32[32]{0:T(128)} %fusion.5.order, bf16[1024,768]{1,0:T(8,128)(2,1)} %bitcast.73, bf16[1024,768]{1,0:T(8,128)(2,1)} %first_norm.1.h1_ref, ...), custom_call_target="tpu_custom_call" | custom-call | flops 22649241600 | bytes 12000000 | tf_op jit(solution)/shard_map/attention_forward/pallas_call | solution.py:882
  80.3 5.1 %collective-permute-done.12 = bf16[2,96,768]{2,1,0:T(8,128)(2,1)S(1)} collective-permute-done((bf16[2,96,768]{2,1,0:T(8,128)(2,1)S(1)}, bf16[2,96,768]{2,1,0:T(8,128)(2,1)S(1)}, u32[]{:S(2)}, u32[]{:S(2)}) %collective-permute-start.12) | collective-permute-done | bytes 294944 | tf_op jit(solution)/shard_map/ppermute | solution.py:60
  95.7 15.9 %up_forward.1 = (bf16[1024,3072]{1,0:T(8,128)(2,1)}, bf16[1024,3072]{1,0:T(8,128)(2,1)}, bf16[64,3072]{1,0:T(8,128)(2,1)}) custom-call(s32[32]{0:T(128)} %fusion.4.order, bf16[1024,768]{1,0:T(8,128)(2,1)} %get-tuple-element.183.h2_ref.left_ref, f32[1024,128]{1,0:T(8,128)} %broadcast_in_dim.65.live_ref, bf16[8,96,768]{2,1,0:T(8,128)(2,1)} %copy-done.10, ...), custom_call_target="tpu_custom_call" | custom-call | flops 19327352832 | bytes 20000000 | tf_op jit(solution)/shard_map/up_forward/pallas_call | solution.py:910
  115.6 11.3 %down_forward.1 = (bf16[1024,768]{1,0:T(8,128)(2,1)}, f32[64,768]{1,0:T(8,128)}) custom-call(s32[32]{0:T(128)} %fusion.4.order, bf16[1024,3072]{1,0:T(8,128)(2,1)} %get-tuple-element.166.hid_ref, f32[1024,768]{1,0:T(8,128)} %get-tuple-element.167.mid_ref, f32[1024,128]{1,0:T(8,128)} %broadcast_in_dim.65.live_ref, bf16[8,96,768]{2,1,0:T(8,128)(2,1)} %copy-done.28, ...), custom_call_target="tpu_custom_call" | custom-call | flops 19327352832 | bytes 20000000 | tf_op jit(solution)/shard_map/down_forward/pallas_call | solution.py:931
  130.2 4.9 %contrast.1 = (f32[64,128]{1,0:T(8,128)}, f32[64,768]{1,0:T(8,128)}, bf16[64,768]{1,0:T(8,128)(2,1)}) custom-call(f32[64,768]{1,0:T(8,128)} %get-tuple-element.169.pooled_ref, f32[64,128]{1,0:T(8,128)} %broadcast_in_dim.67.count_ref, bf16[512,768]{1,0:T(8,128)(2,1)} %bitcast.94, bf16[512,768]{1,0:T(8,128)(2,1)} %bitcast.103, bf16[512,768]{1,0:T(8,128)(2,1)} %bitcast.102, ...), custom_call_target="tpu_custom_call" | custom-call | flops 1610612736 | bytes 4000000 | tf_op jit(solution)/shard_map/contrast/pallas_call | solution.py:946
  135.1 4.7 %weight_gradient.2 = (bf16[8,96,768]{2,1,0:T(8,128)(2,1)}, bf16[8,96,768]{2,1,0:T(8,128)(2,1)}, bf16[8,96,768]{2,1,0:T(8,128)(2,1)}, bf16[8,96,768]{2,1,0:T(8,128)(2,1)}) custom-call(s32[32]{0:T(128)} %fusion.6.inverse, bf16[64,768]{1,0:T(8,128)(2,1)} %get-tuple-element.171.left_ref.low_ref, bf16[64,3072]{1,0:T(8,128)(2,1)} %get-tuple-element.172.right_ref), custom_call_target="tpu_custom_call" | custom-call | flops 1415577600 | bytes 10000000 | tf_op jit(solution)/shard_map/weight_gradient/pallas_call | solution.py:967
  140.4 5.6 %down_backward.1.by_seq_ref = f32[64,3072]{1,0:T(8,128)} custom-call(s32[32]{0:T(128)} %fusion.4.order, bf16[64,768]{1,0:T(8,128)(2,1)} %get-tuple-element.171.left_ref.low_ref, bf16[8,96,768]{2,1,0:T(8,128)(2,1)} %copy-done.28, bf16[8,96,768]{2,1,0:T(8,128)(2,1)} %copy-done.35, bf16[8,96,768]{2,1,0:T(8,128)(2,1)} %copy-done.34, bf16[8,96,768]{2,1,0:T(8,128)(2,1)} %copy-done.37), custom_call_target="tpu_custom_call" | custom-call | flops 4831838208 | bytes 6000000 | tf_op jit(solution)/shard_map/down_backward/pallas_call | solution.py:982
  147.8 14.0 %mlp_backward.1 = (bf16[1024,3072]{1,0:T(8,128)(2,1)}, f32[1024,768]{1,0:T(8,128)}, bf16[1024,768]{1,0:T(8,128)(2,1)}, f32[8,768]{1,0:T(8,128)}) custom-call(s32[32]{0:T(128)} %fusion.4.order, f32[64,768]{1,0:T(8,128)} %get-tuple-element.179.grad_ref, f32[64,3072]{1,0:T(8,128)} %down_backward.1.by_seq_ref, bf16[1024,3072]{1,0:T(8,128)(2,1)} %get-tuple-element.180.slope_ref, ...), custom_call_target="tpu_custom_call" | custom-call | flops 19327352832 | bytes 25000000 | tf_op jit(solution)/shard_map/mlp_backward/pallas_call | solution.py:995
  164.7 9.8 %weight_gradient.3 = (bf16[8,96,768]{2,1,0:T(8,128)(2,1)}, bf16[8,96,768]{2,1,0:T(8,128)(2,1)}, bf16[8,96,768]{2,1,0:T(8,128)(2,1)}, bf16[8,96,768]{2,1,0:T(8,128)(2,1)}) custom-call(s32[32]{0:T(128)} %fusion.6.inverse, bf16[1024,768]{1,0:T(8,128)(2,1)} %get-tuple-element.183.h2_ref.left_ref, bf16[1024,3072]{1,0:T(8,128)(2,1)} %get-tuple-element.184.right_ref), custom_call_target="tpu_custom_call" | custom-call | flops 22649241600 | bytes 10000000 | tf_op jit(solution)/shard_map/weight_gradient/pallas_call | solution.py:967
  180.9 20.6 %attention_backward.1 = (bf16[1024,2560]{1,0:T(8,128)(2,1)}, f32[1024,768]{1,0:T(8,128)}, f32[8,768]{1,0:T(8,128)}) custom-call(s32[32]{0:T(128)} %fusion.5.order, bf16[1024,768]{1,0:T(8,128)(2,1)} %bitcast.74, f32[8,16,256]{2,1,0:T(8,128)} %copy-done.30, f32[4,768]{1,0:T(4,128)} %bitcast.98, bf16[1024,2304]{1,0:T(8,128)(2,1)} %get-tuple-element.193.proj_ref, ...), custom_call_target="tpu_custom_call" | custom-call | flops 16357785600 | bytes 20000000 | tf_op jit(solution)/shard_map/attention_backward/pallas_call | solution.py:1022
  204.9 12.2 %attention_gradient.1 = (bf16[8,96,768]{2,1,0:T(8,128)(2,1)}, bf16[8,96,768]{2,1,0:T(8,128)(2,1)}, bf16[8,96,768]{2,1,0:T(8,128)(2,1)}, bf16[8,96,768]{2,1,0:T(8,128)(2,1)}) custom-call(s32[32]{0:T(128)} %fusion.6.inverse, bf16[1024,768]{1,0:T(8,128)(2,1)} %first_norm.1.h1_ref, bf16[1024,2560]{1,0:T(8,128)(2,1)} %get-tuple-element.203.proj_ref, ...), custom_call_target="tpu_custom_call" | custom-call | flops 22649241600 | bytes 10000000 | tf_op jit(solution)/shard_map/attention_gradient/pallas_call | solution.py:967
  222.4 3.7 %collective-permute-done.41 = f32[4,768]{1,0:T(4,128)S(1)} collective-permute-done((f32[4,768]{1,0:T(4,128)S(1)}, f32[4,768]{1,0:T(4,128)S(1)}, u32[]{:S(2)}, u32[]{:S(2)}) %collective-permute-start.41) | collective-permute-done | bytes 12320 | tf_op jit(solution)/shard_map/ppermute | solution.py:60
  227.0 5.0 %shampoo.2 = (f32[96,768]{1,0:T(8,128)}, f32[96,96]{1,0:T(8,128)}, f32[768,768]{1,0:T(8,128)}, f32[96,768]{1,0:T(8,128)}) custom-call(bf16[4,96,768]{2,1,0:T(8,128)(2,1)} %copy-done, bf16[4,96,768]{2,1,0:T(8,128)(2,1)} %copy-done.5, bf16[1,96,768]{2,1,0:T(8,128)(2,1)} %copy-done.20, bf16[1,96,768]{2,1,0:T(8,128)(2,1)} %copy-done.19, ...), custom_call_target="tpu_custom_call" | custom-call | flops 905969664 | bytes 7077888 | tf_op jit(solution)/shard_map/shampoo/pallas_call | solution.py:731
  232.0 6.2 %collective-permute-done.40 = bf16[8,96,768]{2,1,0:T(8,128)(2,1)S(1)} collective-permute-done((bf16[8,96,768]{2,1,0:T(8,128)(2,1)S(1)}, bf16[8,96,768]{2,1,0:T(8,128)(2,1)S(1)}, u32[]{:S(2)}, u32[]{:S(2)}) %collective-permute-start.40) | collective-permute-done | bytes 1179680 | tf_op jit(solution)/shard_map/ppermute | solution.py:60
  243.8 4.2 %collective-permute-done.46.refs_4_ = bf16[1,96,768]{2,1,0:T(8,128)(2,1)S(1)} collective-permute-done((bf16[1,96,768]{2,1,0:T(8,128)(2,1)S(1)}, bf16[1,96,768]{2,1,0:T(8,128)(2,1)S(1)}, u32[]{:S(2)}, u32[]{:S(2)}) %collective-permute-start.46) | collective-permute-done | bytes 147488 | tf_op jit(solution)/shard_map/ppermute | solution.py:60
  248.0 4.6 %collective-permute-done.45.refs_3_ = bf16[1,96,768]{2,1,0:T(8,128)(2,1)S(1)} collective-permute-done((bf16[1,96,768]{2,1,0:T(8,128)(2,1)S(1)}, bf16[1,96,768]{2,1,0:T(8,128)(2,1)S(1)}, u32[]{:S(2)}, u32[]{:S(2)}) %collective-permute-start.45) | collective-permute-done | bytes 147488 | tf_op jit(solution)/shard_map/ppermute | solution.py:60
  253.3 4.9 %shampoo.3 = (f32[96,768]{1,0:T(8,128)}, f32[96,96]{1,0:T(8,128)}, f32[768,768]{1,0:T(8,128)}, f32[96,768]{1,0:T(8,128)}) custom-call(bf16[4,96,768]{2,1,0:T(8,128)(2,1)} %copy-done.1, bf16[4,96,768]{2,1,0:T(8,128)(2,1)} %copy-done.6, bf16[1,96,768]{2,1,0:T(8,128)(2,1)} %copy-done.27, bf16[1,96,768]{2,1,0:T(8,128)(2,1)} %copy-done.26, ...), custom_call_target="tpu_custom_call" | custom-call | flops 905969664 | bytes 7077888 | tf_op jit(solution)/shard_map/shampoo/pallas_call | solution.py:731
  272.7 4.5 %attention_shampoo.1 = (f32[3,96,192]{2,1,0:T(8,128)}, f32[96,96]{1,0:T(8,128)}, f32[576,576]{1,0:T(8,128)}, f32[3,96,192]{2,1,0:T(8,128)}, f32[96,192]{1,0:T(8,...) custom-call(bf16[4,96,768]{2,1,0:T(8,128)(2,1)} %copy-done.2, bf16[4,96,768]{2,1,0:T(8,128)(2,1)} %copy-done.7, ...), custom_call_target="tpu_custom_call" | custom-call | flops 509607936 | bytes 3981312 | tf_op jit(solution)/shard_map/attention_shampoo/pallas_call | solution.py:1094
  (248 shorter events, 91.0 us)
Async XLA Ops:
  38.6 16.5 %collective-permute-start.7 = (bf16[8,96,768]{2,1,0:T(8,128)(2,1)}, bf16[8,96,768]{2,1,0:T(8,128)(2,1)}, u32[]{:S(2)}, u32[]{:S(2)}) collective-permute-start(bf16[8,96,768]{2,1,0:T(8,128)(2,1)} %constant_dynamic-update-slice_fusion.w0), channel_id=1, source_target_pairs={{0,2},{1,5},{2,0},{3,7},{4,6},{5,1},{6,4},{7,3},{8,10},{9,13},{10,... | collective-permute-start | bytes 3538952 | tf_op jit(solution)/shard_map/ppermute | solution.py:60
  42.2 19.7 %collective-permute-start.9 = (bf16[8,96,768]{2,1,0:T(8,128)(2,1)}, bf16[8,96,768]{2,1,0:T(8,128)(2,1)}, u32[]{:S(2)}, u32[]{:S(2)}) collective-permute-start(bf16[8,96,768]{2,1,0:T(8,128)(2,1)} %constant_dynamic-update-slice_fusion.w0), channel_id=1, source_target_pairs={{0,1},{1,0},{2,3},{3,2},{4,5},{5,4},{6,7},{7,6},{8,9},{9,8},{10,11... | collective-permute-start | bytes 3538952 | tf_op jit(solution)/shard_map/ppermute | solution.py:60
  57.5 22.8 %collective-permute-start.13 = (bf16[2,96,768]{2,1,0:T(8,128)(2,1)S(1)}, bf16[2,96,768]{2,1,0:T(8,128)(2,1)S(1)}, u32[]{:S(2)}, u32[]{:S(2)}) collective-permute-start(bf16[2,96,768]{2,1,0:T(8,128)(2,1)S(1)} %pad_maximum_fusion.4), channel_id=1, source_target_pairs={{0,24},{1,25},{2,26},{3,27},{4,28},{5,29},{6,30},{7,31},{8,16},{9,... | collective-permute-start | bytes 884744 | tf_op jit(solution)/shard_map/ppermute | solution.py:60
  59.5 25.9 %collective-permute-start.12 = (bf16[2,96,768]{2,1,0:T(8,128)(2,1)S(1)}, bf16[2,96,768]{2,1,0:T(8,128)(2,1)S(1)}, u32[]{:S(2)}, u32[]{:S(2)}) collective-permute-start(bf16[2,96,768]{2,1,0:T(8,128)(2,1)S(1)} %pad_maximum_fusion.4), channel_id=1, source_target_pairs={{0,16},{1,17},{2,18},{3,19},{4,20},{5,21},{6,22},{7,23},{8,24},{9,... | collective-permute-start | bytes 884744 | tf_op jit(solution)/shard_map/ppermute | solution.py:60
  59.5 25.9 %collective-permute-start.11 = (bf16[2,96,768]{2,1,0:T(8,128)(2,1)S(1)}, bf16[2,96,768]{2,1,0:T(8,128)(2,1)S(1)}, u32[]{:S(2)}, u32[]{:S(2)}) collective-permute-start(bf16[2,96,768]{2,1,0:T(8,128)(2,1)S(1)} %pad_maximum_fusion.4), channel_id=1, source_target_pairs={{0,8},{1,9},{2,10},{3,11},{4,12},{5,13},{6,14},{7,15},{8,0},{9,1},... | collective-permute-start | bytes 884744 | tf_op jit(solution)/shard_map/ppermute | solution.py:60
  61.9 30.5 %collective-permute-start.15 = (bf16[8,96,768]{2,1,0:T(8,128)(2,1)S(1)}, bf16[8,96,768]{2,1,0:T(8,128)(2,1)}, u32[]{:S(2)}, u32[]{:S(2)}) collective-permute-start(bf16[8,96,768]{2,1,0:T(8,128)(2,1)S(1)} %pad_maximum_fusion.w0), channel_id=1, source_target_pairs={{0,1},{1,0},{2,3},{3,2},{4,5},{5,4},{6,7},{7,6},{8,9},{9,8},{10,11... | collective-permute-start | bytes 3538952 | tf_op jit(solution)/shard_map/ppermute | solution.py:60
  62.0 23.4 %collective-permute-start.14 = (bf16[8,96,768]{2,1,0:T(8,128)(2,1)S(1)}, bf16[8,96,768]{2,1,0:T(8,128)(2,1)}, u32[]{:S(2)}, u32[]{:S(2)}) collective-permute-start(bf16[8,96,768]{2,1,0:T(8,128)(2,1)S(1)} %pad_maximum_fusion.w0), channel_id=1, source_target_pairs={{0,2},{1,5},{2,0},{3,7},{4,6},{5,1},{6,4},{7,3},{8,10},{9,13},{10,... | collective-permute-start | bytes 3538952 | tf_op jit(solution)/shard_map/ppermute | solution.py:60
  88.0 23.6 %collective-permute-start.19 = (bf16[2,64,768]{2,1,0:T(8,128)(2,1)S(1)}, bf16[2,64,768]{2,1,0:T(8,128)(2,1)S(1)}, u32[]{:S(2)}, u32[]{:S(2)}) collective-permute-start(bf16[2,64,768]{2,1,0:T(8,128)(2,1)S(1)} %pad_maximum_fusion.5), channel_id=1, source_target_pairs={{0,24},{1,25},{2,26},{3,27},{4,28},{5,29},{6,30},{7,31},{8,16},{9,... | collective-permute-start | bytes 589832 | tf_op jit(solution)/shard_map/ppermute | solution.py:60
  90.5 21.0 %collective-permute-start.18 = (bf16[2,64,768]{2,1,0:T(8,128)(2,1)S(1)}, bf16[2,64,768]{2,1,0:T(8,128)(2,1)S(1)}, u32[]{:S(2)}, u32[]{:S(2)}) collective-permute-start(bf16[2,64,768]{2,1,0:T(8,128)(2,1)S(1)} %pad_maximum_fusion.5), channel_id=1, source_target_pairs={{0,16},{1,17},{2,18},{3,19},{4,20},{5,21},{6,22},{7,23},{8,24},{9,... | collective-permute-start | bytes 589832 | tf_op jit(solution)/shard_map/ppermute | solution.py:60
  90.5 21.0 %collective-permute-start.17 = (bf16[2,64,768]{2,1,0:T(8,128)(2,1)S(1)}, bf16[2,64,768]{2,1,0:T(8,128)(2,1)S(1)}, u32[]{:S(2)}, u32[]{:S(2)}) collective-permute-start(bf16[2,64,768]{2,1,0:T(8,128)(2,1)S(1)} %pad_maximum_fusion.5), channel_id=1, source_target_pairs={{0,8},{1,9},{2,10},{3,11},{4,12},{5,13},{6,14},{7,15},{8,0},{9,1},... | collective-permute-start | bytes 589832 | tf_op jit(solution)/shard_map/ppermute | solution.py:60
  92.5 21.0 %collective-permute-start.21 = (bf16[8,96,768]{2,1,0:T(8,128)(2,1)}, bf16[8,96,768]{2,1,0:T(8,128)(2,1)S(1)}, u32[]{:S(2)}, u32[]{:S(2)}) collective-permute-start(bf16[8,96,768]{2,1,0:T(8,128)(2,1)} %copy-done.28), channel_id=1, source_target_pairs={{0,1},{1,0},{2,3},{3,2},{4,5},{5,4},{6,7},{7,6},{8,9},{9,8},{10,11... | collective-permute-start | bytes 3538952 | tf_op jit(solution)/shard_map/ppermute | solution.py:60
  92.5 19.1 %collective-permute-start.20 = (bf16[8,96,768]{2,1,0:T(8,128)(2,1)}, bf16[8,96,768]{2,1,0:T(8,128)(2,1)S(1)}, u32[]{:S(2)}, u32[]{:S(2)}) collective-permute-start(bf16[8,96,768]{2,1,0:T(8,128)(2,1)} %copy-done.28), channel_id=1, source_target_pairs={{0,2},{1,5},{2,0},{3,7},{4,6},{5,1},{6,4},{7,3},{8,10},{9,13},{10,... | collective-permute-start | bytes 3538952 | tf_op jit(solution)/shard_map/ppermute | solution.py:60
  111.7 16.6 %collective-permute-start.24 = (bf16[8,64,768]{2,1,0:T(8,128)(2,1)S(1)}, bf16[8,64,768]{2,1,0:T(8,128)(2,1)S(1)}, u32[]{:S(2)}, u32[]{:S(2)}) collective-permute-start(bf16[8,64,768]{2,1,0:T(8,128)(2,1)S(1)} %constant_dynamic-update-slice_fusion.11), channel_id=1, source_target_pairs={{0,1},{1,0},{2,3},{3,2},{4,5},{5,4},{6,7},{7,6},{8,9},{9,8},{10,11... | collective-permute-start | bytes 2359304 | tf_op jit(solution)/shard_map/ppermute | solution.py:60
  140.1 22.6 %collective-permute-start.26 = (bf16[8,96,768]{2,1,0:T(8,128)(2,1)}, bf16[8,96,768]{2,1,0:T(8,128)(2,1)S(1)}, u32[]{:S(2)}, u32[]{:S(2)}) collective-permute-start(bf16[8,96,768]{2,1,0:T(8,128)(2,1)} %get-tuple-element.174), channel_id=1, source_target_pairs={{0,1},{1,0},{2,3},{3,2},{4,5},{5,4},{6,7},{7,6},{8,9},{9,8},{10,11... | collective-permute-start | bytes 3538952 | tf_op jit(solution)/shard_map/ppermute | solution.py:60
  146.4 16.3 %collective-permute-start.28 = (bf16[8,96,768]{2,1,0:T(8,128)(2,1)S(1)}, bf16[8,96,768]{2,1,0:T(8,128)(2,1)S(1)}, u32[]{:S(2)}, u32[]{:S(2)}) collective-permute-start(bf16[8,96,768]{2,1,0:T(8,128)(2,1)S(1)} %add_convert_fusion.2), channel_id=1, source_target_pairs={{0,2},{1,5},{2,0},{3,7},{4,6},{5,1},{6,4},{7,3},{8,10},{9,13},{10,... | collective-permute-start | bytes 3538952 | tf_op jit(solution)/shard_map/ppermute | solution.py:60
  175.8 29.1 %collective-permute-start.34 = (bf16[1,96,768]{2,1,0:T(8,128)(2,1)S(1)}, bf16[1,96,768]{2,1,0:T(8,128)(2,1)S(1)}, u32[]{:S(2)}, u32[]{:S(2)}) collective-permute-start(bf16[1,96,768]{2,1,0:T(8,128)(2,1)S(1)} %get-tuple-element.267), channel_id=1, source_target_pairs={{0,16},{1,17},{2,18},{3,19},{4,20},{5,21},{6,22},{7,23},{8,24},{9,... | collective-permute-start | bytes 442376 | tf_op jit(solution)/shard_map/ppermute | solution.py:60
  176.8 28.1 %collective-permute-start.33 = (bf16[1,96,768]{2,1,0:T(8,128)(2,1)S(1)}, bf16[1,96,768]{2,1,0:T(8,128)(2,1)S(1)}, u32[]{:S(2)}, u32[]{:S(2)}) collective-permute-start(bf16[1,96,768]{2,1,0:T(8,128)(2,1)S(1)} %get-tuple-element.268), channel_id=1, source_target_pairs={{0,8},{1,9},{2,10},{3,11},{4,12},{5,13},{6,14},{7,15},{8,0},{9,1},... | collective-permute-start | bytes 442376 | tf_op jit(solution)/shard_map/ppermute | solution.py:60
  178.8 26.0 %collective-permute-start.35 = (bf16[1,96,768]{2,1,0:T(8,128)(2,1)S(1)}, bf16[1,96,768]{2,1,0:T(8,128)(2,1)S(1)}, u32[]{:S(2)}, u32[]{:S(2)}) collective-permute-start(bf16[1,96,768]{2,1,0:T(8,128)(2,1)S(1)} %get-tuple-element.269), channel_id=1, source_target_pairs={{0,24},{1,25},{2,26},{3,27},{4,28},{5,29},{6,30},{7,31},{8,16},{9,... | collective-permute-start | bytes 442376 | tf_op jit(solution)/shard_map/ppermute | solution.py:60
  180.2 22.6 %collective-permute-start.31 = (bf16[8,96,768]{2,1,0:T(8,128)(2,1)}, bf16[8,96,768]{2,1,0:T(8,128)(2,1)S(1)}, u32[]{:S(2)}, u32[]{:S(2)}) collective-permute-start(bf16[8,96,768]{2,1,0:T(8,128)(2,1)} %get-tuple-element.199), channel_id=1, source_target_pairs={{0,1},{1,0},{2,3},{3,2},{4,5},{5,4},{6,7},{7,6},{8,9},{9,8},{10,11... | collective-permute-start | bytes 3538952 | tf_op jit(solution)/shard_map/ppermute | solution.py:60
  180.5 21.8 %collective-permute-start.32 = (bf16[8,96,768]{2,1,0:T(8,128)(2,1)S(1)}, bf16[8,96,768]{2,1,0:T(8,128)(2,1)S(1)}, u32[]{:S(2)}, u32[]{:S(2)}) collective-permute-start(bf16[8,96,768]{2,1,0:T(8,128)(2,1)S(1)} %add_convert_fusion.1), channel_id=1, source_target_pairs={{0,2},{1,5},{2,0},{3,7},{4,6},{5,1},{6,4},{7,3},{8,10},{9,13},{10,... | collective-permute-start | bytes 3538952 | tf_op jit(solution)/shard_map/ppermute | solution.py:60
  202.3 14.9 %collective-permute-start.37 = (f32[4,768]{1,0:T(4,128)S(1)}, f32[4,768]{1,0:T(4,128)S(1)}, u32[]{:S(2)}, u32[]{:S(2)}) collective-permute-start(f32[4,768]{1,0:T(4,128)S(1)} %pad_maximum_fusion.6), channel_id=1, source_target_pairs={{0,1},{1,0},{2,3},{3,2},{4,5},{5,4},{6,7},{7,6},{8,9},{9,8},{10,11... | collective-permute-start | bytes 36872 | tf_op jit(solution)/shard_map/ppermute | solution.py:60
  221.9 16.3 %collective-permute-start.40 = (bf16[8,96,768]{2,1,0:T(8,128)(2,1)S(1)}, bf16[8,96,768]{2,1,0:T(8,128)(2,1)S(1)}, u32[]{:S(2)}, u32[]{:S(2)}) collective-permute-start(bf16[8,96,768]{2,1,0:T(8,128)(2,1)S(1)} %add_convert_fusion), channel_id=1, source_target_pairs={{0,2},{1,5},{2,0},{3,7},{4,6},{5,1},{6,4},{7,3},{8,10},{9,13},{10,... | collective-permute-start | bytes 3538952 | tf_op jit(solution)/shard_map/ppermute | solution.py:60
  222.3 15.9 %collective-permute-start.38 = (bf16[8,96,768]{2,1,0:T(8,128)(2,1)S(1)}, bf16[8,96,768]{2,1,0:T(8,128)(2,1)S(1)}, u32[]{:S(2)}, u32[]{:S(2)}) collective-permute-start(bf16[8,96,768]{2,1,0:T(8,128)(2,1)S(1)} %copy-done.36), channel_id=1, source_target_pairs={{0,1},{1,0},{2,3},{3,2},{4,5},{5,4},{6,7},{7,6},{8,9},{9,8},{10,11... | collective-permute-start | bytes 3538952 | tf_op jit(solution)/shard_map/ppermute | solution.py:60
  238.7 19.5 %collective-permute-start.43 = (bf16[4,96,768]{2,1,0:T(8,128)(2,1)S(1)}, bf16[4,96,768]{2,1,0:T(8,128)(2,1)S(1)}, u32[]{:S(2)}, u32[]{:S(2)}) collective-permute-start(bf16[4,96,768]{2,1,0:T(8,128)(2,1)S(1)} %get-tuple-element.257), channel_id=1, source_target_pairs={{0,4},{1,3},{2,6},{3,1},{4,0},{5,7},{6,2},{7,5},{8,12},{9,11},{10,... | collective-permute-start | bytes 1769480 | tf_op jit(solution)/shard_map/ppermute | solution.py:60
  (69 other events, 608.0 us)

commit v3 on v2

--- a/solution.py
+++ b/solution.py
@@ -158,28 +158,33 @@
     )
 
 
-def load_weights(order, parts, weights, sems):
+def load_weights(places, parts, weights, sems, first=0):
     size, rows, _ = parts[0].shape
-    groups = weights.shape[0]
+    groups, _, cols = weights.shape
+    me = places[2 * size * len(parts)]
 
     def body(q, carry):
         for i, part in enumerate(parts):
-            index = order[i * size + q]
+            index = places[i * size + q] ^ me
             group = index % groups
             place = pl.multiple_of((index // groups) * rows, 16)
             pltpu.make_async_copy(
-                part.at[q], weights.at[group, pl.ds(place, rows), :], sems.at[group]
+                part.at[q, :, pl.ds(first, cols)],
+                weights.at[group, pl.ds(place, rows), :],
+                sems.at[group],
             ).start()
         return carry
 
     lax.fori_loop(0, size, body, 0)
 
 
-def store_blocks(inverse, source, group, groups, parts, sem):
+def store_blocks(places, source, group, groups, parts, sem):
     size, rows, _ = parts[0].shape
+    count = size * len(parts)
+    me = places[2 * count]
 
     def body(p, carry):
-        position = inverse[p * groups + group]
+        position = places[count + ((p * groups + group) ^ me)]
         block = source.at[pl.ds(pl.multiple_of(p * rows, 16), rows), :]
         for i, part in enumerate(parts):
 
@@ -258,7 +263,21 @@
     return jnp.concatenate([values[:, :LANES], values[:, LANES:]], axis=0)
 
 
-def first_norm(x_ref, norm_ref, h1_ref):
+def spread(values, seq_len):
+    seqs, width = values.shape
+    return jnp.broadcast_to(values[:, None, :], (seqs, seq_len, width)).reshape(
+        seqs * seq_len, width
+    )
+
+
+def live_column(counts, seq_len):
+    wide = spread(counts, seq_len)
+    slot = lax.broadcasted_iota(jnp.int32, wide.shape, 0) % seq_len
+    return jnp.where(slot.astype(F32) < wide, 1.0, 0.0)[:, 0:1]
+
+
+def first_norm(x_ref, norm_ref, *rest):
+    h1_ref = rest[-1]
     n1, _ = normalize(x_ref[...].astype(F32))
     h1_ref[...] = (n1 * norm_ref[0:1, :] + norm_ref[1:2, :]).astype(BF16)
 
@@ -338,43 +357,40 @@
 
 
 def up_forward(
-    order, h2_ref, live_ref, w0, w1, w2, w3,
+    places, h2_ref, count_ref, w0, w1, w2, w3,
     hid_ref, slope_ref, pooled_ref,
     weights, sems, *, seq_len,
 ):
-    groups, _, width = weights.shape
-    first = pl.program_id(0) == 0
-
-    @pl.when(first)
+    groups, _, wide = weights.shape
+
+    @pl.when(pl.program_id(0) == 0)
     def _():
-        load_weights(order, (w0, w1, w2, w3), weights, sems)
-        for group in range(weights.shape[0]):
+        load_weights(places, (w0, w1, w2, w3), weights, sems)
+        for group in range(groups):
             wait_weights(weights, sems, group)
 
     h2 = h2_ref[...]
     rows = h2.shape[0]
-    live = live_ref[:, 0:1]
+    counts = count_ref[...]
+    live = live_column(counts, seq_len)
     seqs = rows // seq_len
-    member = (
-        lax.broadcasted_iota(jnp.int32, (seqs, rows), 1) // seq_len
-        == lax.broadcasted_iota(jnp.int32, (seqs, rows), 0)
-    )
-    pool = jnp.where(member, 1.0, 0.0).astype(BF16)
+    slot = lax.broadcasted_iota(jnp.int32, (seqs, rows), 1)
+    member = slot // seq_len == lax.broadcasted_iota(jnp.int32, (seqs, rows), 0)
+    within = (slot % seq_len).astype(F32) < counts[:, 0:1]
+    pool = jnp.where(jnp.logical_and(member, within), 1.0, 0.0).astype(BF16)
     for group in range(groups):
-
-
-        cols = slice(group * width, (group + 1) * width)
+        cols = slice(group * wide, (group + 1) * wide)
         up = dot(h2, weights[group], 1, 0)
         gate = 0.5 + 0.5 * lax.erf(up * (0.5**0.5))
         hid = (up * gate).astype(BF16)
         hid_ref[:, cols] = hid
         bell = jnp.exp(up * up * -0.5) * (1.0 / math.sqrt(2.0 * math.pi))
         slope_ref[:, cols] = ((gate + up * bell) * live).astype(BF16)
-        pooled_ref[:, cols] = dot(pool, hid * live.astype(BF16), 1, 0).astype(BF16)
+        pooled_ref[:, cols] = dot(pool, hid, 1, 0).astype(BF16)
 
 
 def down_forward(
-    order, hid_ref, mid_ref, live_ref, w0, w1, w2, w3,
+    order, hid_ref, mid_ref, count_ref, w0, w1, w2, w3,
     out_ref, pooled_ref, weights, sems, *, seq_len,
 ):
     groups, _, width = weights.shape
@@ -394,15 +410,20 @@
             hid_ref[:, group * width : (group + 1) * width], weights[group], 1, 1
         )
     out_ref[...] = total.astype(BF16)
-    live = live_ref[:, 0:1]
     rows, features = total.shape
+    counts = count_ref[...]
+    live = live_column(counts, seq_len)
     seqs = rows // seq_len
     sums = jnp.sum((total * live).reshape(seqs, seq_len, features), axis=1)
-    counts = jnp.sum(jnp.broadcast_to(live, (rows, LANES)).reshape(seqs, seq_len, LANES), axis=1)
     pooled_ref[...] = sums / counts[:, 0:1]
 
 
-def contrast(pooled_ref, count_ref, m0, m1, m2, m3, loss_ref, grad_ref, low_ref, *, micros):
+def loss_backward(
+    places, pooled_ref, count_ref, m0, m1, m2, m3, hid_ref,
+    loss_ref, grad_ref, low_ref, g0, g1, g2, g3,
+    slots, slot_sems, *, micros, groups,
+):
+    ff = slots.shape[2]
     pooled = pooled_ref[...]
     seqs, width = pooled.shape
     each = seqs // micros
@@ -439,7 +460,20 @@
     along = jnp.mean(grad_text * pooled, axis=-1, keepdims=True)
     grad = (r * grad_text - (r * r * r) * pooled * along) / count_ref[:, 0:1]
     grad_ref[...] = grad
-    low_ref[...] = grad.astype(BF16)
+    low = grad.astype(BF16)
+    low_ref[...] = low
+    turned = low.T
+    for group in range(groups):
+        cols = slice(group * ff, (group + 1) * ff)
+        if group >= 2:
+            drain(slots, slot_sems, group % 2)
+        slots[group % 2] = dot(turned, hid_ref[:, cols], 1, 0).astype(BF16)
+        store_blocks(
+            places, slots.at[group % 2], group, groups, (g0, g1, g2, g3),
+            slot_sems.at[group % 2],
+        )
+    for which in range(min(groups, 2)):
+        drain(slots, slot_sems, which)
 
 
 def drain(slots, sems, which):
@@ -456,49 +490,30 @@
             drain(slots, sems, 1 - slot)
 
 
-def weight_gradient(
-    inverse, left_ref, right_ref, g0, g1, g2, g3, turned, slots, sems
-):
+def weight_gradient(places, *refs):
+    pairs = (len(refs) - 6) // 3
+    lefts, rights = refs[: 2 * pairs : 2], refs[1 : 2 * pairs : 2]
+    parts, turned = refs[2 * pairs : 2 * pairs + 4], refs[2 * pairs + 4 : -2]
+    slots, sems = refs[-2:]
     group = pl.program_id(0)
     groups = pl.num_programs(0)
     slot = group % 2
 
     @pl.when(group == 0)
     def _():
-        turned[...] = left_ref[...].T
+        for left, across in zip(lefts, turned):
+            across[...] = left[...].T
 
     @pl.when(group >= 2)
     def _():
         drain(slots, sems, slot)
 
-    slots[slot] = dot(turned[...], right_ref[...], 1, 0).astype(BF16)
-    store_blocks(inverse, slots.at[slot], group, groups, (g0, g1, g2, g3), sems.at[slot])
-    finish_blocks(slots, sems, group, groups, slot)
-
-
-def attention_gradient(
-    inverse, h1_ref, proj_ref, mid_ref, heads_ref, g0, g1, g2, g3,
-    turned, turned_mid, slots, sems,
-):
-    group = pl.program_id(0)
-    groups = pl.num_programs(0)
-    slot = group % 2
-
-    @pl.when(group == 0)
-    def _():
-        turned[...] = h1_ref[...].T
-        turned_mid[...] = mid_ref[...].T
-
-    @pl.when(group >= 2)
-    def _():
-        drain(slots, sems, slot)
-
-    slots[slot, :, : 4 * LANES] = dot(turned[...], proj_ref[:, : 4 * LANES], 1, 0).astype(BF16)
-    tail = dot(turned_mid[...], heads_ref[...], 1, 0)
-    keys = dot(turned[...], proj_ref[:, 4 * LANES :], 1, 0)
-    slots[slot, :, 4 * LANES : 5 * LANES] = (keys + tail[:, :LANES]).astype(BF16)
-    slots[slot, :, 5 * LANES :] = tail[:, LANES:].astype(BF16)
-    store_blocks(inverse, slots.at[slot], group, groups, (g0, g1, g2, g3), sems.at[slot])
+    first = 0
+    for across, right in zip(turned, rights):
+        last = first + right.shape[1]
+        slots[slot, :, first:last] = dot(across[...], right[...], 1, 0).astype(BF16)
+        first = last
+    store_blocks(places, slots.at[slot], group, groups, parts, sems.at[slot])
     finish_blocks(slots, sems, group, groups, slot)
 
 
@@ -526,7 +541,7 @@
 
 
 def mlp_backward(
-    order, grad_ref, by_seq_ref, slope_ref, live_ref, mid_ref, norm_ref,
+    order, grad_ref, by_seq_ref, slope_ref, count_ref, mid_ref, norm_ref,
     w0, w1, w2, w3,
     dup_ref, dmid_ref, dmid_low_ref, sums_ref,
     weights, sems, *, seq_len,
@@ -543,23 +558,18 @@
     grad = grad_ref[...]
     mid = mid_ref[...]
     rows, features = mid.shape
-    seqs = rows // seq_len
-
-    def spread(values):
-        return jnp.broadcast_to(
-            values[:, None, :], (seqs, seq_len, values.shape[1])
-        ).reshape(rows, values.shape[1])
 
     total = jnp.zeros((rows, features), F32)
     for group in range(groups):
 
 
         cols = slice(group * width, (group + 1) * width)
-        dup = (slope_ref[:, cols].astype(F32) * spread(by_seq_ref[:, cols])).astype(BF16)
+        dup = (slope_ref[:, cols].astype(F32) * spread(by_seq_ref[:, cols], seq_len)).astype(BF16)
         dup_ref[:, cols] = dup
         total = total + dot(dup, weights[group], 1, 1)
     moved, gain_grad, shift_grad = norm_back(total, norm_ref[2:3, :], mid)
-    dmid = spread(grad) * live_ref[:, 0:1] + moved
+    live = live_column(count_ref[...], seq_len)
+    dmid = spread(grad, seq_len) * live + moved
     dmid_ref[...] = dmid
     dmid_low_ref[...] = dmid.astype(BF16)
     sums_ref[0:1, :] += gain_grad
@@ -567,17 +577,15 @@
 
 
 def attention_backward(
-    order, x_ref, live_ref, norm_ref, proj_ref, lse_ref, dmid_ref, dmid_low_ref,
-    w0, w1, w2, w3, *rest, seq_len,
+    places, x_ref, live_ref, norm_ref, proj_ref, lse_ref, dmid_ref, dmid_low_ref,
+    w0, w1, w2, w3, dproj_ref, dx_ref, sums_ref, weights, sems, *, seq_len,
 ):
-    dproj_ref, dx_ref, sums_ref, weights, sems = rest[-5:]
     groups = weights.shape[0]
-    first = pl.program_id(0) == 0
-
-    @pl.when(first)
+
+    @pl.when(pl.program_id(0) == 0)
     def _():
-        load_weights(order, (w0, w1, w2, w3), weights, sems)
-        for group in range(weights.shape[0]):
+        load_weights(places, (w0, w1, w2, w3), weights, sems)
+        for group in range(groups):
             wait_weights(weights, sems, group)
         sums_ref[...] = jnp.zeros_like(sums_ref)
 
@@ -592,7 +600,8 @@
     count = rows // LANES
     duos = groups // 2
     dheads = [
-        dot(dmid_low, weights[group, :, 4 * LANES :], 1, 0).astype(BF16) for group in range(groups)
+        dot(dmid_low, weights[group, :, 4 * LANES :], 1, 0).astype(BF16)
+        for group in range(groups)
     ]
     chains = []
     for duo in range(duos):
@@ -676,7 +685,7 @@
 
 def shampoo_kernel(*refs):
     terms = refs[:-9]
-    stats, master_ref = refs[-9:-5], refs[-5]
+    master_ref, *stats = refs[-9:-4]
     grad_ref, left_new_ref, right_new_ref, new_ref = refs[-4:]
     grad = sum(term[0].astype(F32) for term in terms)
     grad_ref[...] = grad
@@ -684,21 +693,32 @@
     new_ref[...] = master_ref[...] - step
 
 
+def up_shampoo(*refs):
+    terms = refs[:-18]
+    up_ref, out_ref, *stats = refs[-18:-8]
+    up_grad, up_left, up_right, up_new, out_grad, out_left, out_right, out_new = refs[-8:]
+    packed = sum(term[0].astype(F32) for term in terms)
+    wide = up_ref.shape[1]
+    up, out = packed[:, :wide], unpack_out(packed[:, wide:])
+    up_grad[...] = up
+    up_left[...], up_right[...], step = renew(up, *(ref[...] for ref in stats[:4]))
+    up_new[...] = up_ref[...] - step
+    out_grad[...] = out
+    out_left[...], out_right[...], step = renew(out, *(ref[...] for ref in stats[4:]))
+    out_new[...] = out_ref[...] - step
+
+
 def attention_shampoo(*refs):
-    terms = refs[:-18]
-    qkv_ref, out_ref, *stats = refs[-18:-8]
-    qkv_grad, qkv_left, qkv_right, qkv_new, out_grad, out_left, out_right, out_new = refs[-8:]
-    packed = sum(term[0].astype(F32) for term in terms)
-    qkv, out = unpack_attention(packed)
-    out_grad[...] = out
-    qkv_left[...], qkv_right[...], step = renew(qkv, *(ref[...] for ref in stats[:4]))
+    terms = refs[:-9]
+    qkv_ref, *stats = refs[-9:-4]
+    qkv_grad, qkv_left, qkv_right, qkv_new = refs[-4:]
+    qkv = unpack_qkv(sum(term[0].astype(F32) for term in terms))
+    qkv_left[...], qkv_right[...], step = renew(qkv, *(ref[...] for ref in stats))
     width = qkv_ref.shape[2]
     for i in range(3):
         cols = slice(i * width, (i + 1) * width)
         qkv_grad[i] = qkv[:, cols]
         qkv_new[i] = qkv_ref[i] - step[:, cols]
-    out_left[...], out_right[...], step = renew(out, *(ref[...] for ref in stats[4:]))
-    out_new[...] = out_ref[...] - step
 
 
 ANY = pl.BlockSpec(memory_space=pl.ANY)
@@ -726,39 +746,48 @@
     return jax.ShapeDtypeStruct(dims, dtype)
 
 
-def shampoo(terms, left_stat, right_stat, left_root, right_root, master):
-    rows, cols = master.shape
-    grad, left_new, right_new, new = pl.pallas_call(
-        shampoo_kernel,
+def stat_shapes(rows, cols):
+    return shape_of(rows, rows, dtype=F32), shape_of(cols, cols, dtype=F32)
+
+
+def shampoo(kernel, terms, masters, shapes, stats):
+    rows, cols = terms[0].shape[1:]
+    out_shape = []
+    for master, (left, right) in zip(masters, shapes):
+        value = shape_of(*master.shape, dtype=F32)
+        out_shape += [value, *stat_shapes(left, right), value]
+    return pl.pallas_call(
+        kernel,
         grid=(1,),
-        out_shape=(
-            shape_of(rows, cols, dtype=F32),
-            shape_of(rows, rows, dtype=F32),
-            shape_of(cols, cols, dtype=F32),
-            shape_of(rows, cols, dtype=F32),
-        ),
-        in_specs=[pl.BlockSpec((1, rows, cols), lambda i: (0, 0, 0))] * len(terms) + [WHOLE] * 5,
-        out_specs=(WHOLE,) * 4,
+        out_shape=tuple(out_shape),
+        in_specs=[pl.BlockSpec((1, rows, cols), lambda i: (0, 0, 0))] * len(terms)
+        + [WHOLE] * (len(masters) + len(stats)),
+        out_specs=(WHOLE,) * len(out_shape),
         compiler_params=params(),
         cost_estimate=cost(4 * rows * cols * cols, 12 * cols * cols),
-        name="shampoo",
-    )(*terms, left_stat[0, 0], right_stat[0, 0], left_root[0, 0], right_root[0, 0], master)
-    return grad, left_new[None, None], right_new[None, None], new
-
-
-def pack_attention(qkv, out):
+        name=kernel.__name__,
+    )(*terms, *masters, *(stat[0, 0] for stat in stats))
+
+
+def pack_qkv(qkv):
     q, k, v = (qkv[:, i] for i in range(3))
     a, b = 2 * HD, 3 * HD
-    return jnp.concatenate(
-        [q[:, :a], k[:, :a], v[:, :a], q[:, a:b], v[:, a:b], k[:, a:b], out[:, a:b], out[:, :a]],
-        axis=1,
-    )
-
-
-def unpack_attention(packed):
-    c = [packed[:, i * HD : (i + 1) * HD] for i in range(12)]
-    qkv = jnp.concatenate([c[0], c[1], c[6], c[2], c[3], c[8], c[4], c[5], c[7]], axis=1)
-    return qkv, jnp.concatenate([c[10], c[11], c[9]], axis=1)
+    third = [q[:, a:b], v[:, a:b], k[:, a:b], jnp.zeros_like(k[:, a:b])]
+    return jnp.concatenate([q[:, :a], k[:, :a], v[:, :a]] + third, axis=1)
+
+
+def pack_attention(qkv, out):
+    packed = pack_qkv(qkv)
+    return jnp.concatenate([packed[:, : 9 * HD], out[:, 2 * HD :], out[:, : 2 * HD]], axis=1)
+
+
+def unpack_qkv(packed):
+    c = [packed[:, i * HD : (i + 1) * HD] for i in range(10)]
+    return jnp.concatenate([c[0], c[1], c[6], c[2], c[3], c[8], c[4], c[5], c[7]], axis=1)
+
+
+def unpack_out(packed):
+    return jnp.concatenate([packed[:, 2 * HD :], packed[:, HD : 2 * HD]], axis=1)
 
 
 def per_device(
@@ -782,27 +811,34 @@
     direct = owned % 16 == 0
 
     def places(near_first):
-        table = source_table(count, near_first)
-        return (
-            jnp.asarray(table, jnp.int32)[me],
-            jnp.asarray(np.argsort(table, axis=1), jnp.int32)[me],
-        )
-
-    order, inverse = places(False)
-    near_order, near_inverse = places(True)
-
-    def weights_of(gather, inverse):
+        masks = source_table(count, near_first)[:2] ^ np.arange(2)[:, None]
+        masks = np.concatenate([masks, np.argsort(masks, axis=1)], axis=1)
+        odd = me % 2 == 1
+        mine = jnp.where(odd, jnp.asarray(masks[1], jnp.int32), jnp.asarray(masks[0], jnp.int32))
+        return jnp.concatenate([mine, me.astype(jnp.int32)[None]])
+
+    far_places, near_places = places(False), places(True)
+
+    def order_of(places):
+        return places[:count] ^ me
+
+    def inverse_of(places):
+        return places[count : 2 * count][jnp.arange(count) ^ me]
+
+    def weights_of(gather, places):
         quarters = gather.quarters()
         if direct:
             return quarters
-        whole = jnp.concatenate(quarters, axis=0)[inverse]
+        whole = jnp.concatenate(quarters, axis=0)[inverse_of(places)]
         whole = whole.reshape(dp_count, groups, owned, whole.shape[-1])
         whole = whole.transpose(1, 0, 2, 3).reshape(groups, width, whole.shape[-1])
         return tuple(jnp.split(whole, 4, axis=0))
 
-    kernel_order = order if direct else jnp.arange(groups, dtype=jnp.int32)
-    kernel_near_order = near_order if direct else kernel_order
-    kernel_inverse = inverse if direct else jnp.arange(groups, dtype=jnp.int32)
+    if direct:
+        kernel_far, kernel_near = far_places, near_places
+    else:
+        plain = jnp.arange(groups, dtype=jnp.int32)
+        kernel_far = kernel_near = jnp.concatenate([plain, plain, jnp.zeros(1, jnp.int32)])
     block_rows = owned if direct else width
     quarter = (count if direct else groups) // 4
 
@@ -810,28 +846,32 @@
         if not direct:
             whole = jnp.concatenate(quarters, axis=0)
             whole = whole.reshape(groups, dp_count, owned, whole.shape[2])
-            whole = whole.transpose(1, 0, 2, 3).reshape(count, owned, whole.shape[3])[order]
+            whole = whole.transpose(1, 0, 2, 3).reshape(count, owned, whole.shape[3])[order_of(far_places)]
             quarters = jnp.split(whole, 4, axis=0)
         return Sum(quarters, count)
 
-    own_blocks = [w_up.astype(BF16), w_down.astype(BF16), image_embed.reshape(all_seqs, width)]
-    gather_attention = Gather(pack_attention(w_qkv.astype(BF16), w_out.astype(BF16)), count)
-    gather_up, gather_down, gather_images = (Gather(block, count) for block in own_blocks)
+    def width_of(array):
+        return array.shape[1]
+
+    own_attention = pack_attention(w_qkv.astype(BF16), w_out.astype(BF16))
+    own_up, own_down = w_up.astype(BF16), w_down.astype(BF16)
+    own_images = image_embed.reshape(all_seqs, width)
+    gather_attention, gather_up, gather_down, gather_images = (
+        Gather(block, count) for block in (own_attention, own_up, own_down, own_images)
+    )
     gather_attention.far()
-    from_near = swap(jnp.concatenate(own_blocks, axis=0), near_steps(count)[0])
-    from_near = jnp.split(from_near, (owned, 2 * owned), axis=0)
-    for gather, received in zip((gather_up, gather_down, gather_images), from_near):
-        gather.received = [received[None]]
-    gather_up.keep()
-    gather_attention.keep(gather_up.held)
+    later = gather_down, gather_images
+    for gather in later:
+        gather.first()
+        gather.keep()
+    gather_attention.keep(*(gather.held for gather in later))
     gather_attention.first()
     gather_up.far(gather_attention.held)
 
     x = block_in.reshape(rows, width)
     norms = norm_params.T
     lengths = seq_lengths.reshape(all_seqs)
-    live = (jnp.arange(seq_len)[None, :] < lengths[:, None]).astype(F32).reshape(rows)
-    live_cols = jnp.broadcast_to(live[:, None], (rows, LANES))
+    live = (jnp.arange(seq_len)[None, :] < lengths[:, None]).astype(F32)
     tile_seqs = LANES // seq_len
     live_keys = live.reshape(rows // LANES, tile_seqs, 1, seq_len)
     live_keys = jnp.broadcast_to(
@@ -840,16 +880,19 @@
     live_keys = jnp.concatenate([live_keys, live_keys], axis=2)
     counts = jnp.broadcast_to(lengths.astype(F32)[:, None], (all_seqs, LANES))
 
-    live_spec = rows_of(LANES)
+    count_spec = rows_of(LANES, seq_tile)
     keys_spec = pl.BlockSpec((TILE // LANES, seq_len, 2 * LANES), lambda i: (i, 0, 0))
     lse_spec = pl.BlockSpec((TILE // LANES, 8, 2 * LANES), lambda i: (i, 0, 0))
     norm_spec = fixed((4, width))
+    all_ff, all_heads = groups * ff, groups * 2 * LANES
+    packed = width_of(own_attention)
 
     def weight_scratch(cols):
         return [pltpu.VMEM((groups, width, cols), BF16), pltpu.SemaphoreType.DMA((groups,))]
 
-    packed = 6 * LANES
-    (x_ready,) = after([x], gather_attention.held)
+    x_ready, live_keys, counts, kernel_far, kernel_near = after(
+        [x, live_keys, counts, kernel_far, kernel_near], gather_attention.held
+    )
     h1 = pl.pallas_call(
         first_norm,
         grid=(tiles,),
@@ -860,23 +903,20 @@
         cost_estimate=cost(1, 100e6),
         name="first_norm",
     )(x_ready, norms)
-
+    h1, live_keys, counts, kernel_far, kernel_near = join(
+        h1, live_keys, counts, kernel_far, kernel_near
+    )
     gather_attention.keep(h1)
-    gather_attention.held, *gather_up.received = join(
-        gather_attention.held, *gather_up.received[:-1]
-    ) + (gather_up.received[-1],)
     gather_attention.second()
     gather_attention.third()
-    gather_attention.across, *gather_up.received = join(
-        gather_attention.across, *gather_up.received
-    )
-    gather_attention.last()
-    gather_up.keep()
-    gather_up.second(gather_attention.across)
+    gather_up.keep(gather_attention.held)
+    gather_attention.last(gather_up.held)
+    gather_up.first(gather_attention.across)
+    gather_down.far(gather_up.held)
+    gather_up.keep(gather_attention.across)
+    gather_up.second()
     gather_up.third()
-    attention_w = weights_of(gather_attention, inverse)
-    gather_down.keep()
-    gather_down.far(gather_up.held)
+    attention_w = weights_of(gather_attention, far_places)
 
     (h1_ready,) = after([h1], gather_up.held)
     proj, heads, lse, mid, h2 = pl.pallas_call(
@@ -884,11 +924,11 @@
         grid=(tiles,),
         in_specs=[SMEM, rows_of(width), rows_of(width), keys_spec, norm_spec, ANY, ANY, ANY, ANY],
         out_specs=(
-            rows_of(3 * width), rows_of(groups * 2 * LANES), lse_spec, rows_of(width),
+            rows_of(3 * width), rows_of(all_heads), lse_spec, rows_of(width),
             rows_of(width),
         ),
         out_shape=(
-            shape_of(rows, 3 * width), shape_of(rows, groups * 2 * LANES),
+            shape_of(rows, 3 * width), shape_of(rows, all_heads),
             shape_of(rows // LANES, 8, 2 * LANES, dtype=F32),
             shape_of(rows, width, dtype=F32), shape_of(rows, width),
         ),
@@ -896,21 +936,20 @@
         compiler_params=params(),
         cost_estimate=cost(2 * rows * width * groups * 900, 12e6),
         name="attention_forward",
-    )(kernel_order, x, h1_ready, live_keys, norms, *attention_w)
+    )(kernel_far, x, h1_ready, live_keys, norms, *attention_w)
 
     gather_down.keep(h2)
     gather_up.last(gather_down.held)
     gather_down.second()
     gather_down.third()
-    gather_images.keep()
     gather_images.far(gather_down.held)
-    up_w = weights_of(gather_up, near_inverse)
+    up_w = weights_of(gather_up, far_places)
     (h2_ready,) = after([h2], gather_down.held)
 
     hid, slope, pooled_hid = pl.pallas_call(
         functools.partial(up_forward, seq_len=seq_len),
         grid=(tiles,),
-        in_specs=[SMEM, rows_of(width), live_spec, ANY, ANY, ANY, ANY],
+        in_specs=[SMEM, rows_of(width), count_spec, ANY, ANY, ANY, ANY],
         out_specs=(rows_of(groups * ff), rows_of(groups * ff), rows_of(groups * ff, seq_tile)),
         out_shape=(
             shape_of(rows, groups * ff), shape_of(rows, groups * ff), shape_of(all_seqs, groups * ff),
@@ -919,85 +958,68 @@
         compiler_params=params(),
         cost_estimate=cost(2 * rows * width * groups * ff, 20e6),
         name="up_forward",
-    )(kernel_near_order, h2_ready, live_cols, *up_w)
+    )(kernel_far, h2_ready, counts, *up_w)
 
     gather_images.keep(hid)
     gather_down.last(hid, gather_images.held)
     gather_images.second(gather_down.across)
     gather_images.third()
-    down_w = weights_of(gather_down, near_inverse)
+    down_w = weights_of(gather_down, near_places)
     (hid_ready,) = after([hid], gather_images.held)
 
     block_out, pooled = pl.pallas_call(
         functools.partial(down_forward, seq_len=seq_len),
         grid=(tiles,),
-        in_specs=[SMEM, rows_of(groups * ff), rows_of(width), live_spec, ANY, ANY, ANY, ANY],
+        in_specs=[SMEM, rows_of(all_ff), rows_of(width), count_spec, ANY, ANY, ANY, ANY],
         out_specs=(rows_of(width), rows_of(width, seq_tile)),
         out_shape=(shape_of(rows, width), shape_of(all_seqs, width, dtype=F32)),
         scratch_shapes=weight_scratch(ff),
         compiler_params=params(),
         cost_estimate=cost(2 * rows * width * groups * ff, 20e6),
         name="down_forward",
-    )(kernel_near_order, hid_ready, mid, live_cols, *down_w)
+    )(kernel_near, hid_ready, mid, counts, *down_w)
 
     gather_images.last(pooled)
-    images = gather_images.quarters()
-    images = [part.reshape(-1, width) for part in images]
-    loss, grad_seq, grad_low = pl.pallas_call(
-        functools.partial(contrast, micros=micros),
-        in_specs=[WHOLE] * 6,
-        out_specs=(WHOLE,) * 3,
+    images = [part.reshape(-1, width) for part in gather_images.quarters()]
+
+    def quarters_of(cols):
+        return (shape_of(quarter, block_rows, cols),) * 4
+
+    loss, grad_seq, grad_low, *down_parts = pl.pallas_call(
+        functools.partial(loss_backward, micros=micros, groups=groups),
+        in_specs=[SMEM] + [WHOLE] * 7,
+        out_specs=(WHOLE,) * 3 + (ANY,) * 4,
         out_shape=(
             shape_of(all_seqs, LANES, dtype=F32), shape_of(all_seqs, width, dtype=F32),
             shape_of(all_seqs, width),
-        ),
+        ) + quarters_of(ff),
+        scratch_shapes=[pltpu.VMEM((2, width, ff), BF16), pltpu.SemaphoreType.DMA((2,))],
         compiler_params=params(),
-        cost_estimate=cost(4 * all_seqs * width * images[0].shape[0] * 4, 4e6),
-        name="contrast",
-    )(pooled, counts, *images)
-
-    gradient_out = (shape_of(quarter, block_rows, packed),) * 4
-
-    def gradient(kernel, lefts, rights, widths):
-        depth = lefts[0].shape[0]
-        specs = [
-            (fixed((depth, width)), pl.BlockSpec((depth, cols), lambda i: (0, i)))
-            for cols in widths
-        ]
-        return pl.pallas_call(
-            kernel,
-            grid=(groups,),
-            in_specs=[SMEM] + [spec for pair in specs for spec in pair],
-            out_specs=(ANY,) * 4,
-            out_shape=gradient_out,
-            scratch_shapes=[pltpu.VMEM((width, depth), BF16) for _ in lefts]
-            + [pltpu.VMEM((2, width, packed), BF16), pltpu.SemaphoreType.DMA((2,))],
-            compiler_params=params(),
-            cost_estimate=cost(2 * depth * width * groups * 900, 10e6),
-            name=kernel.__name__,
-        )(kernel_inverse, *(part for pair in zip(lefts, rights) for part in pair))
-
-    sum_down = sum_of(gradient(weight_gradient, (grad_low,), (pooled_hid,), (ff,)))
+        cost_estimate=cost(8 * all_seqs * width * groups * ff, 20e6),
+        name="loss_backward",
+    )(kernel_far, pooled, counts, *images, pooled_hid)
+    sum_down = sum_of(down_parts)
 
     by_seq = pl.pallas_call(
         down_backward,
         in_specs=[SMEM, WHOLE, ANY, ANY, ANY, ANY],
         out_specs=WHOLE,
-        out_shape=shape_of(all_seqs, groups * ff, dtype=F32),
+        out_shape=shape_of(all_seqs, all_ff, dtype=F32),
         scratch_shapes=weight_scratch(ff),
         compiler_params=params(),
         cost_estimate=cost(8 * all_seqs * width * groups * ff, 6e6),
         name="down_backward",
-    )(kernel_near_order, grad_low, *down_w)
-
-    sum_down.second(by_seq)
-    (grad_ready,) = after([grad_seq], sum_down.going)
+    )(kernel_near, grad_low, *down_w)
+    by_seq, sum_down.from_across = join(by_seq, sum_down.from_across)
+    sum_down.second()
+    (grad_seq,) = after([grad_seq], sum_down.going)
+
     dup, dmid, dmid_low, sums_two = pl.pallas_call(
         functools.partial(mlp_backward, seq_len=seq_len),
         grid=(tiles,),
         in_specs=[
             SMEM, rows_of(width, seq_tile), rows_of(groups * ff, seq_tile), rows_of(groups * ff),
-            live_spec, rows_of(width), norm_spec, ANY, ANY, ANY, ANY,
+            count_spec, rows_of(width), norm_spec, ANY, ANY, ANY, ANY,
         ],
         out_specs=(rows_of(groups * ff), rows_of(width), rows_of(width), fixed((8, width))),
         out_shape=(
@@ -1008,121 +1030,139 @@
         compiler_params=params(),
         cost_estimate=cost(2 * rows * width * groups * ff, 25e6),
         name="mlp_backward",
-    )(kernel_near_order, grad_ready, by_seq, slope, live_cols, mid, norms, *up_w)
-
-    sum_down.first(dmid)
+    )(kernel_far, grad_seq, by_seq, slope, counts, mid, norms, *up_w)
+
+    def gradient(name, *pairs):
+        cols = [right.shape[1] // groups for _, right in pairs]
+        return pl.pallas_call(
+            weight_gradient,
+            grid=(groups,),
+            in_specs=[SMEM] + [
+                spec
+                for wide in cols
+                for spec in (
+                    fixed((rows, width)), pl.BlockSpec((rows, wide), lambda i: (0, i))
+                )
+            ],
+            out_specs=(ANY,) * 4,
+            out_shape=quarters_of(sum(cols)),
+            scratch_shapes=[pltpu.VMEM((width, rows), BF16) for _ in pairs]
+            + [pltpu.VMEM((2, width, sum(cols)), BF16), pltpu.SemaphoreType.DMA((2,))],
+            compiler_params=params(),
+            cost_estimate=cost(2 * rows * width * groups * 900, 10e6),
+            name=name,
+        )(kernel_far, *(part for pair in pairs for part in pair))
+
+    dmid, sum_down.received = join(dmid, sum_down.received)
+    sum_down.first()
     (h2_ready,) = after([h2], sum_down.going)
-    up_parts = gradient(weight_gradient, (h2_ready,), (dup,), (ff,))
+    up_parts = gradient("up_gradient", (h2_ready, dup), (dmid_low, heads))
     *up_parts, sum_down.received = join(*up_parts, sum_down.received)
     sum_up = sum_of(up_parts)
     sum_down.far()
+    (sum_up.from_across,) = after([sum_up.from_across], sum_down.going)
     sum_up.second()
 
-    def backward(start, ready, earlier=()):
-        return pl.pallas_call(
-            functools.partial(attention_backward, seq_len=seq_len),
-            grid=(tiles,),
-            in_specs=[
-                SMEM, rows_of(width, start=start),
-                pl.BlockSpec((TILE // LANES, seq_len, 2 * LANES), lambda i: (i + start, 0, 0)),
-                norm_spec, rows_of(3 * width, start=start),
-                pl.BlockSpec((TILE // LANES, 8, 2 * LANES), lambda i: (i + start, 0, 0)),
-                rows_of(width, start=start), rows_of(width, start=start),
-            ] + [ANY] * (4 + len(earlier)),
-            out_specs=(
-                rows_of(groups * 5 * LANES, start=start), rows_of(width, start=start),
-                fixed((8, width)),
-            ),
-            out_shape=(
-                shape_of(rows, groups * 5 * LANES), shape_of(rows, width, dtype=F32),
-                shape_of(8, width, dtype=F32),
-            ),
-            scratch_shapes=weight_scratch(packed),
-            input_output_aliases={12 + i: i for i in range(len(earlier))},
-            compiler_params=params(),
-            cost_estimate=cost(rows * width * groups * 1300, 20e6),
-            name="attention_backward",
-        )(
-            kernel_order, ready, live_keys, norms, proj, lse, dmid, dmid_low, *attention_w, *earlier
-        )
-
-    (x_ready,) = after([x], sum_up.going, sum_down.going)
-    dproj, input_grad, sums_one = backward(0, x_ready)
-    sum_up.first(sums_one)
-    norm_sum = jnp.concatenate([sums_one[:2], sums_two[:2]], axis=0)
+    (x_ready,) = after([x], sum_up.going)
+    dproj, input_grad, sums_one = pl.pallas_call(
+        functools.partial(attention_backward, seq_len=seq_len),
+        grid=(tiles,),
+        in_specs=[
+            SMEM, rows_of(width), keys_spec, norm_spec, rows_of(3 * width), lse_spec,
+            rows_of(width), rows_of(width), ANY, ANY, ANY, ANY,
+        ],
+        out_specs=(rows_of(groups * 5 * LANES), rows_of(width), fixed((8, width))),
+        out_shape=(
+            shape_of(rows, groups * 5 * LANES), shape_of(rows, width, dtype=F32),
+            shape_of(8, width, dtype=F32),
+        ),
+        scratch_shapes=weight_scratch(packed),
+        compiler_params=params(),
+        cost_estimate=cost(2 * rows * width * groups * 1300, 20e6),
+        name="attention_backward",
+    )(kernel_far, x_ready, live_keys, norms, proj, lse, dmid, dmid_low, *attention_w)
 
     def exchanged(values, bit):
         return swap(values, [i ^ bit for i in range(count)])
 
-    (h1_ready,) = after([h1], sum_up.going, *sum_down.keep)
+    sums_one, sum_up.received, sum_down.keep = join(sums_one, sum_up.received, sum_down.keep)
+    norm_sum = jnp.concatenate([sums_one[:2], sums_two[:2]], axis=0)
     received = exchanged(norm_sum, 1)
-    attention_parts = gradient(
-        attention_gradient, (h1_ready, dmid_low), (dproj, heads), (5 * LANES, 2 * LANES)
-    )
-    *attention_parts, sum_up.received, received = join(
-        *attention_parts, sum_up.received, received
+    sum_up.first()
+    (received,) = after([received], sum_up.going)
+    norm_sum = norm_sum + received
+    received = exchanged(norm_sum, 8)
+    (h1_ready,) = after([h1], sum_up.going, norm_sum)
+    attention_parts = gradient("attention_gradient", (h1_ready, dproj))
+    *attention_parts, received, sum_up.received = join(
+        *attention_parts, received, sum_up.received
     )
     norm_sum = norm_sum + received
     sum_attention = sum_of(attention_parts)
+    if count > 16:
+        sum_attention.from_across, received = join(
+            sum_attention.from_across, exchanged(norm_sum, 16)
+        )
+        norm_sum = norm_sum + received
     sum_attention.second()
-    sum_up.far()
-    sum_down.keep = after(sum_down.keep, sum_attention.going)
-    grad_down, down_left_new, down_right_new, down_new = shampoo(
-        sum_down.keep, down_left, down_right, down_left_root, down_right_root, w_down
-    )
-    (norm_sum,) = after([norm_sum], sum_attention.going)
-    bit = 8
+    sum_up.far(sum_attention.going)
+    bit = 32
     while bit < count:
         norm_sum = norm_sum + exchanged(norm_sum, bit)
         bit *= 2
-    sum_attention.first(norm_sum, down_new)
+    received = exchanged(norm_sum, 2)
+    sum_down.keep = after(sum_down.keep, sum_attention.going)
+    grad_down, down_left_new, down_right_new, down_new = shampoo(
+        shampoo_kernel, sum_down.keep, (w_down,), ((owned, ff),),
+        (down_left, down_right, down_left_root, down_right_root),
+    )
+    sum_attention.received, received, *sooner = join(
+        *after([sum_attention.received, received, *sum_up.keep[:-1]], down_new)
+    )
+    sum_up.keep = [*sooner, sum_up.keep[-1]]
+    norm_sum = norm_sum + received
+    sum_attention.first()
+    received = exchanged(norm_sum, 4)
+    (sum_up.keep[-1],) = after([sum_up.keep[-1]], sum_attention.going)
+    sum_attention.received, sum_up.keep[-1], received = join(
+        sum_attention.received, sum_up.keep[-1], received
+    )
+    norm_sum = norm_sum + received
+    sum_attention.far()
     sum_up.keep = after(sum_up.keep, sum_attention.going)
-    grad_up, up_left_new, up_right_new, up_new = shampoo(
-        sum_up.keep, up_left, up_right, up_left_root, up_right_root, w_up
-    )
-    sum_attention.far(up_new)
-    (norm_sum,) = after([norm_sum], sum_attention.going)
-    for bit in (2, 4):
-        norm_sum = norm_sum + exchanged(norm_sum, bit)
-    *sum_attention.keep, norm_sum = join(*sum_attention.keep, norm_sum)
+    (
+        grad_up, up_left_new, up_right_new, up_new, grad_out, out_left_new, out_right_new, out_new
+    ) = shampoo(
+        up_shampoo, sum_up.keep, (w_up, w_out), ((owned, ff), (owned, width_of(w_out))),
+        (
+            up_left, up_right, up_left_root, up_right_root,
+            out_left, out_right, out_left_root, out_right_root,
+        ),
+    )
+    (norm_sum,) = after([norm_sum], up_new)
     grad_norm = lax.dynamic_slice_in_dim(norm_sum, dp_index * owned, owned, 1).T
-
-    qkv_turned = w_qkv.transpose(1, 0, 2)
-    (
-        grad_qkv, qkv_left_new, qkv_right_new, qkv_new,
-        grad_out, out_left_new, out_right_new, out_new,
-    ) = pl.pallas_call(
-        attention_shampoo,
-        grid=(1,),
-        in_specs=[pl.BlockSpec((1, owned, packed), lambda i: (0, 0, 0))] * len(sum_attention.keep)
-        + [WHOLE] * 10,
-        out_specs=(WHOLE,) * 8,
-        out_shape=(
-            shape_of(*qkv_turned.shape, dtype=F32), shape_of(owned, owned, dtype=F32),
-            shape_of(*qkv_right.shape[2:], dtype=F32), shape_of(*qkv_turned.shape, dtype=F32),
-            shape_of(*w_out.shape, dtype=F32), shape_of(owned, owned, dtype=F32),
-            shape_of(*out_right.shape[2:], dtype=F32), shape_of(*w_out.shape, dtype=F32),
-        ),
-        compiler_params=params(),
-        cost_estimate=cost(4 * owned * 576 * 576, 12 * 576 * 576),
-        name="attention_shampoo",
-    )(
-        *sum_attention.keep, qkv_turned, w_out,
-        *(
-            stat[0, 0]
-            for stat in (
-                qkv_left, qkv_right, qkv_left_root, qkv_right_root,
-                out_left, out_right, out_left_root, out_right_root,
-            )
-        ),
-    )
-    grad_qkv, qkv_new = grad_qkv.transpose(1, 0, 2), qkv_new.transpose(1, 0, 2)
-    qkv_left_new, qkv_right_new, out_left_new, out_right_new = (
-        stat[None, None] for stat in (qkv_left_new, qkv_right_new, out_left_new, out_right_new)
-    )
     norm_second_new = STAT_DECAY * norm_second + (1.0 - STAT_DECAY) * grad_norm * grad_norm
     own_params = lax.dynamic_slice_in_dim(norm_params, dp_index * owned, owned, 0)
     norm_new = own_params - NORM_RATE * grad_norm / (jnp.sqrt(norm_second_new) + 1e-08)
+    *sum_attention.keep, grad_norm, norm_second_new, norm_new = join(
+        *sum_attention.keep, grad_norm, norm_second_new, norm_new
+    )
+    qkv_turned = w_qkv.transpose(1, 0, 2)
+    grad_qkv, qkv_left_new, qkv_right_new, qkv_new = shampoo(
+        attention_shampoo, sum_attention.keep, (qkv_turned,), ((owned, 3 * w_qkv.shape[2]),),
+        (qkv_left, qkv_right, qkv_left_root, qkv_right_root),
+    )
+    grad_qkv, qkv_new = grad_qkv.transpose(1, 0, 2), qkv_new.transpose(1, 0, 2)
+    (
+        qkv_left_new, qkv_right_new, out_left_new, out_right_new,
+        up_left_new, up_right_new, down_left_new, down_right_new,
+    ) = (
+        stat[None, None]
+        for stat in (
+            qkv_left_new, qkv_right_new, out_left_new, out_right_new,
+            up_left_new, up_right_new, down_left_new, down_right_new,
+        )
+    )
     return (
         block_out.reshape(block_in.shape),
         input_grad.reshape(block_in.shape),

time: 279 us -> 259 us (0.928)
  waiting for transfers between devices: 61.6 us -> 47 us
  local copies, waits for them, and re-layouts: 15.9 us -> 8.29 us
  other arithmetic: 8.68 us -> 11.6 us
    ppermute x52 -> x54, waiting for transfers between devices: 61.6 us -> 47 us  [swap(): return lax.ppermute(values, AXES, list(enumerate(step)))]
    squeeze x4 -> x1, local copies, waits for them, and re-layouts: 3.72 us -> 0.01 us  [pack_qkv(): q, k, v = (qkv[:, i] for i in range(3))]
    unnamed x93 -> x106, local copies, waits for them, and re-layouts: 6.22 us -> 4.45 us
    ppermute x52 -> x54, starting transfers between devices: 55.4 us -> 57.1 us  [swap(): return lax.ppermute(values, AXES, list(enumerate(step)))]
    pallas_call x8 -> x7, Pallas kernels: 66.7 us -> 65.7 us  [the longest x2 21.6 us: gradient(): pl.pallas_call(weight_gradient, grid=(groups,), in_specs=[SMEM] + [spec f...]
  transfers between devices with their start and end apart: 52 -> 54, of which waited for: 19 -> 16; matrix products, arithmetic and copies ran while one was open for 5% -> 4% of each run, Pallas kernels for 43% -> 46%
where the time goes in v3:
time: 259 us; the launch traced here: 258 us
  Pallas kernels  132 us (51%)
  starting transfers between devices  57.1 us (22%)
  waiting for transfers between devices  47 us (18%)
  other arithmetic  11.6 us (4%)
  local copies, waits for them, and re-layouts  8.29 us (3%)
    ppermute x54, starting transfers between devices, swap(): return lax.ppermute(values, AXES, list(enumerate(step)))  57.1 us
    ppermute x54, waiting for transfers between devices, swap(): return lax.ppermute(values, AXES, list(enumerate(step)))  47 us
    pallas_call x2, Pallas kernels, gradient(): pl.pallas_call(weight_gradient, grid=(groups,), in_specs=[SMEM] + [spec f...  21.6 us
    pallas_call x1, Pallas kernels, per_device(): pl.pallas_call(functools.partial(attention_backward, seq_len=seq_len), gr...  20.7 us
    pallas_call x1, Pallas kernels, per_device(): pl.pallas_call(functools.partial(attention_forward, seq_len=seq_len), gri...  16.4 us
    pallas_call x1, Pallas kernels, per_device(): pl.pallas_call(functools.partial(up_forward, seq_len=seq_len), grid=(tile...  15.8 us
    pallas_call x3, Pallas kernels, shampoo(): pl.pallas_call(kernel, grid=(1,), out_shape=tuple(out_shape), in_specs=[p...  14.4 us
    pallas_call x1, Pallas kernels, per_device(): pl.pallas_call(functools.partial(mlp_backward, seq_len=seq_len), grid=(ti...  13.1 us
  transfers between devices with their start and end apart: 54, of which 16 were waited for; matrix products, arithmetic and copies ran while one was open for 4% of the time, Pallas kernels for 46%

profile of v3, /device:TPU:0, one launch (start us, length us, event | category | flops | bytes accessed | tf_op | source)
XLA Modules:
  0.0 257.9 jit_solution(934615131248759315)
XLA Ops:
  2.9 5.1 %collective-permute-start.2 = (bf16[1,96,768]{2,1,0:T(8,128)(2,1)S(1)}, bf16[1,96,768]{2,1,0:T(8,128)(2,1)S(1)}, u32[]{:S(2)}, u32[]{:S(2)}) collective-permute-start(bf16[1,96,768]{2,1,0:T(8,128)(2,1)S(1)} %bitcast.65), channel_id=1, source_target_pairs={{0,24},{1,25},{2,26},{3,27},{4,28},{5,29},{6,30},{7,31},{8,16},{9,... | collective-permute-start | bytes 442376 | tf_op jit(solution)/shard_map/ppermute | solution.py:60
  15.6 4.9 %collective-permute-done.1 = bf16[1,96,768]{2,1,0:T(8,128)(2,1)S(1)} collective-permute-done((bf16[1,96,768]{2,1,0:T(8,128)(2,1)S(1)}, bf16[1,96,768]{2,1,0:T(8,128)(2,1)S(1)}, u32[]{:S(2)}, u32[]{:S(2)}) %collective-permute-start.1) | collective-permute-done | bytes 147488 | tf_op jit(solution)/shard_map/ppermute | solution.py:60
  23.5 4.1 %first_norm.1.h1_ref.refs_0_ = bf16[1024,768]{1,0:T(8,128)(2,1)} custom-call(bf16[1024,768]{1,0:T(8,128)(2,1)} %bitcast.60, f32[4,768]{1,0:T(4,128)} %bitcast.83), custom_call_target="tpu_custom_call" | custom-call | flops 4 | bytes 100000000 | tf_op jit(solution)/shard_map/first_norm/pallas_call | solution.py:896
  27.7 2.8 %collective-permute-done.8 = bf16[4,96,768]{2,1,0:T(8,128)(2,1)S(1)} collective-permute-done((bf16[4,96,768]{2,1,0:T(8,128)(2,1)S(1)}, bf16[4,96,768]{2,1,0:T(8,128)(2,1)S(1)}, u32[]{:S(2)}, u32[]{:S(2)}) %collective-permute-start.8) | collective-permute-done | bytes 589856 | tf_op jit(solution)/shard_map/ppermute | solution.py:60
  32.2 2.6 %collective-permute-start.7 = (bf16[1,96,768]{2,1,0:T(8,128)(2,1)S(1)}, bf16[1,96,768]{2,1,0:T(8,128)(2,1)S(1)}, u32[]{:S(2)}, u32[]{:S(2)}) collective-permute-start(bf16[1,96,768]{2,1,0:T(8,128)(2,1)S(1)} %convert_bitcast_fusion), channel_id=1, source_target_pairs={{0,24},{1,25},{2,26},{3,27},{4,28},{5,29},{6,30},{7,31},{8,16},{9,... | collective-permute-start | bytes 442376 | tf_op jit(solution)/shard_map/ppermute | solution.py:60
  36.7 4.1 %collective-permute-done.7 = bf16[1,96,768]{2,1,0:T(8,128)(2,1)S(1)} collective-permute-done((bf16[1,96,768]{2,1,0:T(8,128)(2,1)S(1)}, bf16[1,96,768]{2,1,0:T(8,128)(2,1)S(1)}, u32[]{:S(2)}, u32[]{:S(2)}) %collective-permute-start.7) | collective-permute-done | bytes 147488 | tf_op jit(solution)/shard_map/ppermute | solution.py:60
  40.8 4.9 %collective-permute-done.6 = bf16[1,96,768]{2,1,0:T(8,128)(2,1)S(1)} collective-permute-done((bf16[1,96,768]{2,1,0:T(8,128)(2,1)S(1)}, bf16[1,96,768]{2,1,0:T(8,128)(2,1)S(1)}, u32[]{:S(2)}, u32[]{:S(2)}) %collective-permute-start.6) | collective-permute-done | bytes 147488 | tf_op jit(solution)/shard_map/ppermute | solution.py:60
  50.9 5.8 %collective-permute-done.10 = bf16[4,96,768]{2,1,0:T(8,128)(2,1)S(1)} collective-permute-done((bf16[4,96,768]{2,1,0:T(8,128)(2,1)S(1)}, bf16[4,96,768]{2,1,0:T(8,128)(2,1)S(1)}, u32[]{:S(2)}, u32[]{:S(2)}) %collective-permute-start.10) | collective-permute-done | bytes 589856 | tf_op jit(solution)/shard_map/ppermute | solution.py:60
  59.5 16.4 %attention_forward.1 = (bf16[1024,2304]{1,0:T(8,128)(2,1)}, bf16[1024,1024]{1,0:T(8,128)(2,1)}, f32[8,8,256]{2,1,0:T(8,128)}, f32[1024,768]{1,0:T(8,128)}, bf16[1024,768]{1,0:T(8,128)(2,1)}) custom-call(s32[65]{0:T(128)} %get-tuple-element.181.order.places, bf16[1024,768]{1,0:T(8,128)(2,1)} %bitcast.61, bf16[1024,768]{1,0:T(8,128)(2,1)} %first_norm.1.h1_ref.refs_0_, ...), custom_call_target="tpu_custom_call" | custom-call | flops 22649241600 | bytes 12000000 | tf_op jit(solution)/shard_map/attention_forward/pallas_call | solution.py:922
  82.4 15.8 %up_forward.1 = (bf16[1024,3072]{1,0:T(8,128)(2,1)}, bf16[1024,3072]{1,0:T(8,128)(2,1)}, bf16[64,3072]{1,0:T(8,128)(2,1)}) custom-call(s32[65]{0:T(128)} %get-tuple-element.181.order.places, bf16[1024,768]{1,0:T(8,128)(2,1)} %get-tuple-element.226.h2_ref.refs_0_, f32[64,128]{1,0:T(8,128)} %broadcast_in_dim.50.count_ref, bf16[8,96,768]{2,1,0:T(8,128)(2,1)} %copy-done.12, ...), custom_call_target="tpu_custom_call" | custom-call | flops 19327352832 | bytes 20000000 | tf_op jit(solution)/shard_map/up_forward/pallas_call | solution.py:949
  103.2 11.2 %down_forward.1 = (bf16[1024,768]{1,0:T(8,128)(2,1)}, f32[64,768]{1,0:T(8,128)}) custom-call(s32[65]{0:T(128)} %get-tuple-element.180.order, bf16[1024,3072]{1,0:T(8,128)(2,1)} %get-tuple-element.208.hid_ref, f32[1024,768]{1,0:T(8,128)} %get-tuple-element.209.mid_ref, f32[64,128]{1,0:T(8,128)} %broadcast_in_dim.50.count_ref, bf16[8,96,768]{2,1,0:T(8,128)(2,1)} %copy-done.23, ...), custom_call_target="tpu_custom_call" | custom-call | flops 19327352832 | bytes 20000000 | tf_op jit(solution)/shard_map/down_forward/pallas_call | solution.py:970
  117.7 9.0 %loss_backward.1 = (f32[64,128]{1,0:T(8,128)}, f32[64,768]{1,0:T(8,128)}, bf16[64,768]{1,0:T(8,128)(2,1)}, bf16[8,96,768]{2,1,0:T(8,128)(2,1)}, bf16[8,96,768]{2...) custom-call(s32[65]{0:T(128)} %get-tuple-element.181.order.places, ...), custom_call_target="tpu_custom_call" | custom-call | flops 4831838208 | bytes 20000000 | tf_op jit(solution)/shard_map/loss_backward/pallas_call | solution.py:988
  127.3 5.7 %down_backward.1.by_seq_ref = f32[64,3072]{1,0:T(8,128)} custom-call(s32[65]{0:T(128)} %get-tuple-element.180.order, bf16[64,768]{1,0:T(8,128)(2,1)} %get-tuple-element.218.low_ref, bf16[8,96,768]{2,1,0:T(8,128)(2,1)} %copy-done.23, bf16[8,96,768]{2,1,0:T(8,128)(2,1)} %collective-permute-done.22.w1, bf16[8,96,768]{2,1,0:T(8,128)(2,1)} %copy-done.40, ...), custom_call_target="tpu_custom_call" | custom-call | flops 4831838208 | bytes 6000000 | tf_op jit(solution)/shard_map/down_backward/pallas_call | solution.py:1003
  134.0 13.1 %mlp_backward.1 = (bf16[1024,3072]{1,0:T(8,128)(2,1)}, f32[1024,768]{1,0:T(8,128)}, bf16[1024,768]{1,0:T(8,128)(2,1)}, f32[8,768]{1,0:T(8,128)}) custom-call(s32[65]{0:T(128)} %get-tuple-element.181.order.places, f32[64,768]{1,0:T(8,128)} %get-tuple-element.221.grad_ref, f32[64,3072]{1,0:T(8,128)} %down_backward.1.by_seq_ref, ...), custom_call_target="tpu_custom_call" | custom-call | flops 19327352832 | bytes 25000000 | tf_op jit(solution)/shard_map/mlp_backward/pallas_call | solution.py:1017
  150.5 12.3 %up_gradient.1 = (bf16[8,96,1024]{2,1,0:T(8,128)(2,1)}, bf16[8,96,1024]{2,1,0:T(8,128)(2,1)}, bf16[8,96,1024]{2,1,0:T(8,128)(2,1)}, bf16[8,96,1024]{2,1,0:T(8,128)(2,1)}) custom-call(s32[65]{0:T(128)} %get-tuple-element.181.order.places, bf16[1024,768]{1,0:T(8,128)(2,1)} %get-tuple-element.226.h2_ref.refs_0_, bf16[1024,3072]{1,0:T(8,128)(2,1)} %get-tuple-element.227.refs_1_, ...), custom_call_target="tpu_custom_call" | custom-call | flops 22649241600 | bytes 10000000 | tf_op jit(solution)/shard_map/up_gradient/pallas_call | solution.py:1037
  171.5 20.7 %attention_backward.1 = (bf16[1024,2560]{1,0:T(8,128)(2,1)}, f32[1024,768]{1,0:T(8,128)}, f32[8,768]{1,0:T(8,128)}) custom-call(s32[65]{0:T(128)} %get-tuple-element.181.order.places, bf16[1024,768]{1,0:T(8,128)(2,1)} %bitcast.62, f32[8,16,256]{2,1,0:T(8,128)} %pad_maximum_fusion.3.live_ref, f32[4,768]{1,0:T(4,128)} %bitcast.86, ...), custom_call_target="tpu_custom_call" | custom-call | flops 32715571200 | bytes 20000000 | tf_op jit(solution)/shard_map/attention_backward/pallas_call | solution.py:1067
  196.0 9.3 %attention_gradient.1 = (bf16[8,96,640]{2,1,0:T(8,128)(2,1)}, bf16[8,96,640]{2,1,0:T(8,128)(2,1)}, bf16[8,96,640]{2,1,0:T(8,128)(2,1)}, bf16[8,96,640]{2,1,0:T(8,128)(2,1)}) custom-call(s32[65]{0:T(128)} %get-tuple-element.181.order.places, bf16[1024,768]{1,0:T(8,128)(2,1)} %first_norm.1.h1_ref.refs_0_, bf16[1024,2560]{1,0:T(8,128)(2,1)} %get-tuple-element.252.refs_1_), custom_call_target="tpu_custom_call" | custom-call | flops 22649241600 | bytes 10000000 | tf_op jit(solution)/shard_map/attention_gradient/pallas_call | solution.py:1037
  208.5 3.4 %collective-permute-done.43 = f32[4,768]{1,0:T(4,128)S(1)} collective-permute-done((f32[4,768]{1,0:T(4,128)S(1)}, f32[4,768]{1,0:T(4,128)S(1)}, u32[]{:S(2)}, u32[]{:S(2)}) %collective-permute-start.43) | collective-permute-done | bytes 12320 | tf_op jit(solution)/shard_map/ppermute | solution.py:60
  218.8 5.0 %shampoo_kernel.1 = (f32[96,768]{1,0:T(8,128)}, f32[96,96]{1,0:T(8,128)}, f32[768,768]{1,0:T(8,128)}, f32[96,768]{1,0:T(8,128)}) custom-call(bf16[4,96,768]{2,1,0:T(8,128)(2,1)} %copy-done.1, bf16[4,96,768]{2,1,0:T(8,128)(2,1)} %copy-done.4, bf16[1,96,768]{2,1,0:T(8,128)(2,1)} %copy-done.17, bf16[1,96,768]{2,1,0:T(8,128)(2,1)} %copy-done.16, ...), custom_call_target="tpu_custom_call" | custom-call | flops 905969664 | bytes 7077888 | tf_op jit(solution)/shard_map/shampoo_kernel/pallas_call | solution.py:759
  223.9 3.9 %collective-permute-done.45 = f32[4,768]{1,0:T(4,128)S(1)} collective-permute-done((f32[4,768]{1,0:T(4,128)S(1)}, f32[4,768]{1,0:T(4,128)S(1)}, u32[]{:S(2)}, u32[]{:S(2)}) %collective-permute-start.45) | collective-permute-done | bytes 12320 | tf_op jit(solution)/shard_map/ppermute | solution.py:60
  233.8 3.5 %collective-permute-done.49.refs_4_ = bf16[1,96,1024]{2,1,0:T(8,128)(2,1)S(1)} collective-permute-done((bf16[1,96,1024]{2,1,0:T(8,128)(2,1)S(1)}, bf16[1,96,1024]{2,1,0:T(8,128)(2,1)S(1)}, u32[]{:S(2)}, u32[]{:S(2)}) %collective-permute-start.49) | collective-permute-done | bytes 196640 | tf_op jit(solution)/shard_map/ppermute | solution.py:60
  240.3 4.8 %collective-permute-start.52 = (bf16[1,96,640]{2,1,0:T(8,128)(2,1)S(1)}, bf16[1,96,640]{2,1,0:T(8,128)(2,1)S(1)}, u32[]{:S(2)}, u32[]{:S(2)}) collective-permute-start(bf16[1,96,640]{2,1,0:T(8,128)(2,1)S(1)} %get-tuple-element.337), channel_id=1, source_target_pairs={{0,16},{1,17},{2,18},{3,19},{4,20},{5,21},{6,22},{7,23},{8,24},{9,... | collective-permute-start | bytes 368648 | tf_op jit(solution)/shard_map/ppermute | solution.py:60
  245.6 5.4 %up_shampoo.1 = (f32[96,768]{1,0:T(8,128)}, f32[96,96]{1,0:T(8,128)}, f32[768,768]{1,0:T(8,128)}, f32[96,768]{1,0:T(8,128)}, f32[96,192]{1,0:T(8,128)}, /*index=...) custom-call(bf16[4,96,1024]{2,1,0:T(8,128)(2,1)} %copy-done, bf16[4,96,1024]{2,1,0:T(8,128)(2,1)} %copy-done.3, ...), custom_call_target="tpu_custom_call" | custom-call | flops 1610612736 | bytes 12582912 | tf_op jit(solution)/shard_map/up_shampoo/pallas_call | solution.py:759
  253.7 4.0 %attention_shampoo.1 = (f32[3,96,192]{2,1,0:T(8,128)}, f32[96,96]{1,0:T(8,128)}, f32[576,576]{1,0:T(8,128)}, f32[3,96,192]{2,1,0:T(8,128)}) custom-call(bf16[4,96,640]{2,1,0:T(8,128)(2,1)} %copy-done.2, bf16[4,96,640]{2,1,0:T(8,128)(2,1)} %copy-done.6, bf16[1,96,640]{2,1,0:T(8,128)(2,1)} %copy-done.21, bf16[1,96,640]{2,1,0:T(8,128)(2,1)} %copy-done.20, ...), custom_call_target="tpu_custom_call" | custom-call | flops 629145600 | bytes 4915200 | tf_op jit(solution)/shard_map/attention_shampoo/pallas_call | solution.py:759
  (257 shorter events, 78.1 us)
Async XLA Ops:
  30.6 16.3 %collective-permute-start.9 = (bf16[8,96,768]{2,1,0:T(8,128)(2,1)S(1)}, bf16[8,96,768]{2,1,0:T(8,128)(2,1)S(1)}, u32[]{:S(2)}, u32[]{:S(2)}) collective-permute-start(bf16[8,96,768]{2,1,0:T(8,128)(2,1)S(1)} %constant_dynamic-update-slice_fusion.w0), channel_id=1, source_target_pairs={{0,2},{1,5},{2,0},{3,7},{4,6},{5,1},{6,4},{7,3},{8,10},{9,13},{10,... | collective-permute-start | bytes 3538952 | tf_op jit(solution)/shard_map/ppermute | solution.py:60
  36.6 20.2 %collective-permute-start.11 = (bf16[8,96,768]{2,1,0:T(8,128)(2,1)S(1)}, bf16[8,96,768]{2,1,0:T(8,128)(2,1)S(1)}, u32[]{:S(2)}, u32[]{:S(2)}) collective-permute-start(bf16[8,96,768]{2,1,0:T(8,128)(2,1)S(1)} %constant_dynamic-update-slice_fusion.w0), channel_id=1, source_target_pairs={{0,1},{1,0},{2,3},{3,2},{4,5},{5,4},{6,7},{7,6},{8,9},{9,8},{10,11... | collective-permute-start | bytes 3538952 | tf_op jit(solution)/shard_map/ppermute | solution.py:60
  48.3 27.7 %collective-permute-start.15 = (bf16[2,96,768]{2,1,0:T(8,128)(2,1)S(1)}, bf16[2,96,768]{2,1,0:T(8,128)(2,1)S(1)}, u32[]{:S(2)}, u32[]{:S(2)}) collective-permute-start(bf16[2,96,768]{2,1,0:T(8,128)(2,1)S(1)} %pad_maximum_fusion.1), channel_id=1, source_target_pairs={{0,24},{1,25},{2,26},{3,27},{4,28},{5,29},{6,30},{7,31},{8,16},{9,... | collective-permute-start | bytes 884744 | tf_op jit(solution)/shard_map/ppermute | solution.py:60
  50.9 25.1 %collective-permute-start.14 = (bf16[2,96,768]{2,1,0:T(8,128)(2,1)S(1)}, bf16[2,96,768]{2,1,0:T(8,128)(2,1)S(1)}, u32[]{:S(2)}, u32[]{:S(2)}) collective-permute-start(bf16[2,96,768]{2,1,0:T(8,128)(2,1)S(1)} %pad_maximum_fusion.1), channel_id=1, source_target_pairs={{0,16},{1,17},{2,18},{3,19},{4,20},{5,21},{6,22},{7,23},{8,24},{9,... | collective-permute-start | bytes 884744 | tf_op jit(solution)/shard_map/ppermute | solution.py:60
  56.7 19.3 %collective-permute-start.13 = (bf16[2,96,768]{2,1,0:T(8,128)(2,1)S(1)}, bf16[2,96,768]{2,1,0:T(8,128)(2,1)S(1)}, u32[]{:S(2)}, u32[]{:S(2)}) collective-permute-start(bf16[2,96,768]{2,1,0:T(8,128)(2,1)S(1)} %pad_maximum_fusion.1), channel_id=1, source_target_pairs={{0,8},{1,9},{2,10},{3,11},{4,12},{5,13},{6,14},{7,15},{8,0},{9,1},... | collective-permute-start | bytes 884744 | tf_op jit(solution)/shard_map/ppermute | solution.py:60
  56.8 23.9 %collective-permute-start.17 = (bf16[8,96,768]{2,1,0:T(8,128)(2,1)S(1)}, bf16[8,96,768]{2,1,0:T(8,128)(2,1)S(1)}, u32[]{:S(2)}, u32[]{:S(2)}) collective-permute-start(bf16[8,96,768]{2,1,0:T(8,128)(2,1)S(1)} %constant_dynamic-update-slice_fusion.9.w0), channel_id=1, source_target_pairs={{0,1},{1,0},{2,3},{3,2},{4,5},{5,4},{6,7},{7,6},{8,9},{9,8},{10,11... | collective-permute-start | bytes 3538952 | tf_op jit(solution)/shard_map/ppermute | solution.py:60
  58.0 18.1 %collective-permute-start.16 = (bf16[8,96,768]{2,1,0:T(8,128)(2,1)S(1)}, bf16[8,96,768]{2,1,0:T(8,128)(2,1)S(1)}, u32[]{:S(2)}, u32[]{:S(2)}) collective-permute-start(bf16[8,96,768]{2,1,0:T(8,128)(2,1)S(1)} %constant_dynamic-update-slice_fusion.9.w0), channel_id=1, source_target_pairs={{0,2},{1,5},{2,0},{3,7},{4,6},{5,1},{6,4},{7,3},{8,10},{9,13},{10,... | collective-permute-start | bytes 3538952 | tf_op jit(solution)/shard_map/ppermute | solution.py:60
  76.3 21.9 %collective-permute-start.21 = (bf16[2,64,768]{2,1,0:T(8,128)(2,1)S(1)}, bf16[2,64,768]{2,1,0:T(8,128)(2,1)S(1)}, u32[]{:S(2)}, u32[]{:S(2)}) collective-permute-start(bf16[2,64,768]{2,1,0:T(8,128)(2,1)S(1)} %pad_maximum_fusion.2), channel_id=1, source_target_pairs={{0,24},{1,25},{2,26},{3,27},{4,28},{5,29},{6,30},{7,31},{8,16},{9,... | collective-permute-start | bytes 589832 | tf_op jit(solution)/shard_map/ppermute | solution.py:60
  78.8 19.4 %collective-permute-start.20 = (bf16[2,64,768]{2,1,0:T(8,128)(2,1)S(1)}, bf16[2,64,768]{2,1,0:T(8,128)(2,1)S(1)}, u32[]{:S(2)}, u32[]{:S(2)}) collective-permute-start(bf16[2,64,768]{2,1,0:T(8,128)(2,1)S(1)} %pad_maximum_fusion.2), channel_id=1, source_target_pairs={{0,16},{1,17},{2,18},{3,19},{4,20},{5,21},{6,22},{7,23},{8,24},{9,... | collective-permute-start | bytes 589832 | tf_op jit(solution)/shard_map/ppermute | solution.py:60
  79.8 18.5 %collective-permute-start.19 = (bf16[2,64,768]{2,1,0:T(8,128)(2,1)S(1)}, bf16[2,64,768]{2,1,0:T(8,128)(2,1)S(1)}, u32[]{:S(2)}, u32[]{:S(2)}) collective-permute-start(bf16[2,64,768]{2,1,0:T(8,128)(2,1)S(1)} %pad_maximum_fusion.2), channel_id=1, source_target_pairs={{0,8},{1,9},{2,10},{3,11},{4,12},{5,13},{6,14},{7,15},{8,0},{9,1},... | collective-permute-start | bytes 589832 | tf_op jit(solution)/shard_map/ppermute | solution.py:60
  80.7 19.4 %collective-permute-start.23 = (bf16[8,96,768]{2,1,0:T(8,128)(2,1)S(1)}, bf16[8,96,768]{2,1,0:T(8,128)(2,1)S(1)}, u32[]{:S(2)}, u32[]{:S(2)}) collective-permute-start(bf16[8,96,768]{2,1,0:T(8,128)(2,1)S(1)} %constant_dynamic-update-slice_fusion.11.w0), channel_id=1, source_target_pairs={{0,1},{1,0},{2,3},{3,2},{4,5},{5,4},{6,7},{7,6},{8,9},{9,8},{10,11... | collective-permute-start | bytes 3538952 | tf_op jit(solution)/shard_map/ppermute | solution.py:60
  80.8 17.5 %collective-permute-start.22 = (bf16[8,96,768]{2,1,0:T(8,128)(2,1)S(1)}, bf16[8,96,768]{2,1,0:T(8,128)(2,1)}, u32[]{:S(2)}, u32[]{:S(2)}) collective-permute-start(bf16[8,96,768]{2,1,0:T(8,128)(2,1)S(1)} %constant_dynamic-update-slice_fusion.11.w0), channel_id=1, source_target_pairs={{0,2},{1,5},{2,0},{3,7},{4,6},{5,1},{6,4},{7,3},{8,10},{9,13},{10,... | collective-permute-start | bytes 3538952 | tf_op jit(solution)/shard_map/ppermute | solution.py:60
  98.5 16.2 %collective-permute-start.26 = (bf16[8,64,768]{2,1,0:T(8,128)(2,1)S(1)}, bf16[8,64,768]{2,1,0:T(8,128)(2,1)S(1)}, u32[]{:S(2)}, u32[]{:S(2)}) collective-permute-start(bf16[8,64,768]{2,1,0:T(8,128)(2,1)S(1)} %constant_dynamic-update-slice_fusion.15), channel_id=1, source_target_pairs={{0,1},{1,0},{2,3},{3,2},{4,5},{5,4},{6,7},{7,6},{8,9},{9,8},{10,11... | collective-permute-start | bytes 2359304 | tf_op jit(solution)/shard_map/ppermute | solution.py:60
  98.9 15.6 %collective-permute-start.25 = (bf16[8,64,768]{2,1,0:T(8,128)(2,1)S(1)}, bf16[8,64,768]{2,1,0:T(8,128)(2,1)S(1)}, u32[]{:S(2)}, u32[]{:S(2)}) collective-permute-start(bf16[8,64,768]{2,1,0:T(8,128)(2,1)S(1)} %constant_dynamic-update-slice_fusion.15), channel_id=1, source_target_pairs={{0,2},{1,5},{2,0},{3,7},{4,6},{5,1},{6,4},{7,3},{8,10},{9,13},{10,... | collective-permute-start | bytes 2359304 | tf_op jit(solution)/shard_map/ppermute | solution.py:60
  127.0 22.6 %collective-permute-start.28 = (bf16[8,96,768]{2,1,0:T(8,128)(2,1)}, bf16[8,96,768]{2,1,0:T(8,128)(2,1)S(1)}, u32[]{:S(2)}, u32[]{:S(2)}) collective-permute-start(bf16[8,96,768]{2,1,0:T(8,128)(2,1)} %get-tuple-element.215), channel_id=1, source_target_pairs={{0,1},{1,0},{2,3},{3,2},{4,5},{5,4},{6,7},{7,6},{8,9},{9,8},{10,11... | collective-permute-start | bytes 3538952 | tf_op jit(solution)/shard_map/ppermute | solution.py:60
  133.4 16.3 %collective-permute-start.30 = (bf16[8,96,768]{2,1,0:T(8,128)(2,1)S(1)}, bf16[8,96,768]{2,1,0:T(8,128)(2,1)S(1)}, u32[]{:S(2)}, u32[]{:S(2)}) collective-permute-start(bf16[8,96,768]{2,1,0:T(8,128)(2,1)S(1)} %add_convert_fusion.1), channel_id=1, source_target_pairs={{0,2},{1,5},{2,0},{3,7},{4,6},{5,1},{6,4},{7,3},{8,10},{9,13},{10,... | collective-permute-start | bytes 3538952 | tf_op jit(solution)/shard_map/ppermute | solution.py:60
  163.8 28.3 %collective-permute-start.36 = (bf16[1,96,768]{2,1,0:T(8,128)(2,1)S(1)}, bf16[1,96,768]{2,1,0:T(8,128)(2,1)S(1)}, u32[]{:S(2)}, u32[]{:S(2)}) collective-permute-start(bf16[1,96,768]{2,1,0:T(8,128)(2,1)S(1)} %get-tuple-element.333), channel_id=1, source_target_pairs={{0,16},{1,17},{2,18},{3,19},{4,20},{5,21},{6,22},{7,23},{8,24},{9,... | collective-permute-start | bytes 442376 | tf_op jit(solution)/shard_map/ppermute | solution.py:60
  166.1 26.1 %collective-permute-start.35 = (bf16[1,96,768]{2,1,0:T(8,128)(2,1)S(1)}, bf16[1,96,768]{2,1,0:T(8,128)(2,1)S(1)}, u32[]{:S(2)}, u32[]{:S(2)}) collective-permute-start(bf16[1,96,768]{2,1,0:T(8,128)(2,1)S(1)} %get-tuple-element.334), channel_id=1, source_target_pairs={{0,8},{1,9},{2,10},{3,11},{4,12},{5,13},{6,14},{7,15},{8,0},{9,1},... | collective-permute-start | bytes 442376 | tf_op jit(solution)/shard_map/ppermute | solution.py:60
  167.0 25.2 %collective-permute-start.37 = (bf16[1,96,768]{2,1,0:T(8,128)(2,1)S(1)}, bf16[1,96,768]{2,1,0:T(8,128)(2,1)S(1)}, u32[]{:S(2)}, u32[]{:S(2)}) collective-permute-start(bf16[1,96,768]{2,1,0:T(8,128)(2,1)S(1)} %get-tuple-element.335), channel_id=1, source_target_pairs={{0,24},{1,25},{2,26},{3,27},{4,28},{5,29},{6,30},{7,31},{8,16},{9,... | collective-permute-start | bytes 442376 | tf_op jit(solution)/shard_map/ppermute | solution.py:60
  168.3 25.7 %collective-permute-start.33 = (bf16[8,96,1024]{2,1,0:T(8,128)(2,1)}, bf16[8,96,1024]{2,1,0:T(8,128)(2,1)S(1)}, u32[]{:S(2)}, u32[]{:S(2)}) collective-permute-start(bf16[8,96,1024]{2,1,0:T(8,128)(2,1)} %get-tuple-element.245), channel_id=1, source_target_pairs={{0,1},{1,0},{2,3},{3,2},{4,5},{5,4},{6,7},{7,6},{8,9},{9,8},{10,11... | collective-permute-start | bytes 4718600 | tf_op jit(solution)/shard_map/ppermute | solution.py:60
  170.5 21.8 %collective-permute-start.34 = (bf16[8,96,1024]{2,1,0:T(8,128)(2,1)S(1)}, bf16[8,96,1024]{2,1,0:T(8,128)(2,1)S(1)}, u32[]{:S(2)}, u32[]{:S(2)}) collective-permute-start(bf16[8,96,1024]{2,1,0:T(8,128)(2,1)S(1)} %add_convert_fusion), channel_id=1, source_target_pairs={{0,2},{1,5},{2,0},{3,7},{4,6},{5,1},{6,4},{7,3},{8,10},{9,13},{10,... | collective-permute-start | bytes 4718600 | tf_op jit(solution)/shard_map/ppermute | solution.py:60
  213.4 14.5 %collective-permute-start.44 = (bf16[8,96,640]{2,1,0:T(8,128)(2,1)S(1)}, bf16[8,96,640]{2,1,0:T(8,128)(2,1)S(1)}, u32[]{:S(2)}, u32[]{:S(2)}) collective-permute-start(bf16[8,96,640]{2,1,0:T(8,128)(2,1)S(1)} %add_convert_fusion.2), channel_id=1, source_target_pairs={{0,2},{1,5},{2,0},{3,7},{4,6},{5,1},{6,4},{7,3},{8,10},{9,13},{10,... | collective-permute-start | bytes 2949128 | tf_op jit(solution)/shard_map/ppermute | solution.py:60
  214.0 13.8 %collective-permute-start.41 = (bf16[8,96,640]{2,1,0:T(8,128)(2,1)S(1)}, bf16[8,96,640]{2,1,0:T(8,128)(2,1)S(1)}, u32[]{:S(2)}, u32[]{:S(2)}) collective-permute-start(bf16[8,96,640]{2,1,0:T(8,128)(2,1)S(1)} %copy-done.42), channel_id=1, source_target_pairs={{0,1},{1,0},{2,3},{3,2},{4,5},{5,4},{6,7},{7,6},{8,9},{9,8},{10,11... | collective-permute-start | bytes 2949128 | tf_op jit(solution)/shard_map/ppermute | solution.py:60
  237.8 15.2 %collective-permute-start.53 = (bf16[1,96,640]{2,1,0:T(8,128)(2,1)S(1)}, bf16[1,96,640]{2,1,0:T(8,128)(2,1)S(1)}, u32[]{:S(2)}, u32[]{:S(2)}) collective-permute-start(bf16[1,96,640]{2,1,0:T(8,128)(2,1)S(1)} %get-tuple-element.336), channel_id=1, source_target_pairs={{0,24},{1,25},{2,26},{3,27},{4,28},{5,29},{6,30},{7,31},{8,16},{9,... | collective-permute-start | bytes 368648 | tf_op jit(solution)/shard_map/ppermute | solution.py:60
  (76 other events, 611.8 us)

commit v4 on v3

--- a/solution.py
+++ b/solution.py
@@ -19,7 +19,8 @@
 SHAMPOO_RATE = 0.3
 NORM_RATE = 0.5
 TILE = 256
-VMEM_BYTES = 56 * 1024 * 1024
+VMEM_BYTES = 53 * 1024 * 1024
+SMALL_BYTES = 20 * 1024 * 1024
 F32 = jnp.float32
 BF16 = jnp.bfloat16
 
@@ -134,6 +135,24 @@
         self.going = add_low(*(term[half:] for term in terms))
         self.keep = add_low(*(term[:half] for term in terms))
         self.received = swap(self.going, self.near[0])
+
+    def far_half(self, *earlier):
+        if far_digits(self.count) != [(8, 4)]:
+            return self.far(*earlier)
+        (received,) = after([self.received], *earlier)
+        terms = self.keep, received
+        going = add_low(*(term[2:] for term in terms))
+        self.keep = add_low(*(term[:2] for term in terms))
+        self.received = swap(going, far_steps(self.count, 8, 4)[1])
+        self.going = going
+
+    def far_rest(self, *earlier):
+        if far_digits(self.count) != [(8, 4)]:
+            return
+        (received,) = after([self.received], *earlier)
+        going = add_low(self.keep[1:], received[1:])
+        self.keep = [self.keep, received, swap(going, far_steps(self.count, 8, 4)[0])]
+        self.going = going
 
     def far(self, *earlier):
         (received,) = after([self.received], *earlier)
@@ -188,9 +207,9 @@
         block = source.at[pl.ds(pl.multiple_of(p * rows, 16), rows), :]
         for i, part in enumerate(parts):
 
-            @pl.when(jnp.logical_and(position >= i * size, position < (i + 1) * size))
+            @pl.when((position // size) % len(parts) == i)
             def _():
-                pltpu.make_async_copy(block, part.at[position - i * size], sem).start()
+                pltpu.make_async_copy(block, part.at[position % size], sem).start()
 
         return carry
 
@@ -276,10 +295,11 @@
     return jnp.where(slot.astype(F32) < wide, 1.0, 0.0)[:, 0:1]
 
 
-def first_norm(x_ref, norm_ref, *rest):
-    h1_ref = rest[-1]
+def first_norm(x_ref, norm_ref, h1_ref, turned_ref):
     n1, _ = normalize(x_ref[...].astype(F32))
-    h1_ref[...] = (n1 * norm_ref[0:1, :] + norm_ref[1:2, :]).astype(BF16)
+    h1 = (n1 * norm_ref[0:1, :] + norm_ref[1:2, :]).astype(BF16)
+    h1_ref[...] = h1
+    turned_ref[...] = h1.T
 
 
 def attention_forward(
@@ -514,6 +534,20 @@
         slots[slot, :, first:last] = dot(across[...], right[...], 1, 0).astype(BF16)
         first = last
     store_blocks(places, slots.at[slot], group, groups, parts, sems.at[slot])
+    finish_blocks(slots, sems, group, groups, slot)
+
+
+def turned_gradient(places, left_ref, right_ref, g0, g1, g2, g3, slots, sems):
+    group = pl.program_id(0)
+    groups = pl.num_programs(0)
+    slot = group % 2
+
+    @pl.when(group >= 2)
+    def _():
+        drain(slots, sems, slot)
+
+    slots[slot] = dot(left_ref[...], right_ref[...], 1, 0).astype(BF16)
+    store_blocks(places, slots.at[slot], group, groups, (g0, g1, g2, g3), sems.at[slot])
     finish_blocks(slots, sems, group, groups, slot)
 
 
@@ -734,8 +768,8 @@
     return pl.BlockSpec(shape, lambda i: (0,) * len(shape))
 
 
-def params():
-    return pltpu.CompilerParams(vmem_limit_bytes=VMEM_BYTES)
+def params(limit=VMEM_BYTES):
+    return pltpu.CompilerParams(vmem_limit_bytes=limit)
 
 
 def cost(flops, bytes_accessed):
@@ -750,7 +784,7 @@
     return shape_of(rows, rows, dtype=F32), shape_of(cols, cols, dtype=F32)
 
 
-def shampoo(kernel, terms, masters, shapes, stats):
+def shampoo(kernel, terms, masters, shapes, stats, limit=VMEM_BYTES):
     rows, cols = terms[0].shape[1:]
     out_shape = []
     for master, (left, right) in zip(masters, shapes):
@@ -763,7 +797,7 @@
         in_specs=[pl.BlockSpec((1, rows, cols), lambda i: (0, 0, 0))] * len(terms)
         + [WHOLE] * (len(masters) + len(stats)),
         out_specs=(WHOLE,) * len(out_shape),
-        compiler_params=params(),
+        compiler_params=params(limit),
         cost_estimate=cost(4 * rows * cols * cols, 12 * cols * cols),
         name=kernel.__name__,
     )(*terms, *masters, *(stat[0, 0] for stat in stats))
@@ -834,10 +868,10 @@
         whole = whole.transpose(1, 0, 2, 3).reshape(groups, width, whole.shape[-1])
         return tuple(jnp.split(whole, 4, axis=0))
 
+    plain = jnp.arange(groups, dtype=jnp.int32)
     if direct:
         kernel_far, kernel_near = far_places, near_places
     else:
-        plain = jnp.arange(groups, dtype=jnp.int32)
         kernel_far = kernel_near = jnp.concatenate([plain, plain, jnp.zeros(1, jnp.int32)])
     block_rows = owned if direct else width
     quarter = (count if direct else groups) // 4
@@ -893,12 +927,12 @@
     x_ready, live_keys, counts, kernel_far, kernel_near = after(
         [x, live_keys, counts, kernel_far, kernel_near], gather_attention.held
     )
-    h1 = pl.pallas_call(
+    h1, h1_turned = pl.pallas_call(
         first_norm,
         grid=(tiles,),
         in_specs=[rows_of(width), norm_spec],
-        out_specs=rows_of(width),
-        out_shape=shape_of(rows, width),
+        out_specs=(rows_of(width), pl.BlockSpec((width, TILE), lambda i: (0, i))),
+        out_shape=(shape_of(rows, width), shape_of(width, rows)),
         compiler_params=params(),
         cost_estimate=cost(1, 100e6),
         name="first_norm",
@@ -1021,10 +1055,10 @@
             SMEM, rows_of(width, seq_tile), rows_of(groups * ff, seq_tile), rows_of(groups * ff),
             count_spec, rows_of(width), norm_spec, ANY, ANY, ANY, ANY,
         ],
-        out_specs=(rows_of(groups * ff), rows_of(width), rows_of(width), fixed((8, width))),
+        out_specs=(rows_of(groups * ff), rows_of(width), rows_of(width), fixed((2, width))),
         out_shape=(
             shape_of(rows, groups * ff), shape_of(rows, width, dtype=F32), shape_of(rows, width),
-            shape_of(8, width, dtype=F32),
+            shape_of(2, width, dtype=F32),
         ),
         scratch_shapes=weight_scratch(ff),
         compiler_params=params(),
@@ -1059,7 +1093,7 @@
     up_parts = gradient("up_gradient", (h2_ready, dup), (dmid_low, heads))
     *up_parts, sum_down.received = join(*up_parts, sum_down.received)
     sum_up = sum_of(up_parts)
-    sum_down.far()
+    sum_down.far_half()
     (sum_up.from_across,) = after([sum_up.from_across], sum_down.going)
     sum_up.second()
 
@@ -1071,10 +1105,10 @@
             SMEM, rows_of(width), keys_spec, norm_spec, rows_of(3 * width), lse_spec,
             rows_of(width), rows_of(width), ANY, ANY, ANY, ANY,
         ],
-        out_specs=(rows_of(groups * 5 * LANES), rows_of(width), fixed((8, width))),
+        out_specs=(rows_of(groups * 5 * LANES), rows_of(width), fixed((2, width))),
         out_shape=(
             shape_of(rows, groups * 5 * LANES), shape_of(rows, width, dtype=F32),
-            shape_of(8, width, dtype=F32),
+            shape_of(2, width, dtype=F32),
         ),
         scratch_shapes=weight_scratch(packed),
         compiler_params=params(),
@@ -1085,17 +1119,33 @@
     def exchanged(values, bit):
         return swap(values, [i ^ bit for i in range(count)])
 
-    sums_one, sum_up.received, sum_down.keep = join(sums_one, sum_up.received, sum_down.keep)
-    norm_sum = jnp.concatenate([sums_one[:2], sums_two[:2]], axis=0)
+    if far_digits(count) == [(8, 4)]:
+        sums_one, sum_up.received, sum_down.received = join(
+            sums_one, sum_up.received, sum_down.received
+        )
+    sum_down.far_rest()
+    norm_sum = jnp.concatenate([sums_one, sums_two], axis=0)
     received = exchanged(norm_sum, 1)
     sum_up.first()
     (received,) = after([received], sum_up.going)
     norm_sum = norm_sum + received
     received = exchanged(norm_sum, 8)
-    (h1_ready,) = after([h1], sum_up.going, norm_sum)
-    attention_parts = gradient("attention_gradient", (h1_ready, dproj))
-    *attention_parts, received, sum_up.received = join(
-        *attention_parts, received, sum_up.received
+    (h1_ready,) = after([h1_turned], sum_up.going, sum_down.going, norm_sum)
+    attention_parts = pl.pallas_call(
+        turned_gradient,
+        grid=(groups,),
+        in_specs=[
+            SMEM, fixed((width, rows)), pl.BlockSpec((rows, 5 * LANES), lambda i: (0, i))
+        ],
+        out_specs=(ANY,) * 4,
+        out_shape=quarters_of(5 * LANES),
+        scratch_shapes=[pltpu.VMEM((2, width, 5 * LANES), BF16), pltpu.SemaphoreType.DMA((2,))],
+        compiler_params=params(),
+        cost_estimate=cost(2 * rows * width * groups * 900, 10e6),
+        name="attention_gradient",
+    )(kernel_far, h1_ready, dproj)
+    *attention_parts, received, sum_up.received, sum_down.keep[-1] = join(
+        *attention_parts, received, sum_up.received, sum_down.keep[-1]
     )
     norm_sum = norm_sum + received
     sum_attention = sum_of(attention_parts)
@@ -1150,7 +1200,7 @@
     qkv_turned = w_qkv.transpose(1, 0, 2)
     grad_qkv, qkv_left_new, qkv_right_new, qkv_new = shampoo(
         attention_shampoo, sum_attention.keep, (qkv_turned,), ((owned, 3 * w_qkv.shape[2]),),
-        (qkv_left, qkv_right, qkv_left_root, qkv_right_root),
+        (qkv_left, qkv_right, qkv_left_root, qkv_right_root), limit=SMALL_BYTES,
     )
     grad_qkv, qkv_new = grad_qkv.transpose(1, 0, 2), qkv_new.transpose(1, 0, 2)
     (

time: 259 us -> 248 us (0.958)
  Pallas kernels: 132 us -> 126 us
  waiting for transfers between devices: 47 us -> 51 us
  starting transfers between devices: 57.1 us -> 53.5 us
  local copies, waits for them, and re-layouts: 8.29 us -> 5.22 us
    pallas_call x2 -> x1, Pallas kernels: 21.6 us -> 12.4 us  [gradient(): pl.pallas_call(weight_gradient, grid=(groups,), in_specs=[SMEM] + [spec f...]
    pallas_call x0 -> x1, Pallas kernels: none -> 8.94 us  [per_device(): pl.pallas_call(turned_gradient, grid=(groups,), in_specs=[SMEM, fixed((wi...]
    ppermute x54 -> x53, waiting for transfers between devices: 47 us -> 51 us  [swap(): return lax.ppermute(values, AXES, list(enumerate(step)))]
    ppermute x54 -> x53, starting transfers between devices: 57.1 us -> 53.5 us  [swap(): return lax.ppermute(values, AXES, list(enumerate(step)))]
    convert_element_type x9 -> x10, other arithmetic: 6.19 us -> 5.55 us  [add_low(): return sum((term.astype(F32) for term in terms)).astype(BF16)]
  transfers between devices with their start and end apart: 54 -> 53, of which waited for: 16 -> 18; matrix products, arithmetic and copies ran while one was open for 4% -> 3% of each run, Pallas kernels for 46% -> 47%
where the time goes in v4:
time: 248 us; the launch traced here: 247 us
  Pallas kernels  126 us (51%)
  starting transfers between devices  53.5 us (22%)
  waiting for transfers between devices  51 us (21%)
  other arithmetic  9.04 us (4%)
  local copies, waits for them, and re-layouts  5.22 us (2%)
    ppermute x53, starting transfers between devices, swap(): return lax.ppermute(values, AXES, list(enumerate(step)))  53.5 us
    ppermute x53, waiting for transfers between devices, swap(): return lax.ppermute(values, AXES, list(enumerate(step)))  51 us
    pallas_call x1, Pallas kernels, per_device(): pl.pallas_call(functools.partial(attention_backward, seq_len=seq_len), gr...  20.5 us
    pallas_call x1, Pallas kernels, per_device(): pl.pallas_call(functools.partial(attention_forward, seq_len=seq_len), gri...  16 us
    pallas_call x1, Pallas kernels, per_device(): pl.pallas_call(functools.partial(up_forward, seq_len=seq_len), grid=(tile...  15.7 us
    pallas_call x1, Pallas kernels, per_device(): pl.pallas_call(functools.partial(mlp_backward, seq_len=seq_len), grid=(ti...  12.9 us
    pallas_call x1, Pallas kernels, gradient(): pl.pallas_call(weight_gradient, grid=(groups,), in_specs=[SMEM] + [spec f...  12.4 us
    pallas_call x3, Pallas kernels, shampoo(): pl.pallas_call(kernel, grid=(1,), out_shape=tuple(out_shape), in_specs=[p...  11.9 us
  transfers between devices with their start and end apart: 53, of which 18 were waited for; matrix products, arithmetic and copies ran while one was open for 3% of the time, Pallas kernels for 47%

profile of v4, /device:TPU:0, one launch (start us, length us, event | category | flops | bytes accessed | tf_op | source)
XLA Modules:
  0.0 246.9 jit_solution(3557547628043488454)
XLA Ops:
  2.9 5.1 %collective-permute-start.2 = (bf16[1,96,768]{2,1,0:T(8,128)(2,1)S(1)}, bf16[1,96,768]{2,1,0:T(8,128)(2,1)S(1)}, u32[]{:S(2)}, u32[]{:S(2)}) collective-permute-start(bf16[1,96,768]{2,1,0:T(8,128)(2,1)S(1)} %bitcast.78), channel_id=1, source_target_pairs={{0,24},{1,25},{2,26},{3,27},{4,28},{5,29},{6,30},{7,31},{8,16},{9,... | collective-permute-start | bytes 442376 | tf_op jit(solution)/shard_map/ppermute | solution.py:61
  15.6 4.9 %collective-permute-done.1 = bf16[1,96,768]{2,1,0:T(8,128)(2,1)S(1)} collective-permute-done((bf16[1,96,768]{2,1,0:T(8,128)(2,1)S(1)}, bf16[1,96,768]{2,1,0:T(8,128)(2,1)S(1)}, u32[]{:S(2)}, u32[]{:S(2)}) %collective-permute-start.1) | collective-permute-done | bytes 147488 | tf_op jit(solution)/shard_map/ppermute | solution.py:61
  22.4 4.4 %first_norm.1 = (bf16[1024,768]{1,0:T(8,128)(2,1)}, bf16[768,1024]{1,0:T(8,128)(2,1)}) custom-call(bf16[1024,768]{1,0:T(8,128)(2,1)} %bitcast.75, f32[4,768]{1,0:T(4,128)S(1)} %bitcast.67), custom_call_target="tpu_custom_call" | custom-call | flops 4 | bytes 100000000 | tf_op jit(solution)/shard_map/first_norm/pallas_call | solution.py:930
  26.9 3.6 %collective-permute-done.8 = bf16[4,96,768]{2,1,0:T(8,128)(2,1)S(1)} collective-permute-done((bf16[4,96,768]{2,1,0:T(8,128)(2,1)S(1)}, bf16[4,96,768]{2,1,0:T(8,128)(2,1)S(1)}, u32[]{:S(2)}, u32[]{:S(2)}) %collective-permute-start.8) | collective-permute-done | bytes 589856 | tf_op jit(solution)/shard_map/ppermute | solution.py:61
  32.2 2.6 %collective-permute-start.7 = (bf16[1,96,768]{2,1,0:T(8,128)(2,1)S(1)}, bf16[1,96,768]{2,1,0:T(8,128)(2,1)S(1)}, u32[]{:S(2)}, u32[]{:S(2)}) collective-permute-start(bf16[1,96,768]{2,1,0:T(8,128)(2,1)S(1)} %convert_bitcast_fusion), channel_id=1, source_target_pairs={{0,24},{1,25},{2,26},{3,27},{4,28},{5,29},{6,30},{7,31},{8,16},{9,... | collective-permute-start | bytes 442376 | tf_op jit(solution)/shard_map/ppermute | solution.py:61
  36.7 4.1 %collective-permute-done.7 = bf16[1,96,768]{2,1,0:T(8,128)(2,1)S(1)} collective-permute-done((bf16[1,96,768]{2,1,0:T(8,128)(2,1)S(1)}, bf16[1,96,768]{2,1,0:T(8,128)(2,1)S(1)}, u32[]{:S(2)}, u32[]{:S(2)}) %collective-permute-start.7) | collective-permute-done | bytes 147488 | tf_op jit(solution)/shard_map/ppermute | solution.py:61
  40.8 4.9 %collective-permute-done.6 = bf16[1,96,768]{2,1,0:T(8,128)(2,1)S(1)} collective-permute-done((bf16[1,96,768]{2,1,0:T(8,128)(2,1)S(1)}, bf16[1,96,768]{2,1,0:T(8,128)(2,1)S(1)}, u32[]{:S(2)}, u32[]{:S(2)}) %collective-permute-start.6) | collective-permute-done | bytes 147488 | tf_op jit(solution)/shard_map/ppermute | solution.py:61
  48.3 2.5 %collective-permute-start.15 = (bf16[2,96,768]{2,1,0:T(8,128)(2,1)S(1)}, bf16[2,96,768]{2,1,0:T(8,128)(2,1)S(1)}, u32[]{:S(2)}, u32[]{:S(2)}) collective-permute-start(bf16[2,96,768]{2,1,0:T(8,128)(2,1)S(1)} %pad_maximum_fusion.1), channel_id=1, source_target_pairs={{0,24},{1,25},{2,26},{3,27},{4,28},{5,29},{6,30},{7,31},{8,16},{9,... | collective-permute-start | bytes 884744 | tf_op jit(solution)/shard_map/ppermute | solution.py:61
  50.9 5.8 %collective-permute-done.10 = bf16[4,96,768]{2,1,0:T(8,128)(2,1)S(1)} collective-permute-done((bf16[4,96,768]{2,1,0:T(8,128)(2,1)S(1)}, bf16[4,96,768]{2,1,0:T(8,128)(2,1)S(1)}, u32[]{:S(2)}, u32[]{:S(2)}) %collective-permute-start.10) | collective-permute-done | bytes 589856 | tf_op jit(solution)/shard_map/ppermute | solution.py:61
  58.5 16.0 %attention_forward.1 = (bf16[1024,2304]{1,0:T(8,128)(2,1)}, bf16[1024,1024]{1,0:T(8,128)(2,1)}, f32[8,8,256]{2,1,0:T(8,128)S(1)}, f32[1024,768]{1,0:T(8,128)}, bf16[1024,768]{1,0:T(8,128)(2,1)}) custom-call(s32[65]{0:T(128)S(1)} %get-tuple-element.179.order.places, bf16[1024,768]{1,0:T(8,128)(2,1)} %bitcast.76, bf16[1024,768]{1,0:T(8,128)(2,1)} %get-tuple-element.189.h1_ref, ...), custom_call_target="tpu_custom_call" | custom-call | flops 22649241600 | bytes 12000000 | tf_op jit(solution)/shard_map/attention_forward/pallas_call | solution.py:956
  81.7 15.7 %up_forward.1 = (bf16[1024,3072]{1,0:T(8,128)(2,1)}, bf16[1024,3072]{1,0:T(8,128)(2,1)}, bf16[64,3072]{1,0:T(8,128)(2,1)S(1)}) custom-call(s32[65]{0:T(128)S(1)} %get-tuple-element.179.order.places, bf16[1024,768]{1,0:T(8,128)(2,1)} %get-tuple-element.224.h2_ref.refs_0_, f32[64,128]{1,0:T(8,128)S(1)} %broadcast_in_dim.50.count_ref, ...), custom_call_target="tpu_custom_call" | custom-call | flops 19327352832 | bytes 20000000 | tf_op jit(solution)/shard_map/up_forward/pallas_call | solution.py:983
  101.5 11.1 %down_forward.1 = (bf16[1024,768]{1,0:T(8,128)(2,1)}, f32[64,768]{1,0:T(8,128)S(1)}) custom-call(s32[65]{0:T(128)S(1)} %get-tuple-element.178.order, bf16[1024,3072]{1,0:T(8,128)(2,1)} %get-tuple-element.206.hid_ref, f32[1024,768]{1,0:T(8,128)} %get-tuple-element.207.mid_ref, f32[64,128]{1,0:T(8,128)S(1)} %broadcast_in_dim.50.count_ref, ...), custom_call_target="tpu_custom_call" | custom-call | flops 19327352832 | bytes 20000000 | tf_op jit(solution)/shard_map/down_forward/pallas_call | solution.py:1004
  115.9 8.2 %loss_backward.1 = (f32[64,128]{1,0:T(8,128)S(1)}, f32[64,768]{1,0:T(8,128)S(1)}, bf16[64,768]{1,0:T(8,128)(2,1)S(1)}, bf16[8,96,768]{2,1,0:T(8,128)(2,1)}, bf16...) custom-call(s32[65]{0:T(128)S(1)} %get-tuple-element.179.order.places, ...), custom_call_target="tpu_custom_call" | custom-call | flops 4831838208 | bytes 20000000 | tf_op jit(solution)/shard_map/loss_backward/pallas_call | solution.py:1022
  124.6 4.4 %down_backward.1.by_seq_ref = f32[64,3072]{1,0:T(8,128)S(1)} custom-call(s32[65]{0:T(128)S(1)} %get-tuple-element.178.order, bf16[64,768]{1,0:T(8,128)(2,1)S(1)} %get-tuple-element.216.low_ref, bf16[8,96,768]{2,1,0:T(8,128)(2,1)} %copy-done.25, bf16[8,96,768]{2,1,0:T(8,128)(2,1)} %copy-done.42, bf16[8,96,768]{2,1,0:T(8,128)(2,1)} %copy-done.41, ...), custom_call_target="tpu_custom_call" | custom-call | flops 4831838208 | bytes 6000000 | tf_op jit(solution)/shard_map/down_backward/pallas_call | solution.py:1037
  130.9 12.9 %mlp_backward.1 = (bf16[1024,3072]{1,0:T(8,128)(2,1)}, f32[1024,768]{1,0:T(8,128)}, bf16[1024,768]{1,0:T(8,128)(2,1)}, f32[2,768]{1,0:T(2,128)S(1)}) custom-call(s32[65]{0:T(128)S(1)} %get-tuple-element.179.order.places, f32[64,768]{1,0:T(8,128)S(1)} %get-tuple-element.219.grad_ref, f32[64,3072]{1,0:T(8,128)} %copy-done.13, ...), custom_call_target="tpu_custom_call" | custom-call | flops 19327352832 | bytes 25000000 | tf_op jit(solution)/shard_map/mlp_backward/pallas_call | solution.py:1051
  147.8 12.4 %up_gradient.1 = (bf16[8,96,1024]{2,1,0:T(8,128)(2,1)}, bf16[8,96,1024]{2,1,0:T(8,128)(2,1)}, bf16[8,96,1024]{2,1,0:T(8,128)(2,1)}, bf16[8,96,1024]{2,1,0:T(8,128)(2,1)}) custom-call(s32[65]{0:T(128)S(1)} %get-tuple-element.179.order.places, bf16[1024,768]{1,0:T(8,128)(2,1)} %get-tuple-element.224.h2_ref.refs_0_, ...), custom_call_target="tpu_custom_call" | custom-call | flops 22649241600 | bytes 10000000 | tf_op jit(solution)/shard_map/up_gradient/pallas_call | solution.py:1071
  165.7 20.5 %attention_backward.1 = (bf16[1024,2560]{1,0:T(8,128)(2,1)}, f32[1024,768]{1,0:T(8,128)}, f32[2,768]{1,0:T(2,128)S(1)}) custom-call(s32[65]{0:T(128)S(1)} %get-tuple-element.179.order.places, bf16[1024,768]{1,0:T(8,128)(2,1)} %bitcast.77, f32[8,16,256]{2,1,0:T(8,128)S(1)} %pad_maximum_fusion.3.live_ref, f32[4,768]{1,0:T(4,128)S(1)} %bitcast.70, ...), custom_call_target="tpu_custom_call" | custom-call | flops 32715571200 | bytes 20000000 | tf_op jit(solution)/shard_map/attention_backward/pallas_call | solution.py:1101
  190.5 8.9 %attention_gradient.1 = (bf16[8,96,640]{2,1,0:T(8,128)(2,1)}, bf16[8,96,640]{2,1,0:T(8,128)(2,1)}, bf16[8,96,640]{2,1,0:T(8,128)(2,1)}, bf16[8,96,640]{2,1,0:T(8,128)(2,1)}) custom-call(s32[65]{0:T(128)S(1)} %get-tuple-element.179.order.places, bf16[768,1024]{1,0:T(8,128)(2,1)} %get-tuple-element.251.left_ref, bf16[1024,2560]{1,0:T(8,128)(2,1)} %get-tuple-element.252.right_ref), custom_call_target="tpu_custom_call" | custom-call | flops 22649241600 | bytes 10000000 | tf_op jit(solution)/shard_map/attention_gradient/pallas_call | solution.py:1134
  202.5 2.8 %collective-permute-done.42 = f32[4,768]{1,0:T(4,128)S(1)} collective-permute-done((f32[4,768]{1,0:T(4,128)S(1)}, f32[4,768]{1,0:T(4,128)S(1)}, u32[]{:S(2)}, u32[]{:S(2)}) %collective-permute-start.42) | collective-permute-done | bytes 12320 | tf_op jit(solution)/shard_map/ppermute | solution.py:61
  212.7 4.7 %shampoo_kernel.1 = (f32[96,768]{1,0:T(8,128)}, f32[96,96]{1,0:T(8,128)}, f32[768,768]{1,0:T(8,128)}, f32[96,768]{1,0:T(8,128)}) custom-call(bf16[2,96,768]{2,1,0:T(8,128)(2,1)S(1)} %get-tuple-element.267.refs_0_, bf16[2,96,768]{2,1,0:T(8,128)(2,1)S(1)} %collective-permute-done.35.refs_1_, bf16[1,96,768]{2,1,0:T(8,128)(2,1)S(1)} %collective-permute-done.39.refs_2_, ...), custom_call_target="tpu_custom_call" | custom-call | flops 905969664 | bytes 7077888 | tf_op jit(solution)/shard_map/shampoo_kernel/pallas_call | solution.py:793
  217.4 3.8 %collective-permute-done.44 = f32[4,768]{1,0:T(4,128)S(1)} collective-permute-done((f32[4,768]{1,0:T(4,128)S(1)}, f32[4,768]{1,0:T(4,128)S(1)}, u32[]{:S(2)}, u32[]{:S(2)}) %collective-permute-start.44) | collective-permute-done | bytes 12320 | tf_op jit(solution)/shard_map/ppermute | solution.py:61
  226.9 4.2 %collective-permute-done.48.refs_4_ = bf16[1,96,1024]{2,1,0:T(8,128)(2,1)S(1)} collective-permute-done((bf16[1,96,1024]{2,1,0:T(8,128)(2,1)}, bf16[1,96,1024]{2,1,0:T(8,128)(2,1)S(1)}, u32[]{:S(2)}, u32[]{:S(2)}) %collective-permute-start.48) | collective-permute-done | bytes 196640 | tf_op jit(solution)/shard_map/ppermute | solution.py:61
  231.2 2.4 collective-permute-start.52
  236.1 5.3 %up_shampoo.1 = (f32[96,768]{1,0:T(8,128)}, f32[96,96]{1,0:T(8,128)}, f32[768,768]{1,0:T(8,128)}, f32[96,768]{1,0:T(8,128)}, f32[96,192]{1,0:T(8,128)}, /*index=...) custom-call(bf16[4,96,1024]{2,1,0:T(8,128)(2,1)} %copy-done.14, bf16[4,96,1024]{2,1,0:T(8,128)(2,1)} %copy-done.15, ...), custom_call_target="tpu_custom_call" | custom-call | flops 1610612736 | bytes 12582912 | tf_op jit(solution)/shard_map/up_shampoo/pallas_call | solution.py:793
  (258 shorter events, 74.0 us)
Async XLA Ops:
  30.6 16.3 %collective-permute-start.9 = (bf16[8,96,768]{2,1,0:T(8,128)(2,1)S(1)}, bf16[8,96,768]{2,1,0:T(8,128)(2,1)S(1)}, u32[]{:S(2)}, u32[]{:S(2)}) collective-permute-start(bf16[8,96,768]{2,1,0:T(8,128)(2,1)S(1)} %constant_dynamic-update-slice_fusion.w0), channel_id=1, source_target_pairs={{0,2},{1,5},{2,0},{3,7},{4,6},{5,1},{6,4},{7,3},{8,10},{9,13},{10,... | collective-permute-start | bytes 3538952 | tf_op jit(solution)/shard_map/ppermute | solution.py:61
  36.6 20.2 %collective-permute-start.11 = (bf16[8,96,768]{2,1,0:T(8,128)(2,1)S(1)}, bf16[8,96,768]{2,1,0:T(8,128)(2,1)S(1)}, u32[]{:S(2)}, u32[]{:S(2)}) collective-permute-start(bf16[8,96,768]{2,1,0:T(8,128)(2,1)S(1)} %constant_dynamic-update-slice_fusion.w0), channel_id=1, source_target_pairs={{0,1},{1,0},{2,3},{3,2},{4,5},{5,4},{6,7},{7,6},{8,9},{9,8},{10,11... | collective-permute-start | bytes 3538952 | tf_op jit(solution)/shard_map/ppermute | solution.py:61
  48.3 26.2 %collective-permute-start.15 = (bf16[2,96,768]{2,1,0:T(8,128)(2,1)S(1)}, bf16[2,96,768]{2,1,0:T(8,128)(2,1)S(1)}, u32[]{:S(2)}, u32[]{:S(2)}) collective-permute-start(bf16[2,96,768]{2,1,0:T(8,128)(2,1)S(1)} %pad_maximum_fusion.1), channel_id=1, source_target_pairs={{0,24},{1,25},{2,26},{3,27},{4,28},{5,29},{6,30},{7,31},{8,16},{9,... | collective-permute-start | bytes 884744 | tf_op jit(solution)/shard_map/ppermute | solution.py:61
  50.9 24.7 %collective-permute-start.14 = (bf16[2,96,768]{2,1,0:T(8,128)(2,1)S(1)}, bf16[2,96,768]{2,1,0:T(8,128)(2,1)S(1)}, u32[]{:S(2)}, u32[]{:S(2)}) collective-permute-start(bf16[2,96,768]{2,1,0:T(8,128)(2,1)S(1)} %pad_maximum_fusion.1), channel_id=1, source_target_pairs={{0,16},{1,17},{2,18},{3,19},{4,20},{5,21},{6,22},{7,23},{8,24},{9,... | collective-permute-start | bytes 884744 | tf_op jit(solution)/shard_map/ppermute | solution.py:61
  56.7 18.9 %collective-permute-start.13 = (bf16[2,96,768]{2,1,0:T(8,128)(2,1)S(1)}, bf16[2,96,768]{2,1,0:T(8,128)(2,1)S(1)}, u32[]{:S(2)}, u32[]{:S(2)}) collective-permute-start(bf16[2,96,768]{2,1,0:T(8,128)(2,1)S(1)} %pad_maximum_fusion.1), channel_id=1, source_target_pairs={{0,8},{1,9},{2,10},{3,11},{4,12},{5,13},{6,14},{7,15},{8,0},{9,1},... | collective-permute-start | bytes 884744 | tf_op jit(solution)/shard_map/ppermute | solution.py:61
  56.8 23.5 %collective-permute-start.17 = (bf16[8,96,768]{2,1,0:T(8,128)(2,1)S(1)}, bf16[8,96,768]{2,1,0:T(8,128)(2,1)S(1)}, u32[]{:S(2)}, u32[]{:S(2)}) collective-permute-start(bf16[8,96,768]{2,1,0:T(8,128)(2,1)S(1)} %constant_dynamic-update-slice_fusion.9.w0), channel_id=1, source_target_pairs={{0,1},{1,0},{2,3},{3,2},{4,5},{5,4},{6,7},{7,6},{8,9},{9,8},{10,11... | collective-permute-start | bytes 3538952 | tf_op jit(solution)/shard_map/ppermute | solution.py:61
  56.9 18.8 %collective-permute-start.16 = (bf16[8,96,768]{2,1,0:T(8,128)(2,1)S(1)}, bf16[8,96,768]{2,1,0:T(8,128)(2,1)S(1)}, u32[]{:S(2)}, u32[]{:S(2)}) collective-permute-start(bf16[8,96,768]{2,1,0:T(8,128)(2,1)S(1)} %constant_dynamic-update-slice_fusion.9.w0), channel_id=1, source_target_pairs={{0,2},{1,5},{2,0},{3,7},{4,6},{5,1},{6,4},{7,3},{8,10},{9,13},{10,... | collective-permute-start | bytes 3538952 | tf_op jit(solution)/shard_map/ppermute | solution.py:61
  75.8 21.6 %collective-permute-start.21 = (bf16[2,64,768]{2,1,0:T(8,128)(2,1)S(1)}, bf16[2,64,768]{2,1,0:T(8,128)(2,1)S(1)}, u32[]{:S(2)}, u32[]{:S(2)}) collective-permute-start(bf16[2,64,768]{2,1,0:T(8,128)(2,1)S(1)} %pad_maximum_fusion.2), channel_id=1, source_target_pairs={{0,24},{1,25},{2,26},{3,27},{4,28},{5,29},{6,30},{7,31},{8,16},{9,... | collective-permute-start | bytes 589832 | tf_op jit(solution)/shard_map/ppermute | solution.py:61
  77.4 20.0 %collective-permute-start.20 = (bf16[2,64,768]{2,1,0:T(8,128)(2,1)S(1)}, bf16[2,64,768]{2,1,0:T(8,128)(2,1)S(1)}, u32[]{:S(2)}, u32[]{:S(2)}) collective-permute-start(bf16[2,64,768]{2,1,0:T(8,128)(2,1)S(1)} %pad_maximum_fusion.2), channel_id=1, source_target_pairs={{0,16},{1,17},{2,18},{3,19},{4,20},{5,21},{6,22},{7,23},{8,24},{9,... | collective-permute-start | bytes 589832 | tf_op jit(solution)/shard_map/ppermute | solution.py:61
  78.4 19.1 %collective-permute-start.19 = (bf16[2,64,768]{2,1,0:T(8,128)(2,1)S(1)}, bf16[2,64,768]{2,1,0:T(8,128)(2,1)S(1)}, u32[]{:S(2)}, u32[]{:S(2)}) collective-permute-start(bf16[2,64,768]{2,1,0:T(8,128)(2,1)S(1)} %pad_maximum_fusion.2), channel_id=1, source_target_pairs={{0,8},{1,9},{2,10},{3,11},{4,12},{5,13},{6,14},{7,15},{8,0},{9,1},... | collective-permute-start | bytes 589832 | tf_op jit(solution)/shard_map/ppermute | solution.py:61
  80.3 18.7 %collective-permute-start.23 = (bf16[8,96,768]{2,1,0:T(8,128)(2,1)S(1)}, bf16[8,96,768]{2,1,0:T(8,128)(2,1)S(1)}, u32[]{:S(2)}, u32[]{:S(2)}) collective-permute-start(bf16[8,96,768]{2,1,0:T(8,128)(2,1)S(1)} %constant_dynamic-update-slice_fusion.11.w0), channel_id=1, source_target_pairs={{0,1},{1,0},{2,3},{3,2},{4,5},{5,4},{6,7},{7,6},{8,9},{9,8},{10,11... | collective-permute-start | bytes 3538952 | tf_op jit(solution)/shard_map/ppermute | solution.py:61
  80.4 17.1 %collective-permute-start.22 = (bf16[8,96,768]{2,1,0:T(8,128)(2,1)S(1)}, bf16[8,96,768]{2,1,0:T(8,128)(2,1)S(1)}, u32[]{:S(2)}, u32[]{:S(2)}) collective-permute-start(bf16[8,96,768]{2,1,0:T(8,128)(2,1)S(1)} %constant_dynamic-update-slice_fusion.11.w0), channel_id=1, source_target_pairs={{0,2},{1,5},{2,0},{3,7},{4,6},{5,1},{6,4},{7,3},{8,10},{9,13},{10,... | collective-permute-start | bytes 3538952 | tf_op jit(solution)/shard_map/ppermute | solution.py:61
  97.9 15.1 %collective-permute-start.26 = (bf16[8,64,768]{2,1,0:T(8,128)(2,1)S(1)}, bf16[8,64,768]{2,1,0:T(8,128)(2,1)S(1)}, u32[]{:S(2)}, u32[]{:S(2)}) collective-permute-start(bf16[8,64,768]{2,1,0:T(8,128)(2,1)S(1)} %constant_dynamic-update-slice_fusion.15), channel_id=1, source_target_pairs={{0,1},{1,0},{2,3},{3,2},{4,5},{5,4},{6,7},{7,6},{8,9},{9,8},{10,11... | collective-permute-start | bytes 2359304 | tf_op jit(solution)/shard_map/ppermute | solution.py:61
  98.1 14.5 %collective-permute-start.25 = (bf16[8,64,768]{2,1,0:T(8,128)(2,1)S(1)}, bf16[8,64,768]{2,1,0:T(8,128)(2,1)S(1)}, u32[]{:S(2)}, u32[]{:S(2)}) collective-permute-start(bf16[8,64,768]{2,1,0:T(8,128)(2,1)S(1)} %constant_dynamic-update-slice_fusion.15), channel_id=1, source_target_pairs={{0,2},{1,5},{2,0},{3,7},{4,6},{5,1},{6,4},{7,3},{8,10},{9,13},{10,... | collective-permute-start | bytes 2359304 | tf_op jit(solution)/shard_map/ppermute | solution.py:61
  124.4 21.7 %collective-permute-start.28 = (bf16[8,96,768]{2,1,0:T(8,128)(2,1)}, bf16[8,96,768]{2,1,0:T(8,128)(2,1)S(1)}, u32[]{:S(2)}, u32[]{:S(2)}) collective-permute-start(bf16[8,96,768]{2,1,0:T(8,128)(2,1)} %get-tuple-element.213), channel_id=1, source_target_pairs={{0,1},{1,0},{2,3},{3,2},{4,5},{5,4},{6,7},{7,6},{8,9},{9,8},{10,11... | collective-permute-start | bytes 3538952 | tf_op jit(solution)/shard_map/ppermute | solution.py:61
  129.9 16.2 %collective-permute-start.30 = (bf16[8,96,768]{2,1,0:T(8,128)(2,1)S(1)}, bf16[8,96,768]{2,1,0:T(8,128)(2,1)S(1)}, u32[]{:S(2)}, u32[]{:S(2)}) collective-permute-start(bf16[8,96,768]{2,1,0:T(8,128)(2,1)S(1)} %add_convert_fusion.1), channel_id=1, source_target_pairs={{0,2},{1,5},{2,0},{3,7},{4,6},{5,1},{6,4},{7,3},{8,10},{9,13},{10,... | collective-permute-start | bytes 3538952 | tf_op jit(solution)/shard_map/ppermute | solution.py:61
  146.6 13.5 %collective-permute-start.31 = (bf16[4,96,768]{2,1,0:T(8,128)(2,1)S(1)}, bf16[4,96,768]{2,1,0:T(8,128)(2,1)S(1)}, u32[]{:S(2)}, u32[]{:S(2)}) collective-permute-start(bf16[4,96,768]{2,1,0:T(8,128)(2,1)S(1)} %get-tuple-element.321), channel_id=1, source_target_pairs={{0,4},{1,3},{2,6},{3,1},{4,0},{5,7},{6,2},{7,5},{8,12},{9,11},{10,... | collective-permute-start | bytes 1769480 | tf_op jit(solution)/shard_map/ppermute | solution.py:61
  160.4 25.8 %collective-permute-start.35 = (bf16[2,96,768]{2,1,0:T(8,128)(2,1)S(1)}, bf16[2,96,768]{2,1,0:T(8,128)(2,1)S(1)}, u32[]{:S(2)}, u32[]{:S(2)}) collective-permute-start(bf16[2,96,768]{2,1,0:T(8,128)(2,1)S(1)} %get-tuple-element.328), channel_id=1, source_target_pairs={{0,16},{1,17},{2,18},{3,19},{4,20},{5,21},{6,22},{7,23},{8,24},{9,... | collective-permute-start | bytes 884744 | tf_op jit(solution)/shard_map/ppermute | solution.py:61
  162.2 25.2 %collective-permute-start.33 = (bf16[8,96,1024]{2,1,0:T(8,128)(2,1)}, bf16[8,96,1024]{2,1,0:T(8,128)(2,1)S(1)}, u32[]{:S(2)}, u32[]{:S(2)}) collective-permute-start(bf16[8,96,1024]{2,1,0:T(8,128)(2,1)} %get-tuple-element.244), channel_id=1, source_target_pairs={{0,1},{1,0},{2,3},{3,2},{4,5},{5,4},{6,7},{7,6},{8,9},{9,8},{10,11... | collective-permute-start | bytes 4718600 | tf_op jit(solution)/shard_map/ppermute | solution.py:61
  164.6 21.6 %collective-permute-start.34 = (bf16[8,96,1024]{2,1,0:T(8,128)(2,1)S(1)}, bf16[8,96,1024]{2,1,0:T(8,128)(2,1)S(1)}, u32[]{:S(2)}, u32[]{:S(2)}) collective-permute-start(bf16[8,96,1024]{2,1,0:T(8,128)(2,1)S(1)} %add_convert_fusion), channel_id=1, source_target_pairs={{0,2},{1,5},{2,0},{3,7},{4,6},{5,1},{6,4},{7,3},{8,10},{9,13},{10,... | collective-permute-start | bytes 4718600 | tf_op jit(solution)/shard_map/ppermute | solution.py:61
  186.3 13.2 %collective-permute-start.39 = (bf16[1,96,768]{2,1,0:T(8,128)(2,1)S(1)}, bf16[1,96,768]{2,1,0:T(8,128)(2,1)S(1)}, u32[]{:S(2)}, u32[]{:S(2)}) collective-permute-start(bf16[1,96,768]{2,1,0:T(8,128)(2,1)S(1)} %add_convert_fusion.14), channel_id=1, source_target_pairs={{0,8},{1,9},{2,10},{3,11},{4,12},{5,13},{6,14},{7,15},{8,0},{9,1},... | collective-permute-start | bytes 442376 | tf_op jit(solution)/shard_map/ppermute | solution.py:61
  206.7 14.4 %collective-permute-start.43 = (bf16[8,96,640]{2,1,0:T(8,128)(2,1)S(1)}, bf16[8,96,640]{2,1,0:T(8,128)(2,1)S(1)}, u32[]{:S(2)}, u32[]{:S(2)}) collective-permute-start(bf16[8,96,640]{2,1,0:T(8,128)(2,1)S(1)} %add_convert_fusion.2), channel_id=1, source_target_pairs={{0,2},{1,5},{2,0},{3,7},{4,6},{5,1},{6,4},{7,3},{8,10},{9,13},{10,... | collective-permute-start | bytes 2949128 | tf_op jit(solution)/shard_map/ppermute | solution.py:61
  207.5 13.7 %collective-permute-start.40 = (bf16[8,96,640]{2,1,0:T(8,128)(2,1)S(1)}, bf16[8,96,640]{2,1,0:T(8,128)(2,1)S(1)}, u32[]{:S(2)}, u32[]{:S(2)}) collective-permute-start(bf16[8,96,640]{2,1,0:T(8,128)(2,1)S(1)} %copy-done.44), channel_id=1, source_target_pairs={{0,1},{1,0},{2,3},{3,2},{4,5},{5,4},{6,7},{7,6},{8,9},{9,8},{10,11... | collective-permute-start | bytes 2949128 | tf_op jit(solution)/shard_map/ppermute | solution.py:61
  231.2 13.7 %collective-permute-start.52 = (bf16[1,96,640]{2,1,0:T(8,128)(2,1)S(1)}, bf16[1,96,640]{2,1,0:T(8,128)(2,1)S(1)}, u32[]{:S(2)}, u32[]{:S(2)}) collective-permute-start(bf16[1,96,640]{2,1,0:T(8,128)(2,1)S(1)} %get-tuple-element.329), channel_id=1, source_target_pairs={{0,24},{1,25},{2,26},{3,27},{4,28},{5,29},{6,30},{7,31},{8,16},{9,... | collective-permute-start | bytes 368648 | tf_op jit(solution)/shard_map/ppermute | solution.py:61
  (77 other events, 650.4 us)

commit v5 on v4

--- a/solution.py
+++ b/solution.py
@@ -1149,18 +1149,10 @@
     )
     norm_sum = norm_sum + received
     sum_attention = sum_of(attention_parts)
-    if count > 16:
-        sum_attention.from_across, received = join(
-            sum_attention.from_across, exchanged(norm_sum, 16)
-        )
-        norm_sum = norm_sum + received
     sum_attention.second()
+    (norm_sum,) = after([norm_sum], sum_attention.going)
     sum_up.far(sum_attention.going)
-    bit = 32
-    while bit < count:
-        norm_sum = norm_sum + exchanged(norm_sum, bit)
-        bit *= 2
-    received = exchanged(norm_sum, 2)
+    received = exchanged(norm_sum, 16) if count > 16 else jnp.zeros_like(norm_sum)
     sum_down.keep = after(sum_down.keep, sum_attention.going)
     grad_down, down_left_new, down_right_new, down_new = shampoo(
         shampoo_kernel, sum_down.keep, (w_down,), ((owned, ff),),
@@ -1172,7 +1164,7 @@
     sum_up.keep = [*sooner, sum_up.keep[-1]]
     norm_sum = norm_sum + received
     sum_attention.first()
-    received = exchanged(norm_sum, 4)
+    received = exchanged(norm_sum, 2)
     (sum_up.keep[-1],) = after([sum_up.keep[-1]], sum_attention.going)
     sum_attention.received, sum_up.keep[-1], received = join(
         sum_attention.received, sum_up.keep[-1], received
@@ -1189,7 +1181,12 @@
             out_left, out_right, out_left_root, out_right_root,
         ),
     )
-    (norm_sum,) = after([norm_sum], up_new)
+    bit = 32
+    while bit < count:
+        norm_sum = norm_sum + exchanged(norm_sum, bit)
+        bit *= 2
+    (received,) = after([exchanged(norm_sum, 4)], up_new)
+    norm_sum = norm_sum + received
     grad_norm = lax.dynamic_slice_in_dim(norm_sum, dp_index * owned, owned, 1).T
     norm_second_new = STAT_DECAY * norm_second + (1.0 - STAT_DECAY) * grad_norm * grad_norm
     own_params = lax.dynamic_slice_in_dim(norm_params, dp_index * owned, owned, 0)

time: 248 us -> 246 us (level)
  no operation moved by 1% of the time
where the time goes in v5:
time: 246 us
  Pallas kernels  126 us (51%)
  starting transfers between devices  52.5 us (21%)
  waiting for transfers between devices  50.8 us (21%)
  other arithmetic  9.04 us (4%)
  local copies, waits for them, and re-layouts  5.22 us (2%)
    ppermute x53, starting transfers between devices, swap(): return lax.ppermute(values, AXES, list(enumerate(step)))  52.5 us
    ppermute x53, waiting for transfers between devices, swap(): return lax.ppermute(values, AXES, list(enumerate(step)))  50.8 us
    pallas_call x1, Pallas kernels, per_device(): pl.pallas_call(functools.partial(attention_backward, seq_len=seq_len), gr...  20.5 us
    pallas_call x1, Pallas kernels, per_device(): pl.pallas_call(functools.partial(attention_forward, seq_len=seq_len), gri...  16 us
    pallas_call x1, Pallas kernels, per_device(): pl.pallas_call(functools.partial(up_forward, seq_len=seq_len), grid=(tile...  15.7 us
    pallas_call x1, Pallas kernels, per_device(): pl.pallas_call(functools.partial(mlp_backward, seq_len=seq_len), grid=(ti...  12.9 us
    pallas_call x1, Pallas kernels, gradient(): pl.pallas_call(weight_gradient, grid=(groups,), in_specs=[SMEM] + [spec f...  12.4 us
    pallas_call x3, Pallas kernels, shampoo(): pl.pallas_call(kernel, grid=(1,), out_shape=tuple(out_shape), in_specs=[p...  11.9 us
  transfers between devices with their start and end apart: 53, of which 18 were waited for; matrix products, arithmetic and copies ran while one was open for 3% of the time, Pallas kernels for 47%

profile of v5, /device:TPU:0, one launch (start us, length us, event | category | flops | bytes accessed | tf_op | source)
XLA Modules:
  0.0 245.7 jit_solution(16165190888044168048)
XLA Ops:
  2.9 5.1 %collective-permute-start.2 = (bf16[1,96,768]{2,1,0:T(8,128)(2,1)S(1)}, bf16[1,96,768]{2,1,0:T(8,128)(2,1)S(1)}, u32[]{:S(2)}, u32[]{:S(2)}) collective-permute-start(bf16[1,96,768]{2,1,0:T(8,128)(2,1)S(1)} %bitcast.78), channel_id=1, source_target_pairs={{0,24},{1,25},{2,26},{3,27},{4,28},{5,29},{6,30},{7,31},{8,16},{9,... | collective-permute-start | bytes 442376 | tf_op jit(solution)/shard_map/ppermute | solution.py:61
  15.6 4.9 %collective-permute-done.1 = bf16[1,96,768]{2,1,0:T(8,128)(2,1)S(1)} collective-permute-done((bf16[1,96,768]{2,1,0:T(8,128)(2,1)S(1)}, bf16[1,96,768]{2,1,0:T(8,128)(2,1)S(1)}, u32[]{:S(2)}, u32[]{:S(2)}) %collective-permute-start.1) | collective-permute-done | bytes 147488 | tf_op jit(solution)/shard_map/ppermute | solution.py:61
  22.4 4.4 %first_norm.1 = (bf16[1024,768]{1,0:T(8,128)(2,1)}, bf16[768,1024]{1,0:T(8,128)(2,1)}) custom-call(bf16[1024,768]{1,0:T(8,128)(2,1)} %bitcast.75, f32[4,768]{1,0:T(4,128)S(1)} %bitcast.67), custom_call_target="tpu_custom_call" | custom-call | flops 4 | bytes 100000000 | tf_op jit(solution)/shard_map/first_norm/pallas_call | solution.py:930
  26.9 3.6 %collective-permute-done.8 = bf16[4,96,768]{2,1,0:T(8,128)(2,1)S(1)} collective-permute-done((bf16[4,96,768]{2,1,0:T(8,128)(2,1)S(1)}, bf16[4,96,768]{2,1,0:T(8,128)(2,1)S(1)}, u32[]{:S(2)}, u32[]{:S(2)}) %collective-permute-start.8) | collective-permute-done | bytes 589856 | tf_op jit(solution)/shard_map/ppermute | solution.py:61
  32.2 2.6 %collective-permute-start.7 = (bf16[1,96,768]{2,1,0:T(8,128)(2,1)S(1)}, bf16[1,96,768]{2,1,0:T(8,128)(2,1)S(1)}, u32[]{:S(2)}, u32[]{:S(2)}) collective-permute-start(bf16[1,96,768]{2,1,0:T(8,128)(2,1)S(1)} %convert_bitcast_fusion), channel_id=1, source_target_pairs={{0,24},{1,25},{2,26},{3,27},{4,28},{5,29},{6,30},{7,31},{8,16},{9,... | collective-permute-start | bytes 442376 | tf_op jit(solution)/shard_map/ppermute | solution.py:61
  36.7 4.1 %collective-permute-done.7 = bf16[1,96,768]{2,1,0:T(8,128)(2,1)S(1)} collective-permute-done((bf16[1,96,768]{2,1,0:T(8,128)(2,1)S(1)}, bf16[1,96,768]{2,1,0:T(8,128)(2,1)S(1)}, u32[]{:S(2)}, u32[]{:S(2)}) %collective-permute-start.7) | collective-permute-done | bytes 147488 | tf_op jit(solution)/shard_map/ppermute | solution.py:61
  40.8 4.9 %collective-permute-done.6 = bf16[1,96,768]{2,1,0:T(8,128)(2,1)S(1)} collective-permute-done((bf16[1,96,768]{2,1,0:T(8,128)(2,1)S(1)}, bf16[1,96,768]{2,1,0:T(8,128)(2,1)S(1)}, u32[]{:S(2)}, u32[]{:S(2)}) %collective-permute-start.6) | collective-permute-done | bytes 147488 | tf_op jit(solution)/shard_map/ppermute | solution.py:61
  50.9 5.8 %collective-permute-done.10 = bf16[4,96,768]{2,1,0:T(8,128)(2,1)S(1)} collective-permute-done((bf16[4,96,768]{2,1,0:T(8,128)(2,1)S(1)}, bf16[4,96,768]{2,1,0:T(8,128)(2,1)S(1)}, u32[]{:S(2)}, u32[]{:S(2)}) %collective-permute-start.10) | collective-permute-done | bytes 589856 | tf_op jit(solution)/shard_map/ppermute | solution.py:61
  58.5 16.0 %attention_forward.1 = (bf16[1024,2304]{1,0:T(8,128)(2,1)}, bf16[1024,1024]{1,0:T(8,128)(2,1)}, f32[8,8,256]{2,1,0:T(8,128)S(1)}, f32[1024,768]{1,0:T(8,128)}, bf16[1024,768]{1,0:T(8,128)(2,1)}) custom-call(s32[65]{0:T(128)S(1)} %get-tuple-element.178.order.places, bf16[1024,768]{1,0:T(8,128)(2,1)} %bitcast.76, bf16[1024,768]{1,0:T(8,128)(2,1)} %get-tuple-element.188.h1_ref, ...), custom_call_target="tpu_custom_call" | custom-call | flops 22649241600 | bytes 12000000 | tf_op jit(solution)/shard_map/attention_forward/pallas_call | solution.py:956
  81.7 15.7 %up_forward.1 = (bf16[1024,3072]{1,0:T(8,128)(2,1)}, bf16[1024,3072]{1,0:T(8,128)(2,1)}, bf16[64,3072]{1,0:T(8,128)(2,1)S(1)}) custom-call(s32[65]{0:T(128)S(1)} %get-tuple-element.178.order.places, bf16[1024,768]{1,0:T(8,128)(2,1)} %get-tuple-element.223.h2_ref.refs_0_, f32[64,128]{1,0:T(8,128)S(1)} %broadcast_in_dim.50.count_ref, ...), custom_call_target="tpu_custom_call" | custom-call | flops 19327352832 | bytes 20000000 | tf_op jit(solution)/shard_map/up_forward/pallas_call | solution.py:983
  101.5 11.1 %down_forward.1 = (bf16[1024,768]{1,0:T(8,128)(2,1)}, f32[64,768]{1,0:T(8,128)S(1)}) custom-call(s32[65]{0:T(128)S(1)} %get-tuple-element.177.order, bf16[1024,3072]{1,0:T(8,128)(2,1)} %get-tuple-element.205.hid_ref, f32[1024,768]{1,0:T(8,128)} %get-tuple-element.206.mid_ref, f32[64,128]{1,0:T(8,128)S(1)} %broadcast_in_dim.50.count_ref, ...), custom_call_target="tpu_custom_call" | custom-call | flops 19327352832 | bytes 20000000 | tf_op jit(solution)/shard_map/down_forward/pallas_call | solution.py:1004
  115.9 8.2 %loss_backward.1 = (f32[64,128]{1,0:T(8,128)S(1)}, f32[64,768]{1,0:T(8,128)S(1)}, bf16[64,768]{1,0:T(8,128)(2,1)S(1)}, bf16[8,96,768]{2,1,0:T(8,128)(2,1)}, bf16...) custom-call(s32[65]{0:T(128)S(1)} %get-tuple-element.178.order.places, ...), custom_call_target="tpu_custom_call" | custom-call | flops 4831838208 | bytes 20000000 | tf_op jit(solution)/shard_map/loss_backward/pallas_call | solution.py:1022
  124.6 4.4 %down_backward.1.by_seq_ref = f32[64,3072]{1,0:T(8,128)S(1)} custom-call(s32[65]{0:T(128)S(1)} %get-tuple-element.177.order, bf16[64,768]{1,0:T(8,128)(2,1)S(1)} %get-tuple-element.215.low_ref, bf16[8,96,768]{2,1,0:T(8,128)(2,1)} %copy-done.25, bf16[8,96,768]{2,1,0:T(8,128)(2,1)} %copy-done.42, bf16[8,96,768]{2,1,0:T(8,128)(2,1)} %copy-done.41, ...), custom_call_target="tpu_custom_call" | custom-call | flops 4831838208 | bytes 6000000 | tf_op jit(solution)/shard_map/down_backward/pallas_call | solution.py:1037
  130.9 12.9 %mlp_backward.1 = (bf16[1024,3072]{1,0:T(8,128)(2,1)}, f32[1024,768]{1,0:T(8,128)}, bf16[1024,768]{1,0:T(8,128)(2,1)}, f32[2,768]{1,0:T(2,128)S(1)}) custom-call(s32[65]{0:T(128)S(1)} %get-tuple-element.178.order.places, f32[64,768]{1,0:T(8,128)S(1)} %get-tuple-element.218.grad_ref, f32[64,3072]{1,0:T(8,128)} %copy-done.13, ...), custom_call_target="tpu_custom_call" | custom-call | flops 19327352832 | bytes 25000000 | tf_op jit(solution)/shard_map/mlp_backward/pallas_call | solution.py:1051
  147.8 12.4 %up_gradient.1 = (bf16[8,96,1024]{2,1,0:T(8,128)(2,1)}, bf16[8,96,1024]{2,1,0:T(8,128)(2,1)}, bf16[8,96,1024]{2,1,0:T(8,128)(2,1)}, bf16[8,96,1024]{2,1,0:T(8,128)(2,1)}) custom-call(s32[65]{0:T(128)S(1)} %get-tuple-element.178.order.places, bf16[1024,768]{1,0:T(8,128)(2,1)} %get-tuple-element.223.h2_ref.refs_0_, ...), custom_call_target="tpu_custom_call" | custom-call | flops 22649241600 | bytes 10000000 | tf_op jit(solution)/shard_map/up_gradient/pallas_call | solution.py:1071
  165.7 20.5 %attention_backward.1 = (bf16[1024,2560]{1,0:T(8,128)(2,1)}, f32[1024,768]{1,0:T(8,128)}, f32[2,768]{1,0:T(2,128)S(1)}) custom-call(s32[65]{0:T(128)S(1)} %get-tuple-element.178.order.places, bf16[1024,768]{1,0:T(8,128)(2,1)} %bitcast.77, f32[8,16,256]{2,1,0:T(8,128)S(1)} %pad_maximum_fusion.3.live_ref, f32[4,768]{1,0:T(4,128)S(1)} %bitcast.70, ...), custom_call_target="tpu_custom_call" | custom-call | flops 32715571200 | bytes 20000000 | tf_op jit(solution)/shard_map/attention_backward/pallas_call | solution.py:1101
  190.5 8.9 %attention_gradient.1 = (bf16[8,96,640]{2,1,0:T(8,128)(2,1)}, bf16[8,96,640]{2,1,0:T(8,128)(2,1)}, bf16[8,96,640]{2,1,0:T(8,128)(2,1)}, bf16[8,96,640]{2,1,0:T(8,128)(2,1)}) custom-call(s32[65]{0:T(128)S(1)} %get-tuple-element.178.order.places, bf16[768,1024]{1,0:T(8,128)(2,1)} %get-tuple-element.250.left_ref, bf16[1024,2560]{1,0:T(8,128)(2,1)} %get-tuple-element.251.right_ref), custom_call_target="tpu_custom_call" | custom-call | flops 22649241600 | bytes 10000000 | tf_op jit(solution)/shard_map/attention_gradient/pallas_call | solution.py:1134
  200.5 2.8 %collective-permute-done.41 = bf16[8,96,640]{2,1,0:T(8,128)(2,1)S(1)} collective-permute-done((bf16[8,96,640]{2,1,0:T(8,128)(2,1)}, bf16[8,96,640]{2,1,0:T(8,128)(2,1)S(1)}, u32[]{:S(2)}, u32[]{:S(2)}) %collective-permute-start.41) | collective-permute-done | bytes 983072 | tf_op jit(solution)/shard_map/ppermute | solution.py:61
  210.7 4.7 %shampoo_kernel.1 = (f32[96,768]{1,0:T(8,128)}, f32[96,96]{1,0:T(8,128)}, f32[768,768]{1,0:T(8,128)}, f32[96,768]{1,0:T(8,128)}) custom-call(bf16[2,96,768]{2,1,0:T(8,128)(2,1)S(1)} %get-tuple-element.265.refs_0_, bf16[2,96,768]{2,1,0:T(8,128)(2,1)S(1)} %collective-permute-done.35.refs_1_, bf16[1,96,768]{2,1,0:T(8,128)(2,1)S(1)} %collective-permute-done.39.refs_2_, ...), custom_call_target="tpu_custom_call" | custom-call | flops 905969664 | bytes 7077888 | tf_op jit(solution)/shard_map/shampoo_kernel/pallas_call | solution.py:793
  215.4 3.8 %collective-permute-done.43 = f32[4,768]{1,0:T(4,128)S(1)} collective-permute-done((f32[4,768]{1,0:T(4,128)S(1)}, f32[4,768]{1,0:T(4,128)S(1)}, u32[]{:S(2)}, u32[]{:S(2)}) %collective-permute-start.43) | collective-permute-done | bytes 12320 | tf_op jit(solution)/shard_map/ppermute | solution.py:61
  220.9 2.5 %collective-permute-start.47 = (bf16[1,96,1024]{2,1,0:T(8,128)(2,1)}, bf16[1,96,1024]{2,1,0:T(8,128)(2,1)S(1)}, u32[]{:S(2)}, u32[]{:S(2)}) collective-permute-start(bf16[1,96,1024]{2,1,0:T(8,128)(2,1)} %get-tuple-element.322), channel_id=1, source_target_pairs={{0,24},{1,25},{2,26},{3,27},{4,28},{5,29},{6,30},{7,31},{8,16},{9,... | collective-permute-start | bytes 589832 | tf_op jit(solution)/shard_map/ppermute | solution.py:61
  225.2 4.2 %collective-permute-done.47.refs_4_ = bf16[1,96,1024]{2,1,0:T(8,128)(2,1)S(1)} collective-permute-done((bf16[1,96,1024]{2,1,0:T(8,128)(2,1)}, bf16[1,96,1024]{2,1,0:T(8,128)(2,1)S(1)}, u32[]{:S(2)}, u32[]{:S(2)}) %collective-permute-start.47) | collective-permute-done | bytes 196640 | tf_op jit(solution)/shard_map/ppermute | solution.py:61
  230.3 2.7 %collective-permute-start.51 = (bf16[1,96,640]{2,1,0:T(8,128)(2,1)S(1)}, bf16[1,96,640]{2,1,0:T(8,128)(2,1)S(1)}, u32[]{:S(2)}, u32[]{:S(2)}) collective-permute-start(bf16[1,96,640]{2,1,0:T(8,128)(2,1)S(1)} %get-tuple-element.327), channel_id=1, source_target_pairs={{0,24},{1,25},{2,26},{3,27},{4,28},{5,29},{6,30},{7,31},{8,16},{9,... | collective-permute-start | bytes 368648 | tf_op jit(solution)/shard_map/ppermute | solution.py:61
  235.1 5.3 %up_shampoo.1 = (f32[96,768]{1,0:T(8,128)}, f32[96,96]{1,0:T(8,128)}, f32[768,768]{1,0:T(8,128)}, f32[96,768]{1,0:T(8,128)}, f32[96,192]{1,0:T(8,128)}, /*index=...) custom-call(bf16[4,96,1024]{2,1,0:T(8,128)(2,1)} %copy-done.14, bf16[4,96,1024]{2,1,0:T(8,128)(2,1)} %copy-done.15, ...), custom_call_target="tpu_custom_call" | custom-call | flops 1610612736 | bytes 12582912 | tf_op jit(solution)/shard_map/up_shampoo/pallas_call | solution.py:793
  (257 shorter events, 72.4 us)
Async XLA Ops:
  30.6 16.3 %collective-permute-start.9 = (bf16[8,96,768]{2,1,0:T(8,128)(2,1)S(1)}, bf16[8,96,768]{2,1,0:T(8,128)(2,1)S(1)}, u32[]{:S(2)}, u32[]{:S(2)}) collective-permute-start(bf16[8,96,768]{2,1,0:T(8,128)(2,1)S(1)} %constant_dynamic-update-slice_fusion.w0), channel_id=1, source_target_pairs={{0,2},{1,5},{2,0},{3,7},{4,6},{5,1},{6,4},{7,3},{8,10},{9,13},{10,... | collective-permute-start | bytes 3538952 | tf_op jit(solution)/shard_map/ppermute | solution.py:61
  36.6 20.2 %collective-permute-start.11 = (bf16[8,96,768]{2,1,0:T(8,128)(2,1)S(1)}, bf16[8,96,768]{2,1,0:T(8,128)(2,1)S(1)}, u32[]{:S(2)}, u32[]{:S(2)}) collective-permute-start(bf16[8,96,768]{2,1,0:T(8,128)(2,1)S(1)} %constant_dynamic-update-slice_fusion.w0), channel_id=1, source_target_pairs={{0,1},{1,0},{2,3},{3,2},{4,5},{5,4},{6,7},{7,6},{8,9},{9,8},{10,11... | collective-permute-start | bytes 3538952 | tf_op jit(solution)/shard_map/ppermute | solution.py:61
  48.3 26.2 %collective-permute-start.15 = (bf16[2,96,768]{2,1,0:T(8,128)(2,1)S(1)}, bf16[2,96,768]{2,1,0:T(8,128)(2,1)S(1)}, u32[]{:S(2)}, u32[]{:S(2)}) collective-permute-start(bf16[2,96,768]{2,1,0:T(8,128)(2,1)S(1)} %pad_maximum_fusion.1), channel_id=1, source_target_pairs={{0,24},{1,25},{2,26},{3,27},{4,28},{5,29},{6,30},{7,31},{8,16},{9,... | collective-permute-start | bytes 884744 | tf_op jit(solution)/shard_map/ppermute | solution.py:61
  50.9 24.7 %collective-permute-start.14 = (bf16[2,96,768]{2,1,0:T(8,128)(2,1)S(1)}, bf16[2,96,768]{2,1,0:T(8,128)(2,1)S(1)}, u32[]{:S(2)}, u32[]{:S(2)}) collective-permute-start(bf16[2,96,768]{2,1,0:T(8,128)(2,1)S(1)} %pad_maximum_fusion.1), channel_id=1, source_target_pairs={{0,16},{1,17},{2,18},{3,19},{4,20},{5,21},{6,22},{7,23},{8,24},{9,... | collective-permute-start | bytes 884744 | tf_op jit(solution)/shard_map/ppermute | solution.py:61
  56.7 18.9 %collective-permute-start.13 = (bf16[2,96,768]{2,1,0:T(8,128)(2,1)S(1)}, bf16[2,96,768]{2,1,0:T(8,128)(2,1)S(1)}, u32[]{:S(2)}, u32[]{:S(2)}) collective-permute-start(bf16[2,96,768]{2,1,0:T(8,128)(2,1)S(1)} %pad_maximum_fusion.1), channel_id=1, source_target_pairs={{0,8},{1,9},{2,10},{3,11},{4,12},{5,13},{6,14},{7,15},{8,0},{9,1},... | collective-permute-start | bytes 884744 | tf_op jit(solution)/shard_map/ppermute | solution.py:61
  56.8 23.5 %collective-permute-start.17 = (bf16[8,96,768]{2,1,0:T(8,128)(2,1)S(1)}, bf16[8,96,768]{2,1,0:T(8,128)(2,1)S(1)}, u32[]{:S(2)}, u32[]{:S(2)}) collective-permute-start(bf16[8,96,768]{2,1,0:T(8,128)(2,1)S(1)} %constant_dynamic-update-slice_fusion.9.w0), channel_id=1, source_target_pairs={{0,1},{1,0},{2,3},{3,2},{4,5},{5,4},{6,7},{7,6},{8,9},{9,8},{10,11... | collective-permute-start | bytes 3538952 | tf_op jit(solution)/shard_map/ppermute | solution.py:61
  56.9 18.8 %collective-permute-start.16 = (bf16[8,96,768]{2,1,0:T(8,128)(2,1)S(1)}, bf16[8,96,768]{2,1,0:T(8,128)(2,1)S(1)}, u32[]{:S(2)}, u32[]{:S(2)}) collective-permute-start(bf16[8,96,768]{2,1,0:T(8,128)(2,1)S(1)} %constant_dynamic-update-slice_fusion.9.w0), channel_id=1, source_target_pairs={{0,2},{1,5},{2,0},{3,7},{4,6},{5,1},{6,4},{7,3},{8,10},{9,13},{10,... | collective-permute-start | bytes 3538952 | tf_op jit(solution)/shard_map/ppermute | solution.py:61
  75.8 21.6 %collective-permute-start.21 = (bf16[2,64,768]{2,1,0:T(8,128)(2,1)S(1)}, bf16[2,64,768]{2,1,0:T(8,128)(2,1)S(1)}, u32[]{:S(2)}, u32[]{:S(2)}) collective-permute-start(bf16[2,64,768]{2,1,0:T(8,128)(2,1)S(1)} %pad_maximum_fusion.2), channel_id=1, source_target_pairs={{0,24},{1,25},{2,26},{3,27},{4,28},{5,29},{6,30},{7,31},{8,16},{9,... | collective-permute-start | bytes 589832 | tf_op jit(solution)/shard_map/ppermute | solution.py:61
  77.4 20.0 %collective-permute-start.20 = (bf16[2,64,768]{2,1,0:T(8,128)(2,1)S(1)}, bf16[2,64,768]{2,1,0:T(8,128)(2,1)S(1)}, u32[]{:S(2)}, u32[]{:S(2)}) collective-permute-start(bf16[2,64,768]{2,1,0:T(8,128)(2,1)S(1)} %pad_maximum_fusion.2), channel_id=1, source_target_pairs={{0,16},{1,17},{2,18},{3,19},{4,20},{5,21},{6,22},{7,23},{8,24},{9,... | collective-permute-start | bytes 589832 | tf_op jit(solution)/shard_map/ppermute | solution.py:61
  78.4 19.1 %collective-permute-start.19 = (bf16[2,64,768]{2,1,0:T(8,128)(2,1)S(1)}, bf16[2,64,768]{2,1,0:T(8,128)(2,1)S(1)}, u32[]{:S(2)}, u32[]{:S(2)}) collective-permute-start(bf16[2,64,768]{2,1,0:T(8,128)(2,1)S(1)} %pad_maximum_fusion.2), channel_id=1, source_target_pairs={{0,8},{1,9},{2,10},{3,11},{4,12},{5,13},{6,14},{7,15},{8,0},{9,1},... | collective-permute-start | bytes 589832 | tf_op jit(solution)/shard_map/ppermute | solution.py:61
  80.3 18.7 %collective-permute-start.23 = (bf16[8,96,768]{2,1,0:T(8,128)(2,1)S(1)}, bf16[8,96,768]{2,1,0:T(8,128)(2,1)S(1)}, u32[]{:S(2)}, u32[]{:S(2)}) collective-permute-start(bf16[8,96,768]{2,1,0:T(8,128)(2,1)S(1)} %constant_dynamic-update-slice_fusion.11.w0), channel_id=1, source_target_pairs={{0,1},{1,0},{2,3},{3,2},{4,5},{5,4},{6,7},{7,6},{8,9},{9,8},{10,11... | collective-permute-start | bytes 3538952 | tf_op jit(solution)/shard_map/ppermute | solution.py:61
  80.4 17.1 %collective-permute-start.22 = (bf16[8,96,768]{2,1,0:T(8,128)(2,1)S(1)}, bf16[8,96,768]{2,1,0:T(8,128)(2,1)S(1)}, u32[]{:S(2)}, u32[]{:S(2)}) collective-permute-start(bf16[8,96,768]{2,1,0:T(8,128)(2,1)S(1)} %constant_dynamic-update-slice_fusion.11.w0), channel_id=1, source_target_pairs={{0,2},{1,5},{2,0},{3,7},{4,6},{5,1},{6,4},{7,3},{8,10},{9,13},{10,... | collective-permute-start | bytes 3538952 | tf_op jit(solution)/shard_map/ppermute | solution.py:61
  97.9 15.1 %collective-permute-start.26 = (bf16[8,64,768]{2,1,0:T(8,128)(2,1)S(1)}, bf16[8,64,768]{2,1,0:T(8,128)(2,1)S(1)}, u32[]{:S(2)}, u32[]{:S(2)}) collective-permute-start(bf16[8,64,768]{2,1,0:T(8,128)(2,1)S(1)} %constant_dynamic-update-slice_fusion.15), channel_id=1, source_target_pairs={{0,1},{1,0},{2,3},{3,2},{4,5},{5,4},{6,7},{7,6},{8,9},{9,8},{10,11... | collective-permute-start | bytes 2359304 | tf_op jit(solution)/shard_map/ppermute | solution.py:61
  98.1 14.5 %collective-permute-start.25 = (bf16[8,64,768]{2,1,0:T(8,128)(2,1)S(1)}, bf16[8,64,768]{2,1,0:T(8,128)(2,1)S(1)}, u32[]{:S(2)}, u32[]{:S(2)}) collective-permute-start(bf16[8,64,768]{2,1,0:T(8,128)(2,1)S(1)} %constant_dynamic-update-slice_fusion.15), channel_id=1, source_target_pairs={{0,2},{1,5},{2,0},{3,7},{4,6},{5,1},{6,4},{7,3},{8,10},{9,13},{10,... | collective-permute-start | bytes 2359304 | tf_op jit(solution)/shard_map/ppermute | solution.py:61
  124.4 21.7 %collective-permute-start.28 = (bf16[8,96,768]{2,1,0:T(8,128)(2,1)}, bf16[8,96,768]{2,1,0:T(8,128)(2,1)S(1)}, u32[]{:S(2)}, u32[]{:S(2)}) collective-permute-start(bf16[8,96,768]{2,1,0:T(8,128)(2,1)} %get-tuple-element.212), channel_id=1, source_target_pairs={{0,1},{1,0},{2,3},{3,2},{4,5},{5,4},{6,7},{7,6},{8,9},{9,8},{10,11... | collective-permute-start | bytes 3538952 | tf_op jit(solution)/shard_map/ppermute | solution.py:61
  129.9 16.2 %collective-permute-start.30 = (bf16[8,96,768]{2,1,0:T(8,128)(2,1)S(1)}, bf16[8,96,768]{2,1,0:T(8,128)(2,1)S(1)}, u32[]{:S(2)}, u32[]{:S(2)}) collective-permute-start(bf16[8,96,768]{2,1,0:T(8,128)(2,1)S(1)} %add_convert_fusion.1), channel_id=1, source_target_pairs={{0,2},{1,5},{2,0},{3,7},{4,6},{5,1},{6,4},{7,3},{8,10},{9,13},{10,... | collective-permute-start | bytes 3538952 | tf_op jit(solution)/shard_map/ppermute | solution.py:61
  146.6 13.5 %collective-permute-start.31 = (bf16[4,96,768]{2,1,0:T(8,128)(2,1)S(1)}, bf16[4,96,768]{2,1,0:T(8,128)(2,1)S(1)}, u32[]{:S(2)}, u32[]{:S(2)}) collective-permute-start(bf16[4,96,768]{2,1,0:T(8,128)(2,1)S(1)} %get-tuple-element.319), channel_id=1, source_target_pairs={{0,4},{1,3},{2,6},{3,1},{4,0},{5,7},{6,2},{7,5},{8,12},{9,11},{10,... | collective-permute-start | bytes 1769480 | tf_op jit(solution)/shard_map/ppermute | solution.py:61
  160.4 25.8 %collective-permute-start.35 = (bf16[2,96,768]{2,1,0:T(8,128)(2,1)S(1)}, bf16[2,96,768]{2,1,0:T(8,128)(2,1)S(1)}, u32[]{:S(2)}, u32[]{:S(2)}) collective-permute-start(bf16[2,96,768]{2,1,0:T(8,128)(2,1)S(1)} %get-tuple-element.326), channel_id=1, source_target_pairs={{0,16},{1,17},{2,18},{3,19},{4,20},{5,21},{6,22},{7,23},{8,24},{9,... | collective-permute-start | bytes 884744 | tf_op jit(solution)/shard_map/ppermute | solution.py:61
  162.2 25.2 %collective-permute-start.33 = (bf16[8,96,1024]{2,1,0:T(8,128)(2,1)}, bf16[8,96,1024]{2,1,0:T(8,128)(2,1)S(1)}, u32[]{:S(2)}, u32[]{:S(2)}) collective-permute-start(bf16[8,96,1024]{2,1,0:T(8,128)(2,1)} %get-tuple-element.243), channel_id=1, source_target_pairs={{0,1},{1,0},{2,3},{3,2},{4,5},{5,4},{6,7},{7,6},{8,9},{9,8},{10,11... | collective-permute-start | bytes 4718600 | tf_op jit(solution)/shard_map/ppermute | solution.py:61
  164.6 21.6 %collective-permute-start.34 = (bf16[8,96,1024]{2,1,0:T(8,128)(2,1)S(1)}, bf16[8,96,1024]{2,1,0:T(8,128)(2,1)S(1)}, u32[]{:S(2)}, u32[]{:S(2)}) collective-permute-start(bf16[8,96,1024]{2,1,0:T(8,128)(2,1)S(1)} %add_convert_fusion), channel_id=1, source_target_pairs={{0,2},{1,5},{2,0},{3,7},{4,6},{5,1},{6,4},{7,3},{8,10},{9,13},{10,... | collective-permute-start | bytes 4718600 | tf_op jit(solution)/shard_map/ppermute | solution.py:61
  186.3 13.2 %collective-permute-start.39 = (bf16[1,96,768]{2,1,0:T(8,128)(2,1)S(1)}, bf16[1,96,768]{2,1,0:T(8,128)(2,1)S(1)}, u32[]{:S(2)}, u32[]{:S(2)}) collective-permute-start(bf16[1,96,768]{2,1,0:T(8,128)(2,1)S(1)} %add_convert_fusion.14), channel_id=1, source_target_pairs={{0,8},{1,9},{2,10},{3,11},{4,12},{5,13},{6,14},{7,15},{8,0},{9,1},... | collective-permute-start | bytes 442376 | tf_op jit(solution)/shard_map/ppermute | solution.py:61
  204.8 14.4 %collective-permute-start.42 = (bf16[8,96,640]{2,1,0:T(8,128)(2,1)S(1)}, bf16[8,96,640]{2,1,0:T(8,128)(2,1)S(1)}, u32[]{:S(2)}, u32[]{:S(2)}) collective-permute-start(bf16[8,96,640]{2,1,0:T(8,128)(2,1)S(1)} %add_convert_fusion.2), channel_id=1, source_target_pairs={{0,2},{1,5},{2,0},{3,7},{4,6},{5,1},{6,4},{7,3},{8,10},{9,13},{10,... | collective-permute-start | bytes 2949128 | tf_op jit(solution)/shard_map/ppermute | solution.py:61
  205.6 13.6 %collective-permute-start.40 = (bf16[8,96,640]{2,1,0:T(8,128)(2,1)S(1)}, bf16[8,96,640]{2,1,0:T(8,128)(2,1)S(1)}, u32[]{:S(2)}, u32[]{:S(2)}) collective-permute-start(bf16[8,96,640]{2,1,0:T(8,128)(2,1)S(1)} %copy-done.44), channel_id=1, source_target_pairs={{0,1},{1,0},{2,3},{3,2},{4,5},{5,4},{6,7},{7,6},{8,9},{9,8},{10,11... | collective-permute-start | bytes 2949128 | tf_op jit(solution)/shard_map/ppermute | solution.py:61
  230.3 13.4 %collective-permute-start.51 = (bf16[1,96,640]{2,1,0:T(8,128)(2,1)S(1)}, bf16[1,96,640]{2,1,0:T(8,128)(2,1)S(1)}, u32[]{:S(2)}, u32[]{:S(2)}) collective-permute-start(bf16[1,96,640]{2,1,0:T(8,128)(2,1)S(1)} %get-tuple-element.327), channel_id=1, source_target_pairs={{0,24},{1,25},{2,26},{3,27},{4,28},{5,29},{6,30},{7,31},{8,16},{9,... | collective-permute-start | bytes 368648 | tf_op jit(solution)/shard_map/ppermute | solution.py:61
  (77 other events, 651.1 us)
